TPU v7x, 128 devices: a whole 4x4x4 slice. The times are simulated.
128 devices in a mesh: rad: 4 (over z_lo, core), phi: 32 (over x, y, z_hi).
Axes of the slice: x: 4, y: 4, z: 4 (z_hi: 2, z_lo: 2; z = z_hi * 2 + z_lo), core: 2. Of those that a mesh axis runs over, the one named last changes fastest.
Arguments:
- density: float32 [2, 512, 16384], P(None, 'rad', 'phi'), may hold values from 0.5 to 2
- carried: float32 [7, 2, 512, 16384], P(None, None, 'rad', 'phi'), may hold values from -1.5 to 1.5
- cycle_shift: int32 [512], P('rad'), may hold values from 0 to 16383
- cycle_fraction: float32 [512], P('rad'), may hold values from 0 to 1
Outputs:
- density_next: float32 [2, 512, 16384], P(None, 'rad', 'phi')
- carried_next: float32 [7, 2, 512, 16384], P(None, None, 'rad', 'phi')
All inputs are finite; a program needn't handle non-finite values.
Results may differ from a plain program's by a relative error of at most 0.00002.
Values sent between devices are 32-bit elements; how exact they have to be, the bound alone decides.
No kernel may reach another device: no remote copies, remote signals or barrier semaphores. Data moves between devices by JAX's collectives and lax.ppermute only.
A program may use at most 192 MiB of HBM per device.

v0:
```python
import jax
import jax.numpy as jnp
from jax import lax
from jax.sharding import PartitionSpec as P


def padded_2(shard, sides, width, wrap):
    for axis, dim in sides:
        peers, length = (lax.axis_size(axis), shard.shape[dim])
        up = [(i, (i + 1) % peers) for i in range(peers if wrap else peers - 1)]
        down = [(j, i) for i, j in up]
        last = lax.slice_in_dim(shard, length - width, length, axis=dim)
        leading = lax.slice_in_dim(shard, 0, width, axis=dim)
        before = lax.ppermute(last, axis, up)
        after = lax.ppermute(leading, axis, down)
        shard = jnp.concatenate([before, shard, after], axis=dim)
    return shard


def from_behind(value, axis, steps):
    count = lax.axis_size(axis)
    pairs = [(source, (source + steps) % count) for source in range(count)]
    return lax.ppermute(value, axis, pairs)


def face_divergence(padded, axis, direction):
    count = padded.shape[axis] - 2
    left = lax.slice_in_dim(padded, 0, count + 1, axis=axis)
    right = lax.slice_in_dim(padded, 1, count + 2, axis=axis)
    q_left = left[:8]
    q_right = right[:8]
    v_left = left[8 + direction][None]
    v_right = right[8 + direction][None]
    speed = jnp.maximum(jnp.abs(v_left), jnp.abs(v_right)) + 1.0
    flux = 0.5 * (v_left * q_left + v_right * q_right) - 0.5 * speed * (q_right - q_left)
    upper = lax.slice_in_dim(flux, 1, count + 1, axis=axis)
    lower = lax.slice_in_dim(flux, 0, count, axis=axis)
    return upper - lower


def rotate_rows(values, amounts, row_axis, limit):
    last = values.ndim - 1
    shape = [1] * values.ndim
    shape[row_axis] = amounts.shape[0]
    level = 0
    while 1 << level < limit:
        taken = (jnp.right_shift(amounts, level) % 2 == 1).reshape(shape)
        values = jnp.where(taken, jnp.roll(values, 1 << level, axis=last), values)
        level = level + 1
    return values


def local(density, carried, cycle_shift, cycle_fraction):
    state = jnp.concatenate([density[None], carried], axis=0)
    velocity = carried[0:3] / density[None]
    extended = jnp.concatenate([state, velocity], axis=0)
    radial = padded_2(extended, (("rad", 2),), 1, False)
    azimuth = padded_2(extended, (("phi", 3),), 1, True)
    height = jnp.concatenate([extended[:, -1:], extended, extended[:, :1]], axis=1)
    update = 0.08 * (
        face_divergence(radial, 2, 0)
        + face_divergence(azimuth, 3, 1)
        + face_divergence(height, 1, 2)
    )
    block_width = state.shape[3]
    devices_phi = lax.axis_size("phi")
    whole_hops = cycle_shift // block_width
    remain = cycle_shift % block_width
    bit_total = 0
    while 1 << bit_total < devices_phi:
        bit_total = bit_total + 1
    current = state
    for level in range(bit_total):
        arrived = from_behind(current, "phi", 1 << level)
        taken = jnp.right_shift(whole_hops, level) % 2 == 1
        current = jnp.where(taken[None, None, :, None], arrived, current)
    previous = from_behind(current, "phi", 1)
    window = jnp.concatenate([previous, current], axis=3)
    rolled = rotate_rows(window, remain, 2, block_width)
    part_one = rolled[:, :, :, block_width:]
    part_two = rolled[:, :, :, block_width - 1 : 2 * block_width - 1]
    weight = cycle_fraction[None, None, :, None]
    moved = (1.0 - weight) * part_one + weight * part_two
    new_state = moved - update
    return (new_state[0], new_state[1:])


def solution(mesh):
    placed = (P(None, "rad", "phi"), P(None, None, "rad", "phi"), P("rad"), P("rad"))
    return jax.shard_map(
        local,
        mesh=mesh,
        in_specs=placed,
        out_specs=(P(None, "rad", "phi"), P(None, None, "rad", "phi")),
        check_vma=False,
    )
```

profile of v0, /device:TPU:0, one launch (start us, length us, event | category | flops | bytes accessed | tf_op | source)
XLA Modules:
  0.0 653.1 jit_solution(3280119060887981141)
XLA Ops:
  0.7 2.9 pad_maximum_fusion.20
  3.6 4.0 collective-permute-start
  8.2 94.6 %collective-permute-done = f32[8,2,128,512]{3,2,1,0:T(8,128)S(1)} collective-permute-done((f32[8,2,128,512]{3,2,1,0:T(8,128)S(1)}, f32[8,2,128,512]{3,2,1,0:T(8,128)S(1)}, u32[]{:S(2)}, u32[]{:S(2)}) %collective-permute-start) | collective-permute-done | bytes 4194336 | tf_op jit(solution)/shard_map/ppermute | solution.py:23
  104.0 95.1 %collective-permute-done.1 = f32[8,2,128,512]{3,2,1,0:T(8,128)S(1)} collective-permute-done((f32[8,2,128,512]{3,2,1,0:T(8,128)S(1)}, f32[8,2,128,512]{3,2,1,0:T(8,128)S(1)}, u32[]{:S(2)}, u32[]{:S(2)}) %collective-permute-start.1) | collective-permute-done | bytes 4194336 | tf_op jit(solution)/shard_map/ppermute | solution.py:23
  200.2 94.4 %collective-permute-done.2 = f32[8,2,128,512]{3,2,1,0:T(8,128)S(1)} collective-permute-done((f32[8,2,128,512]{3,2,1,0:T(8,128)S(1)}, f32[8,2,128,512]{3,2,1,0:T(8,128)S(1)}, u32[]{:S(2)}, u32[]{:S(2)}) %collective-permute-start.2) | collective-permute-done | bytes 4194336 | tf_op jit(solution)/shard_map/ppermute | solution.py:23
  295.8 91.1 %collective-permute-done.3 = f32[8,2,128,512]{3,2,1,0:T(8,128)S(1)} collective-permute-done((f32[8,2,128,512]{3,2,1,0:T(8,128)S(1)}, f32[8,2,128,512]{3,2,1,0:T(8,128)S(1)}, u32[]{:S(2)}, u32[]{:S(2)}) %collective-permute-start.3) | collective-permute-done | bytes 4194336 | tf_op jit(solution)/shard_map/ppermute | solution.py:23
  389.2 89.4 %collective-permute-done.4 = f32[8,2,128,512]{3,2,1,0:T(8,128)S(1)} collective-permute-done((f32[8,2,128,512]{3,2,1,0:T(8,128)S(1)}, f32[8,2,128,512]{3,2,1,0:T(8,128)S(1)}, u32[]{:S(2)}, u32[]{:S(2)}) %collective-permute-start.4) | collective-permute-done | bytes 4194336 | tf_op jit(solution)/shard_map/ppermute | solution.py:23
  478.6 3.0 broadcast_select_fusion.4
  483.3 2.0 copy.13
  487.3 7.0 %collective-permute-start.9 = (f32[11,2,128,1]{2,0,3,1:T(8,128)}, f32[11,2,128,1]{2,0,3,1:T(8,128)}, u32[]{:S(2)}, u32[]{:S(2)}) collective-permute-start(f32[11,2,128,1]{2,0,3,1:T(8,128)} %copy.17), channel_id=1, source_target_pairs={{1,0},{2,1},{3,2},{4,3},{5,4},{6,5},{7,6},{8,7},{9,8},{10,9},{11,1... | collective-permute-start | bytes 33800 | tf_op jit(solution)/shard_map/ppermute | solution.py:15
  494.3 1.8 pad_maximum_fusion.28
  496.0 1.9 collective-permute-start.6
  501.4 4.2 multiply_subtract_fusion
  506.2 70.0 %collective-permute-done.8 = f32[11,2,128,1]{2,0,3,1:T(8,128)} collective-permute-done((f32[11,2,128,1]{2,0,3,1:T(8,128)S(1)}, f32[11,2,128,1]{2,0,3,1:T(8,128)}, u32[]{:S(2)}, u32[]{:S(2)}) %collective-permute-start.8) | collective-permute-done | bytes 11296 | tf_op jit(solution)/shard_map/ppermute | solution.py:14
  577.4 2.3 copy.18
  582.2 3.7 multiply_subtract_fusion.1
  586.8 3.6 multiply_subtract_fusion.2
  591.9 3.9 fusion
  595.8 5.1 fusion.1
  601.3 3.3 maximum_select_fusion
  605.0 2.9 maximum_select_fusion.1
  608.3 3.3 maximum_select_fusion.2
  611.9 3.3 maximum_select_fusion.3
  615.6 3.5 maximum_select_fusion.4
  619.4 3.3 maximum_select_fusion.5
  623.8 2.2 maximum_select_fusion.6
  626.0 3.4 slice.243
  629.8 7.2 %maximum_select_fusion.7 = f32[8,2,128,1024]{3,2,1,0:T(8,128)} fusion(f32[8,2,128,1024]{3,2,1,0:T(8,128)S(1)} %maximum_select_fusion.6, f32[8,2,128,768]{3,2,1,0:T(8,128)} %slice.243, f32[8,2,128,256]{3,2,1,0:T(8,128)S(1)} %slice.242, pred[128]{0:T(512)(128)(4,1)S(1)} %copy-done.7), kind=kLoop, calls=%fused_computation.12 | loop fusion | flops 4194304 | bytes 25165952 | tf_op jit(solution)/shard_map/jit(_where)/select_n | solution.py:48
  636.9 1.9 slice-done.4
  639.9 7.1 %fusion.4 = f32[8,2,128,512]{3,2,1,0:T(8,128)} fusion(f32[8,3,128,512]{3,2,1,0:T(8,128)S(1)} %bitcast.42, f32[8,2,128,513]{3,2,1,0:T(8,128)S(1)} %bitcast.40, f32[8,2,129,512]{3,2,1,0:T(8,128)S(1)} %bitcast.38, f32[8,2,128,1024]{3,2,1,0:T(8,128)} %maximum_select_fusion.7, f32[128]{0:T(128)S(1)} %copy-done.19, f32[128]{0:T(128)S(1)} %copy-done.20), kind=kLoop, calls=%fused_computation.38 | loop fusion | flops 10485760 | bytes 37749760 | tf_op jit(solution)/shard_map/sub | solution.py:84
  647.0 4.3 slice.257
  651.3 1.9 slice_bitcast_fusion
  (94 shorter events, 24.6 us)
Async XLA Ops:
  0.6 102.2 %copy-start.3 = (f32[2,128,512]{2,1,0:T(8,128)S(1)}, f32[2,128,512]{2,1,0:T(8,128)}, u32[]{:S(2)}) copy-start(f32[2,128,512]{2,1,0:T(8,128)} %param.4) | copy-start | bytes 1572868
  0.6 102.2 %copy-start = (f32[7,2,128,512]{3,2,1,0:T(8,128)S(1)}, f32[7,2,128,512]{3,2,1,0:T(8,128)}, u32[]{:S(2)}) copy-start(f32[7,2,128,512]{3,2,1,0:T(8,128)} %param.5) | copy-start | bytes 11010052
  0.7 6.9 %copy-start.17 = (s32[128]{0:T(128)S(1)}, s32[128]{0:T(128)}, u32[]{:S(2)}) copy-start(s32[128]{0:T(128)} %param.6) | copy-start | bytes 1540
  3.6 99.2 %collective-permute-start = (f32[8,2,128,512]{3,2,1,0:T(8,128)S(1)}, f32[8,2,128,512]{3,2,1,0:T(8,128)S(1)}, u32[]{:S(2)}, u32[]{:S(2)}) collective-permute-start(f32[8,2,128,512]{3,2,1,0:T(8,128)S(1)} %pad_maximum_fusion.20), channel_id=1, source_target_pairs={{0,1},{1,2},{2,3},{3,4},{4,5},{5,6},{6,7},{7,8},{8,9},{9,10},{10,1... | collective-permute-start | bytes 12582920 | tf_op jit(solution)/shard_map/ppermute | solution.py:23
  103.9 95.1 %collective-permute-start.1 = (f32[8,2,128,512]{3,2,1,0:T(8,128)S(1)}, f32[8,2,128,512]{3,2,1,0:T(8,128)S(1)}, u32[]{:S(2)}, u32[]{:S(2)}) collective-permute-start(f32[8,2,128,512]{3,2,1,0:T(8,128)S(1)} %broadcast_select_fusion), channel_id=1, source_target_pairs={{0,2},{1,3},{2,4},{3,5},{4,6},{5,7},{6,8},{7,9},{8,10},{9,11},{10,... | collective-permute-start | bytes 12582920 | tf_op jit(solution)/shard_map/ppermute | solution.py:23
  200.1 94.5 %collective-permute-start.2 = (f32[8,2,128,512]{3,2,1,0:T(8,128)S(1)}, f32[8,2,128,512]{3,2,1,0:T(8,128)S(1)}, u32[]{:S(2)}, u32[]{:S(2)}) collective-permute-start(f32[8,2,128,512]{3,2,1,0:T(8,128)S(1)} %broadcast_select_fusion.1), channel_id=1, source_target_pairs={{0,4},{1,5},{2,6},{3,7},{4,8},{5,9},{6,10},{7,11},{8,12},{9,13},{1... | collective-permute-start | bytes 12582920 | tf_op jit(solution)/shard_map/ppermute | solution.py:23
  295.7 91.2 %collective-permute-start.3 = (f32[8,2,128,512]{3,2,1,0:T(8,128)S(1)}, f32[8,2,128,512]{3,2,1,0:T(8,128)S(1)}, u32[]{:S(2)}, u32[]{:S(2)}) collective-permute-start(f32[8,2,128,512]{3,2,1,0:T(8,128)S(1)} %broadcast_select_fusion.2), channel_id=1, source_target_pairs={{0,8},{1,9},{2,10},{3,11},{4,12},{5,13},{6,14},{7,15},{8,16},{9,17... | collective-permute-start | bytes 12582920 | tf_op jit(solution)/shard_map/ppermute | solution.py:23
  388.0 90.6 %collective-permute-start.4 = (f32[8,2,128,512]{3,2,1,0:T(8,128)S(1)}, f32[8,2,128,512]{3,2,1,0:T(8,128)S(1)}, u32[]{:S(2)}, u32[]{:S(2)}) collective-permute-start(f32[8,2,128,512]{3,2,1,0:T(8,128)S(1)} %broadcast_select_fusion.3), channel_id=1, source_target_pairs={{0,16},{1,17},{2,18},{3,19},{4,20},{5,21},{6,22},{7,23},{8,24},{9,... | collective-permute-start | bytes 12582920 | tf_op jit(solution)/shard_map/ppermute | solution.py:23
  389.2 92.4 %copy-start.4 = (f32[11,2,128,512]{3,2,1,0:T(8,128)}, f32[11,2,128,512]{3,2,1,0:T(8,128)S(1)}, u32[]{:S(2)}) copy-start(f32[11,2,128,512]{3,2,1,0:T(8,128)S(1)} %pad_maximum_fusion.7) | copy-start | bytes 17301508
  481.6 110.3 %collective-permute-start.5 = (f32[8,2,128,512]{3,2,1,0:T(8,128)}, f32[8,2,128,512]{3,2,1,0:T(8,128)}, u32[]{:S(2)}, u32[]{:S(2)}) collective-permute-start(f32[8,2,128,512]{3,2,1,0:T(8,128)} %broadcast_select_fusion.4), channel_id=1, source_target_pairs={{0,1},{1,2},{2,3},{3,4},{4,5},{5,6},{6,7},{7,8},{8,9},{9,10},{10,1... | collective-permute-start | bytes 12582920 | tf_op jit(solution)/shard_map/ppermute | solution.py:23
  485.2 90.9 %collective-permute-start.8 = (f32[11,2,128,1]{2,0,3,1:T(8,128)S(1)}, f32[11,2,128,1]{2,0,3,1:T(8,128)}, u32[]{:S(2)}, u32[]{:S(2)}) collective-permute-start(f32[11,2,128,1]{2,0,3,1:T(8,128)S(1)} %copy.13), channel_id=1, source_target_pairs={{0,1},{1,2},{2,3},{3,4},{4,5},{5,6},{6,7},{7,8},{8,9},{9,10},{10,1... | collective-permute-start | bytes 33800 | tf_op jit(solution)/shard_map/ppermute | solution.py:14
  487.3 12.2 %copy-start.5 = (f32[11,2,128,512]{3,2,1,0:T(8,128)S(1)}, f32[11,2,128,512]{3,2,1,0:T(8,128)}, u32[]{:S(2)}) copy-start(f32[11,2,128,512]{3,2,1,0:T(8,128)} %copy-done.4) | copy-start | bytes 17301508
  487.3 90.1 %collective-permute-start.9 = (f32[11,2,128,1]{2,0,3,1:T(8,128)}, f32[11,2,128,1]{2,0,3,1:T(8,128)}, u32[]{:S(2)}, u32[]{:S(2)}) collective-permute-start(f32[11,2,128,1]{2,0,3,1:T(8,128)} %copy.17), channel_id=1, source_target_pairs={{1,0},{2,1},{3,2},{4,3},{5,4},{6,5},{7,6},{8,7},{9,8},{10,9},{11,1... | collective-permute-start | bytes 33800 | tf_op jit(solution)/shard_map/ppermute | solution.py:15
  496.0 89.9 %collective-permute-start.6 = (f32[11,2,1,512]{3,2,1,0:T(1,128)}, f32[11,2,1,512]{3,2,1,0:T(1,128)}, u32[]{:S(2)}, u32[]{:S(2)}) collective-permute-start(f32[11,2,1,512]{3,2,1,0:T(1,128)} %get-tuple-element.17), channel_id=1, source_target_pairs={{0,32},{32,64},{64,96},{1,33},{33,65},{65,97},{2,34},{34,66},{66,9... | collective-permute-start | bytes 135176 | tf_op jit(solution)/shard_map/ppermute | solution.py:14
  497.9 88.0 %collective-permute-start.7 = (f32[11,2,1,512]{3,2,1,0:T(1,128)}, f32[11,2,1,512]{3,2,1,0:T(1,128)}, u32[]{:S(2)}, u32[]{:S(2)}) collective-permute-start(f32[11,2,1,512]{3,2,1,0:T(1,128)} %get-tuple-element.18), channel_id=1, source_target_pairs={{32,0},{64,32},{96,64},{33,1},{65,33},{97,65},{34,2},{66,34},{98,6... | collective-permute-start | bytes 135176 | tf_op jit(solution)/shard_map/ppermute | solution.py:15
  501.4 4.2 copy-start.18
  591.9 3.9 copy-start.15
  595.8 5.5 copy-start.14
  601.3 3.7 copy-start.13
  605.0 3.3 copy-start.12
  608.2 3.6 copy-start.11
  611.9 3.6 copy-start.10
  615.5 3.9 copy-start.9
  626.0 3.7 copy-start.7
  629.4 7.5 %slice-start = ((s8[4456448]{0:T(1024)(128)(4,1)}), s8[4194304]{0:T(1024)(128)(4,1)S(1)}, s32[]{:S(2)}) async-start(s8[4456448]{0:T(1024)(128)(4,1)} %bitcast.37), calls=%async_computation | async-start | bytes 8388608
  629.4 7.5 %slice-start.2 = ((s8[5242880]{0:T(1024)(128)(4,1)}), s8[4194304]{0:T(1024)(128)(4,1)S(1)}, s32[]{:S(2)}) async-start(s8[5242880]{0:T(1024)(128)(4,1)} %bitcast.39), calls=%async_computation.2 | async-start | bytes 8388608
  629.4 9.4 %slice-start.4 = ((s8[6291456]{0:T(1024)(128)(4,1)}), s8[4194304]{0:T(1024)(128)(4,1)S(1)}, s32[]{:S(2)}) async-start(s8[6291456]{0:T(1024)(128)(4,1)} %bitcast.41), calls=%async_computation.4 | async-start | bytes 8388608
  629.7 9.1 %slice-start.1 = ((s8[4456448]{0:T(1024)(128)(4,1)}), s8[262144]{0:T(1024)(128)(4,1)S(1)}, s32[]{:S(2)}) async-start(s8[4456448]{0:T(1024)(128)(4,1)} %bitcast.37), calls=%async_computation.1 | async-start | bytes 524288
  629.7 9.5 %slice-start.3 = ((s8[5242880]{0:T(1024)(128)(4,1)}), s8[1048576]{0:T(1024)(128)(4,1)S(1)}, s32[]{:S(2)}) async-start(s8[5242880]{0:T(1024)(128)(4,1)} %bitcast.39), calls=%async_computation.3 | async-start | bytes 2097152
  629.7 10.1 %slice-start.5 = ((s8[6291456]{0:T(1024)(128)(4,1)}), s8[2097152]{0:T(1024)(128)(4,1)S(1)}, s32[]{:S(2)}) async-start(s8[6291456]{0:T(1024)(128)(4,1)} %bitcast.41), calls=%async_computation.5 | async-start | bytes 4194304
  629.8 10.1 %copy-start.19 = (f32[128]{0:T(128)S(1)}, f32[128]{0:T(128)}, u32[]{:S(2)}) copy-start(f32[128]{0:T(128)} %param.7) | copy-start | bytes 1540
  629.8 10.1 %copy-start.20 = (f32[128]{0:T(128)S(1)}, f32[128]{0:T(128)}, u32[]{:S(2)}) copy-start(f32[128]{0:T(128)} %broadcast_subtract_fusion) | copy-start | bytes 1540
  (5 other events, 8.6 us)
where the time goes:
time: 654 us; the launch traced here: 653 us
  waiting for transfers between devices  535 us (82%)
  other arithmetic  73.8 us (11%)
  local copies, waits for them, and re-layouts  28 us (4%)
  starting transfers between devices  15.6 us (2%)
    ppermute x6, waiting for transfers between devices, from_behind(): return lax.ppermute(value, axis, pairs)  465 us
    ppermute x2, waiting for transfers between devices, padded_2(): before = lax.ppermute(last, axis, up)  70 us
    select_n x9, other arithmetic, rotate_rows(): values = jnp.where(taken, jnp.roll(values, 1 << level, axis=last), values)  34.1 us
  transfers between devices with their start and end apart: 10, of which 6 were waited for; matrix products, arithmetic and copies ran while one was open for 4% of the time, Pallas kernels for 0%

commit v1 on v0

v1 whole, which is shorter than its diff:
```python
import functools

import jax
import jax.numpy as jnp
from jax import lax
from jax.experimental import pallas as pl
from jax.experimental.pallas import tpu as pltpu
from jax.sharding import PartitionSpec as P

FIELDS = 8
ROWS = 8
LANES = 128


def neighbours(value, axis, step, wrap):
    count = lax.axis_size(axis)
    pairs = [(i, i + step) for i in range(count)]
    if wrap:
        pairs = [(i, j % count) for i, j in pairs]
    else:
        pairs = [(i, j) for i, j in pairs if 0 <= j < count]
    return lax.ppermute(value, axis, pairs)


def shift_kernel(blocks, tiles, shift_ref, fraction_ref, x_ref, o_ref):
    total = blocks * tiles
    lane = lax.broadcasted_iota(jnp.int32, (FIELDS, LANES), 1)
    shifts = [shift_ref[row] for row in range(ROWS)]
    whole = [s // LANES for s in shifts]
    part = [s % LANES for s in shifts]
    fraction = [fraction_ref[row] for row in range(ROWS)]

    def place(row, tile):
        start = (tile // tiles) * (FIELDS * tiles * ROWS) + (tile % tiles) * ROWS + row
        return pl.ds(start, FIELDS, stride=tiles * ROWS)

    def turned(row, tile):
        tile = lax.rem(tile - whole[row] + 2 * total, total)
        return pltpu.roll(x_ref[place(row, tile), :], part[row], 1)

    def step(tile, row, carry):
        turned_before, moved_before = carry
        now = turned(row, tile)
        first = jnp.where(lane >= part[row], now, turned_before)
        rolled = pltpu.roll(first, 1, 1)
        second = jnp.where(lane >= 1, rolled, moved_before)
        value = (1.0 - fraction[row]) * first + fraction[row] * second
        return value, (now, rolled)

    carries = []
    for row in range(ROWS):
        before = turned(row, -2)
        _, carry = step(-1, row, (before, before))
        carries.append(carry)

    def body(block, carries):
        carries = list(carries)
        for t in range(tiles):
            for row in range(ROWS):
                value, carries[row] = step(block * tiles + t, row, carries[row])
                o_ref[place(row, block * tiles + t), :] = value
        return tuple(carries)

    lax.fori_loop(0, blocks, body, tuple(carries))


def shift_rows(received, shifts, fractions, blocks, tiles):
    flat = received.reshape(-1, LANES)
    out = pl.pallas_call(
        functools.partial(shift_kernel, blocks, tiles),
        out_shape=jax.ShapeDtypeStruct(flat.shape, flat.dtype),
        in_specs=[
            pl.BlockSpec(memory_space=pltpu.SMEM),
            pl.BlockSpec(memory_space=pltpu.SMEM),
            pl.BlockSpec(memory_space=pltpu.VMEM),
        ],
        out_specs=pl.BlockSpec(memory_space=pltpu.VMEM),
        cost_estimate=pl.CostEstimate(
            flops=8 * flat.size, bytes_accessed=8 * flat.size, transcendentals=0
        ),
        compiler_params=pltpu.CompilerParams(vmem_limit_bytes=24 * 2**20),
        name="shift_rows",
    )(shifts, fractions, flat)
    return out.reshape(received.shape)


def flux2(v_left, v_right, speed, q_left, q_right):
    return v_left * q_left + v_right * q_right - speed * (q_right - q_left)


def face_speed(v_left, v_right):
    return jnp.maximum(jnp.abs(v_left), jnp.abs(v_right)) + 1.0


def update_kernel(
    groups, width, density_ref, carried_ref, inner_ref, outer_ref, left_ref, right_ref, o_ref, lower_ref
):
    column = lax.broadcasted_iota(jnp.int32, (ROWS, width), 1)
    sub = lax.broadcasted_iota(jnp.int32, (ROWS, width), 0)

    def field(c, z, rows):
        return density_ref[z, rows, :] if c == 0 else carried_ref[c - 1, z, rows, :]

    def edge(ref, c, z):
        return jnp.broadcast_to(ref[c, z], (ROWS, width))

    def edge_velocity(ref, z):
        rho = edge(ref, 0, z)
        return edge(ref, 1, z) / jnp.where(rho == 0.0, 1.0, rho)

    for z in range(2):
        v_left = edge_velocity(inner_ref, z)
        v_right = field(1, z, pl.ds(0, ROWS)) / field(0, z, pl.ds(0, ROWS))
        v_right = jnp.broadcast_to(v_right[0:1], (ROWS, width))
        speed = face_speed(v_left, v_right)
        for c in range(FIELDS):
            q_right = jnp.broadcast_to(field(c, z, pl.ds(0, ROWS))[0:1], (ROWS, width))
            lower_ref[c, z] = flux2(v_left, v_right, speed, edge(inner_ref, c, z), q_right)

    def body(g, _):
        rows = pl.ds(pl.multiple_of(g * ROWS, ROWS), ROWS)
        after = pl.ds(pl.multiple_of(jnp.minimum(g + 1, groups - 1) * ROWS, ROWS), ROWS)
        last = g == groups - 1
        left, right = left_ref[rows, :], right_ref[rows, :]

        def at(block, c, z):
            return block[:, 2 * c + z : 2 * c + z + 1]

        rho = [field(0, z, rows) for z in range(2)]
        v_height = [field(3, z, rows) / rho[z] for z in range(2)]
        speed_height = 2.0 * face_speed(v_height[0], v_height[1])
        for z in range(2):
            other = 1 - z
            v_r = field(1, z, rows) / rho[z]
            v_a = field(2, z, rows) / rho[z]
            v_r_next = jnp.where(
                last, edge_velocity(outer_ref, z), field(1, z, after) / field(0, z, after)
            )
            v_r_up = pltpu.roll(jnp.where(sub == 0, v_r_next, v_r), ROWS - 1, 0)
            speed_r = face_speed(v_r, v_r_up)
            v_a_left = at(left, 2, z) / at(left, 0, z)
            v_a_right = at(right, 2, z) / at(right, 0, z)
            v_a_up = jnp.where(column == width - 1, v_a_right, pltpu.roll(v_a, width - 1, 1))
            speed_a = face_speed(v_a, v_a_up)
            speed_left = face_speed(v_a_left, v_a[:, 0:1])
            for c in range(FIELDS):
                q = field(c, z, rows)
                q_next = jnp.where(last, edge(outer_ref, c, z), field(c, z, after))
                q_up = pltpu.roll(jnp.where(sub == 0, q_next, q), ROWS - 1, 0)
                upper = flux2(v_r, v_r_up, speed_r, q, q_up)
                lower = pltpu.roll(jnp.where(sub == ROWS - 1, lower_ref[c, z], upper), 1, 0)
                lower_ref[c, z] = upper
                total = upper - lower
                q_up = jnp.where(column == width - 1, at(right, c, z), pltpu.roll(q, width - 1, 1))
                upper = flux2(v_a, v_a_up, speed_a, q, q_up)
                first = flux2(v_a_left, v_a[:, 0:1], speed_left, at(left, c, z), q[:, 0:1])
                lower = jnp.where(column == 0, first, pltpu.roll(upper, 1, 1))
                total = total + (upper - lower)
                total = total + speed_height * (q - field(c, other, rows))
                o_ref[c, z, rows, :] = 0.04 * total
        return 0

    lax.fori_loop(0, groups, body, 0)


def update_of(density, carried, inner, outer, left, right):
    rows, width = density.shape[1:]
    size = FIELDS * density.size
    vmem = pl.BlockSpec(memory_space=pltpu.VMEM)
    return pl.pallas_call(
        functools.partial(update_kernel, rows // ROWS, width),
        out_shape=jax.ShapeDtypeStruct((FIELDS,) + density.shape, density.dtype),
        in_specs=[vmem] * 6,
        out_specs=vmem,
        scratch_shapes=[pltpu.VMEM((FIELDS, 2, ROWS, width), jnp.float32)],
        cost_estimate=pl.CostEstimate(flops=40 * size, bytes_accessed=8 * size, transcendentals=0),
        compiler_params=pltpu.CompilerParams(vmem_limit_bytes=24 * 2**20),
        name="flux_update",
    )(density, carried, inner, outer, left, right)


def local(density, carried, cycle_shift, cycle_fraction):
    height, rows, width = density.shape
    devices = lax.axis_size("phi")
    groups, tiles = rows // ROWS, width // LANES
    state = jnp.concatenate([density[None], carried], axis=0)
    sent = state.reshape(FIELDS, height, groups, ROWS, tiles, LANES)
    sent = sent.transpose(2, 1, 0, 4, 3, 5).reshape(devices, FIELDS, tiles, ROWS, LANES)
    received = lax.all_to_all(sent, "phi", 0, 0, tiled=True)

    inner = neighbours(state[:, :, -1:], "rad", 1, False)
    outer = neighbours(state[:, :, :1], "rad", -1, False)
    left = neighbours(state[:, :, :, -1], "phi", 1, True)
    right = neighbours(state[:, :, :, 0], "phi", -1, True)
    left = left.reshape(FIELDS * height, rows).T
    right = right.reshape(FIELDS * height, rows).T
    update = update_of(density, carried, inner, outer, left, right)

    group = lax.axis_index("phi") // height
    shifts = lax.dynamic_slice_in_dim(cycle_shift, group * ROWS, ROWS)
    fractions = lax.dynamic_slice_in_dim(cycle_fraction, group * ROWS, ROWS)
    moved = shift_rows(received, shifts, fractions, devices, tiles)
    moved = lax.all_to_all(moved, "phi", 0, 0, tiled=True)
    moved = moved.reshape(groups, height, FIELDS, tiles, ROWS, LANES).transpose(2, 1, 0, 4, 3, 5)
    new_state = moved.reshape(state.shape) - update
    return new_state[0], new_state[1:]


def solution(mesh):
    placed = (P(None, "rad", "phi"), P(None, None, "rad", "phi"), P("rad"), P("rad"))
    return jax.shard_map(
        local,
        mesh=mesh,
        in_specs=placed,
        out_specs=(P(None, "rad", "phi"), P(None, None, "rad", "phi")),
        check_vma=False,
    )
```

time: 654 us -> 180 us (0.28)
  waiting for transfers between devices: 535 us -> 101 us
  other arithmetic: 73.8 us -> 8.87 us
  Pallas kernels: 0 us -> 28.9 us
  local copies, waits for them, and re-layouts: 28 us -> 12.7 us
  starting transfers between devices: 15.6 us -> 26.6 us
    ppermute x10 -> x4, waiting for transfers between devices: 535 us -> 39.7 us  [neighbours(): return lax.ppermute(value, axis, pairs)]
    all_to_all x0 -> x2, waiting for transfers between devices: none -> 61 us  [the longest x1 61 us: local(): received = lax.all_to_all(sent, 'phi', 0, 0, tiled=True)]
    select_n x14 -> x0, other arithmetic: 41.4 us -> none  [the longest x9 34.1 us: rotate_rows(): values = jnp.where(taken, jnp.roll(values, 1 << level, axis=last), values)]
    pallas_call x0 -> x2, Pallas kernels: none -> 28.9 us  [the longest x1 15.9 us: shift_rows(): pl.pallas_call(functools.partial(shift_kernel, blocks, tiles), out_shape=...]
    all_to_all x0 -> x2, starting transfers between devices: none -> 16 us  [the longest x1 11 us: local(): received = lax.all_to_all(sent, 'phi', 0, 0, tiled=True)]
    sub x5 -> x1, other arithmetic: 19.1 us -> 4.48 us  [local(): new_state = moved.reshape(state.shape) - update]
    slice x15 -> x2, local copies, waits for them, and re-layouts: 13.8 us -> 0.66 us  [the longest x1 0.33 us: local(): left = neighbours(state[:, :, :, -1], 'phi', 1, True)]
    ppermute x10 -> x4, starting transfers between devices: 15.6 us -> 10.6 us  [neighbours(): return lax.ppermute(value, axis, pairs)]
  transfers between devices with their start and end apart: 10 -> 6, of which waited for: 6 -> 2; matrix products, arithmetic and copies ran while one was open for 4% -> 1% of each run, Pallas kernels for 0% -> 7%
where the time goes in v1:
time: 180 us; the launch traced here: 179 us
  waiting for transfers between devices  101 us (56%)
  Pallas kernels  28.9 us (16%)
  starting transfers between devices  26.6 us (15%)
  local copies, waits for them, and re-layouts  12.7 us (7%)
  other arithmetic  8.87 us (5%)
    all_to_all x1, waiting for transfers between devices, local(): received = lax.all_to_all(sent, 'phi', 0, 0, tiled=True)  61 us
    ppermute x4, waiting for transfers between devices, neighbours(): return lax.ppermute(value, axis, pairs)  39.7 us
    pallas_call x1, Pallas kernels, shift_rows(): pl.pallas_call(functools.partial(shift_kernel, blocks, tiles), out_shape=...  15.9 us
    pallas_call x1, Pallas kernels, update_of(): pl.pallas_call(functools.partial(update_kernel, rows // ROWS, width), out...  13 us
    all_to_all x1, starting transfers between devices, local(): received = lax.all_to_all(sent, 'phi', 0, 0, tiled=True)  11 us
    ppermute x4, starting transfers between devices, neighbours(): return lax.ppermute(value, axis, pairs)  10.6 us
    unnamed x14, local copies, waits for them, and re-layouts  5.99 us
    all_to_all x1, starting transfers between devices, local(): moved = lax.all_to_all(moved, 'phi', 0, 0, tiled=True)  5 us
  transfers between devices with their start and end apart: 6, of which 2 were waited for; matrix products, arithmetic and copies ran while one was open for 1% of the time, Pallas kernels for 7%

profile of v1, /device:TPU:0, one launch (start us, length us, event | category | flops | bytes accessed | tf_op | source)
XLA Modules:
  0.0 178.5 jit_solution(6816133865952139419)
XLA Ops:
  0.6 2.7 %maximum_bitcast_fusion = f32[16,2,8,4,8,128]{5,4,3,0,1,2:T(8,128)S(1)} fusion(f32[7,2,16,8,4,128]{5,3,4,2,1,0:T(8,128)} %bitcast.21, f32[1,2,16,8,4,128]{5,3,4,2,1,0:T(8,128)} %bitcast.23), kind=kLoop, calls=%fused_computation | loop fusion | flops 1048576 | bytes 8388608 | tf_op jit(solution)/shard_map/transpose | solution.py:188
  3.4 2.6 %copy.9 = f32[16,2,8,4,8,128]{5,4,3,2,1,0:T(8,128)} copy(f32[16,2,8,4,8,128]{5,4,3,0,1,2:T(8,128)S(1)} %maximum_bitcast_fusion) | data formatting | bytes 8388608 | tf_op jit(solution)/shard_map/transpose | solution.py:188
  6.0 11.0 %all-to-all-start = ((f32[32,8,4,8,128]{4,3,2,1,0:T(8,128)}), f32[32,8,4,8,128]{4,3,2,1,0:T(8,128)}, u32[]{:S(2)}, u32[]{:S(2)}) async-start(f32[32,8,4,8,128]{4,3,2,1,0:T(8,128)} %bitcast.28), calls=%async_computation | async-start | bytes 8388608 | tf_op jit(solution)/shard_map/all_to_all | solution.py:189
  17.0 0.1 dynamic_slice.6.shift_ref
  17.1 0.1 dynamic_slice.7.fraction_ref
  17.2 61.0 %all-to-all-done = f32[32,8,4,8,128]{4,3,2,1,0:T(8,128)} async-done(((f32[32,8,4,8,128]{4,3,2,1,0:T(8,128)}), f32[32,8,4,8,128]{4,3,2,1,0:T(8,128)}, u32[]{:S(2)}, u32[]{:S(2)}) %all-to-all-start) | async-done | bytes 4194336 | tf_op jit(solution)/shard_map/all_to_all | solution.py:189
  78.2 15.9 %shift_rows.1 = f32[8192,128]{1,0:T(8,128)S(1)} custom-call(s32[8]{0:T(128)S(1)} %dynamic_slice.6.shift_ref, f32[8]{0:T(128)S(1)} %dynamic_slice.7.fraction_ref, f32[8192,128]{1,0:T(8,128)} %bitcast.4.x_ref), custom_call_target="tpu_custom_call" | custom-call | flops 8388608 | bytes 8388608 | tf_op jit(solution)/shard_map/shift_rows/pallas_call | solution.py:69
  94.1 2.0 %copy-done.3 = f32[8192,128]{1,0:T(8,128)} copy-done((f32[8192,128]{1,0:T(8,128)}, f32[8192,128]{1,0:T(8,128)S(1)}, u32[]{:S(2)}) %copy-start.3) | copy-done | bytes 4194328
  96.1 5.0 %all-to-all-start.1 = ((f32[32,8,4,8,128]{4,3,2,1,0:T(8,128)}), f32[32,8,4,8,128]{4,3,2,1,0:T(8,128)}, u32[]{:S(2)}, u32[]{:S(2)}) async-start(f32[32,8,4,8,128]{4,3,2,1,0:T(8,128)} %bitcast.22), calls=%async_computation.1 | async-start | bytes 8388608 | tf_op jit(solution)/shard_map/all_to_all | solution.py:203
  101.1 0.0 copy-start
  101.1 1.3 pad_maximum_fusion.2
  102.3 1.5 collective-permute-start
  103.9 1.3 collective-permute-start.1
  105.2 0.4 pad_maximum_fusion
  105.6 0.3 copy.11
  105.9 3.1 %collective-permute-start.2 = (f32[8,2,128]{2,0,1:T(8,128)S(1)}, f32[8,2,128]{2,0,1:T(8,128)S(1)}, u32[]{:S(2)}, u32[]{:S(2)}) collective-permute-start(f32[8,2,128]{2,0,1:T(8,128)S(1)} %bitcast.32), channel_id=1, source_target_pairs={{0,1},{1,2},{2,3},{3,4},{4,5},{5,6},{6,7},{7,8},{8,9},{9,10},{10,1... | collective-permute-start | bytes 24584 | tf_op jit(solution)/shard_map/ppermute | solution.py:22
  109.0 0.3 copy.14
  109.3 4.8 %collective-permute-start.3 = (f32[8,2,128]{2,0,1:T(8,128)S(1)}, f32[8,2,128]{2,0,1:T(8,128)S(1)}, u32[]{:S(2)}, u32[]{:S(2)}) collective-permute-start(f32[8,2,128]{2,0,1:T(8,128)S(1)} %bitcast.31), channel_id=1, source_target_pairs={{0,31},{1,0},{2,1},{3,2},{4,3},{5,4},{6,5},{7,6},{8,7},{9,8},{10,9... | collective-permute-start | bytes 24584 | tf_op jit(solution)/shard_map/ppermute | solution.py:22
  114.1 39.7 %collective-permute-done.2 = f32[8,2,128]{2,0,1:T(8,128)S(1)} collective-permute-done((f32[8,2,128]{2,0,1:T(8,128)S(1)}, f32[8,2,128]{2,0,1:T(8,128)S(1)}, u32[]{:S(2)}, u32[]{:S(2)}) %collective-permute-start.2) | collective-permute-done | bytes 8224 | tf_op jit(solution)/shard_map/ppermute | solution.py:22
  153.7 0.1 copy.13
  153.8 0.0 collective-permute-done.3
  153.8 0.1 copy.16
  153.9 0.0 collective-permute-done.inner_ref
  154.0 0.0 collective-permute-done.1.outer_ref
  154.0 0.0 copy-start.1
  154.0 2.0 %copy-done.1 = f32[7,2,128,512]{3,2,1,0:T(8,128)S(1)} copy-done((f32[7,2,128,512]{3,2,1,0:T(8,128)S(1)}, f32[7,2,128,512]{3,2,1,0:T(8,128)}, u32[]{:S(2)}) %copy-start.1) | copy-done | bytes 3670040
  156.0 13.0 %flux_update.1 = f32[8,2,128,512]{3,2,1,0:T(8,128)S(1)} custom-call(f32[2,128,512]{2,1,0:T(8,128)S(1)} %copy-done.4, f32[7,2,128,512]{3,2,1,0:T(8,128)S(1)} %copy-done.1, f32[8,2,1,512]{3,2,1,0:T(1,128)S(1)} %collective-permute-done.inner_ref, f32[8,2,1,512]{3,2,1,0:T(1,128)S(1)} %collective-permute-done.1.outer_ref, f32[128,16]{1,0:T(8,128)S(1)} %bitcast.26, ...), custom_call_target="tpu_custom_call" | custom-call | flops 41943040 | bytes 8388608 | tf_op jit(solution)/shard_map/flux_update/pallas_call | solution.py:170
  169.0 2.0 %copy-done.2 = f32[8,2,128,512]{3,2,1,0:T(8,128)} copy-done((f32[8,2,128,512]{3,2,1,0:T(8,128)}, f32[8,2,128,512]{3,2,1,0:T(8,128)S(1)}, u32[]{:S(2)}) %copy-start.2) | copy-done | bytes 4194328
  171.0 0.0 all-to-all-done.1
  171.0 4.5 %bitcast_subtract_fusion = f32[8,2,128,512]{3,2,1,0:T(8,128)S(1)} fusion(f32[8,2,128,512]{3,2,1,0:T(8,128)} %copy-done.2, f32[8,2,16,8,4,128]{5,3,4,0,1,2:T(8,128)} %bitcast.7), kind=kLoop, calls=%fused_computation.1 | loop fusion | flops 1048576 | bytes 12582912 | tf_op jit(solution)/shard_map/sub | solution.py:205
  175.5 2.2 %slice.25 = f32[7,2,128,512]{3,2,1,0:T(8,128)} slice(f32[8,2,128,512]{3,2,1,0:T(8,128)S(1)} %bitcast_subtract_fusion), slice={[1:8], [0:2], [0:128], [0:512]} | slice | bytes 7340032 | tf_op jit(solution)/shard_map/slice | solution.py:206
  177.7 0.8 slice_bitcast_fusion
  (11 shorter events, 0.0 us)
Async XLA Ops:
  6.0 11.0 %copy-start.5 = (s32[128]{0:T(128)S(1)}, s32[128]{0:T(128)}, u32[]{:S(2)}) copy-start(s32[128]{0:T(128)} %param.6) | copy-start | bytes 1540
  6.0 11.1 %copy-start.6 = (f32[128]{0:T(128)S(1)}, f32[128]{0:T(128)}, u32[]{:S(2)}) copy-start(f32[128]{0:T(128)} %param.7) | copy-start | bytes 1540
  6.0 72.2 %all-to-all-start = ((f32[32,8,4,8,128]{4,3,2,1,0:T(8,128)}), f32[32,8,4,8,128]{4,3,2,1,0:T(8,128)}, u32[]{:S(2)}, u32[]{:S(2)}) async-start(f32[32,8,4,8,128]{4,3,2,1,0:T(8,128)} %bitcast.28), calls=%async_computation | async-start | bytes 8388608 | tf_op jit(solution)/shard_map/all_to_all | solution.py:189
  94.1 2.0 %copy-start.3 = (f32[8192,128]{1,0:T(8,128)}, f32[8192,128]{1,0:T(8,128)S(1)}, u32[]{:S(2)}) copy-start(f32[8192,128]{1,0:T(8,128)S(1)} %shift_rows.1) | copy-start | bytes 12582916
  96.1 5.0 %copy-start.4 = (f32[2,128,512]{2,1,0:T(8,128)S(1)}, f32[2,128,512]{2,1,0:T(8,128)}, u32[]{:S(2)}) copy-start(f32[2,128,512]{2,1,0:T(8,128)} %density_ref.1) | copy-start | bytes 1572868
  96.1 75.0 %all-to-all-start.1 = ((f32[32,8,4,8,128]{4,3,2,1,0:T(8,128)}), f32[32,8,4,8,128]{4,3,2,1,0:T(8,128)}, u32[]{:S(2)}, u32[]{:S(2)}) async-start(f32[32,8,4,8,128]{4,3,2,1,0:T(8,128)} %bitcast.22), calls=%async_computation.1 | async-start | bytes 8388608 | tf_op jit(solution)/shard_map/all_to_all | solution.py:203
  101.1 4.1 %copy-start = (f32[7,2,128,512]{3,2,1,0:T(8,128)S(1)}, f32[7,2,128,512]{3,2,1,0:T(8,128)}, u32[]{:S(2)}) copy-start(f32[7,2,128,512]{3,2,1,0:T(8,128)} %carried_ref.1) | copy-start | bytes 11010052
  102.3 51.6 %collective-permute-start = (f32[8,2,1,512]{3,2,1,0:T(1,128)S(1)}, f32[8,2,1,512]{3,2,1,0:T(1,128)S(1)}, u32[]{:S(2)}, u32[]{:S(2)}) collective-permute-start(f32[8,2,1,512]{3,2,1,0:T(1,128)S(1)} %get-tuple-element.5), channel_id=1, source_target_pairs={{0,32},{32,64},{64,96},{1,33},{33,65},{65,97},{2,34},{34,66},{66,9... | collective-permute-start | bytes 98312 | tf_op jit(solution)/shard_map/ppermute | solution.py:22
  103.9 50.1 %collective-permute-start.1 = (f32[8,2,1,512]{3,2,1,0:T(1,128)S(1)}, f32[8,2,1,512]{3,2,1,0:T(1,128)S(1)}, u32[]{:S(2)}, u32[]{:S(2)}) collective-permute-start(f32[8,2,1,512]{3,2,1,0:T(1,128)S(1)} %get-tuple-element.4), channel_id=1, source_target_pairs={{32,0},{64,32},{96,64},{33,1},{65,33},{97,65},{34,2},{66,34},{98,6... | collective-permute-start | bytes 98312 | tf_op jit(solution)/shard_map/ppermute | solution.py:22
  105.9 47.8 %collective-permute-start.2 = (f32[8,2,128]{2,0,1:T(8,128)S(1)}, f32[8,2,128]{2,0,1:T(8,128)S(1)}, u32[]{:S(2)}, u32[]{:S(2)}) collective-permute-start(f32[8,2,128]{2,0,1:T(8,128)S(1)} %bitcast.32), channel_id=1, source_target_pairs={{0,1},{1,2},{2,3},{3,4},{4,5},{5,6},{6,7},{7,8},{8,9},{9,10},{10,1... | collective-permute-start | bytes 24584 | tf_op jit(solution)/shard_map/ppermute | solution.py:22
  109.3 44.5 %collective-permute-start.3 = (f32[8,2,128]{2,0,1:T(8,128)S(1)}, f32[8,2,128]{2,0,1:T(8,128)S(1)}, u32[]{:S(2)}, u32[]{:S(2)}) collective-permute-start(f32[8,2,128]{2,0,1:T(8,128)S(1)} %bitcast.31), channel_id=1, source_target_pairs={{0,31},{1,0},{2,1},{3,2},{4,3},{5,4},{6,5},{7,6},{8,7},{9,8},{10,9... | collective-permute-start | bytes 24584 | tf_op jit(solution)/shard_map/ppermute | solution.py:22
  154.0 2.0 %copy-start.1 = (f32[7,2,128,512]{3,2,1,0:T(8,128)S(1)}, f32[7,2,128,512]{3,2,1,0:T(8,128)}, u32[]{:S(2)}) copy-start(f32[7,2,128,512]{3,2,1,0:T(8,128)} %carried_ref.1) | copy-start | bytes 11010052
  169.0 2.0 %copy-start.2 = (f32[8,2,128,512]{3,2,1,0:T(8,128)}, f32[8,2,128,512]{3,2,1,0:T(8,128)S(1)}, u32[]{:S(2)}) copy-start(f32[8,2,128,512]{3,2,1,0:T(8,128)S(1)} %flux_update.1) | copy-start | bytes 12582916

commit v2 on v1

--- a/solution.py
+++ b/solution.py
@@ -22,21 +22,108 @@
     return lax.ppermute(value, axis, pairs)
 
 
-def shift_kernel(blocks, tiles, shift_ref, fraction_ref, x_ref, o_ref):
+def in_hbm(value):
+    return pltpu.with_memory_space_constraint(value, pltpu.HBM)
+
+
+def pack_kernel(groups, height, chunks, density_ref, carried_ref, o_ref, taken, packed, in_sems, out_sems):
+    size = groups // chunks
+    arrivals, departures = [], []
+    for i in range(chunks):
+        piece = pl.ds(i * size, size)
+        ends = ((density_ref.at[:, piece], taken.at[0, :, piece]), (carried_ref.at[:, :, piece], taken.at[1:, :, piece]))
+        arrivals.append([pltpu.make_async_copy(*pair, in_sems.at[i, k]) for k, pair in enumerate(ends)])
+        for copy in arrivals[i]:
+            copy.start()
+    for i in range(chunks):
+        piece = pl.ds(i * size, size)
+        for copy in arrivals[i]:
+            copy.wait()
+
+        def reorder(g, _):
+            for z in range(height):
+                for c in range(FIELDS):
+                    packed[g, z, c] = taken[c, z, g]
+            return 0
+
+        lax.fori_loop(i * size, (i + 1) * size, reorder, 0)
+        departures.append(pltpu.make_async_copy(packed.at[piece], o_ref.at[piece], out_sems.at[i]))
+        departures[i].start()
+    for copy in departures:
+        copy.wait()
+
+
+def pack(density, carried, chunks=8):
+    height, rows, width = density.shape
+    groups = rows // ROWS
+    natural = (height, groups, ROWS, width)
+    shape = (groups, height, FIELDS, ROWS, width)
+    hbm = pl.BlockSpec(memory_space=pltpu.HBM)
+    return pl.pallas_call(
+        functools.partial(pack_kernel, groups, height, chunks),
+        out_shape=pltpu.HBM(shape, density.dtype),
+        in_specs=[hbm, hbm],
+        out_specs=hbm,
+        scratch_shapes=[
+            pltpu.VMEM((FIELDS,) + natural, jnp.float32),
+            pltpu.VMEM(shape, jnp.float32),
+            pltpu.SemaphoreType.DMA((chunks, 2)),
+            pltpu.SemaphoreType.DMA((chunks,)),
+        ],
+        cost_estimate=pl.CostEstimate(flops=0, bytes_accessed=64 * density.size, transcendentals=0),
+        compiler_params=pltpu.CompilerParams(vmem_limit_bytes=12 * 2**20),
+        name="pack",
+    )(in_hbm(density.reshape(natural)), in_hbm(carried.reshape((FIELDS - 1,) + natural)))
+
+
+def exchanged(registers, sub):
+    values = list(registers)
+    for k in (4, 2, 1):
+        low = (sub & k) == 0
+        result = list(values)
+        for i in range(ROWS):
+            if not i & k:
+                a, b = values[i], values[i + k]
+                result[i] = jnp.where(low, a, pltpu.roll(b, k, 0))
+                result[i + k] = jnp.where(low, pltpu.roll(a, ROWS - k, 0), b)
+        values = result
+    return values
+
+
+def shift_kernel(
+    blocks, tiles, chunks, shift_ref, fraction_ref, x_ref, o_ref, taken, cycles, placed, in_sems, out_sems
+):
+    size = blocks // chunks
     total = blocks * tiles
     lane = lax.broadcasted_iota(jnp.int32, (FIELDS, LANES), 1)
+    sub = lax.broadcasted_iota(jnp.int32, (FIELDS, LANES), 0)
     shifts = [shift_ref[row] for row in range(ROWS)]
     whole = [s // LANES for s in shifts]
     part = [s % LANES for s in shifts]
     fraction = [fraction_ref[row] for row in range(ROWS)]
 
-    def place(row, tile):
-        start = (tile // tiles) * (FIELDS * tiles * ROWS) + (tile % tiles) * ROWS + row
-        return pl.ds(start, FIELDS, stride=tiles * ROWS)
+    def lanes(t):
+        return pl.ds(t * LANES, LANES)
+
+    arrivals = []
+    for i in range(chunks):
+        piece = pl.ds(i * size, size)
+        arrivals.append(pltpu.make_async_copy(x_ref.at[piece], taken.at[piece], in_sems.at[i]))
+        arrivals[i].start()
+
+    def collect(block, _):
+        for t in range(tiles):
+            by_row = exchanged([taken[block, c, :, lanes(t)] for c in range(FIELDS)], sub)
+            for row in range(ROWS):
+                cycles[row, block * tiles + t] = by_row[row]
+        return 0
+
+    for i in range(chunks):
+        arrivals[i].wait()
+        lax.fori_loop(i * size, (i + 1) * size, collect, 0, unroll=4)
 
     def turned(row, tile):
-        tile = lax.rem(tile - whole[row] + 2 * total, total)
-        return pltpu.roll(x_ref[place(row, tile), :], part[row], 1)
+        return pltpu.roll(cycles[row, (tile - whole[row]) & (total - 1)], part[row], 1)
 
     def step(tile, row, carry):
         turned_before, moved_before = carry
@@ -47,41 +134,113 @@
         value = (1.0 - fraction[row]) * first + fraction[row] * second
         return value, (now, rolled)
 
+    def place(block, carries):
+        carries = list(carries)
+        for t in range(tiles):
+            by_row = []
+            for row in range(ROWS):
+                value, carries[row] = step(block * tiles + t, row, carries[row])
+                by_row.append(value)
+            by_field = exchanged(by_row, sub)
+            for c in range(FIELDS):
+                placed[block, c, :, lanes(t)] = by_field[c]
+        return tuple(carries)
+
     carries = []
     for row in range(ROWS):
         before = turned(row, -2)
-        _, carry = step(-1, row, (before, before))
-        carries.append(carry)
-
-    def body(block, carries):
-        carries = list(carries)
-        for t in range(tiles):
-            for row in range(ROWS):
-                value, carries[row] = step(block * tiles + t, row, carries[row])
-                o_ref[place(row, block * tiles + t), :] = value
-        return tuple(carries)
-
-    lax.fori_loop(0, blocks, body, tuple(carries))
-
-
-def shift_rows(received, shifts, fractions, blocks, tiles):
-    flat = received.reshape(-1, LANES)
-    out = pl.pallas_call(
-        functools.partial(shift_kernel, blocks, tiles),
-        out_shape=jax.ShapeDtypeStruct(flat.shape, flat.dtype),
-        in_specs=[
-            pl.BlockSpec(memory_space=pltpu.SMEM),
-            pl.BlockSpec(memory_space=pltpu.SMEM),
-            pl.BlockSpec(memory_space=pltpu.VMEM),
+        carries.append(step(-1, row, (before, before))[1])
+    carries = tuple(carries)
+    departures = []
+    for i in range(chunks):
+        piece = pl.ds(i * size, size)
+        carries = lax.fori_loop(i * size, (i + 1) * size, place, carries, unroll=4)
+        departures.append(pltpu.make_async_copy(placed.at[piece], o_ref.at[piece], out_sems.at[i]))
+        departures[i].start()
+    for copy in departures:
+        copy.wait()
+
+
+def shift_rows(received, shifts, fractions, chunks=8):
+    blocks, _, _, width = received.shape
+    tiles = width // LANES
+    smem, hbm = pl.BlockSpec(memory_space=pltpu.SMEM), pl.BlockSpec(memory_space=pltpu.HBM)
+    return pl.pallas_call(
+        functools.partial(shift_kernel, blocks, tiles, chunks),
+        out_shape=pltpu.HBM(received.shape, received.dtype),
+        in_specs=[smem, smem, hbm],
+        out_specs=hbm,
+        scratch_shapes=[
+            pltpu.VMEM(received.shape, jnp.float32),
+            pltpu.VMEM((ROWS, blocks * tiles, FIELDS, LANES), jnp.float32),
+            pltpu.VMEM(received.shape, jnp.float32),
+            pltpu.SemaphoreType.DMA((chunks,)),
+            pltpu.SemaphoreType.DMA((chunks,)),
         ],
-        out_specs=pl.BlockSpec(memory_space=pltpu.VMEM),
         cost_estimate=pl.CostEstimate(
-            flops=8 * flat.size, bytes_accessed=8 * flat.size, transcendentals=0
+            flops=8 * received.size, bytes_accessed=8 * received.size, transcendentals=0
         ),
-        compiler_params=pltpu.CompilerParams(vmem_limit_bytes=24 * 2**20),
+        compiler_params=pltpu.CompilerParams(vmem_limit_bytes=20 * 2**20),
         name="shift_rows",
-    )(shifts, fractions, flat)
-    return out.reshape(received.shape)
+    )(shifts, fractions, in_hbm(received))
+
+
+def finish_kernel(groups, height, chunks, moved_ref, update_ref, density_ref, carried_ref, taken, change, new, in_sems, out_sems):
+    size = groups // chunks
+    arrivals, departures = [], []
+    for i in range(chunks):
+        piece = pl.ds(i * size, size)
+        arrivals.append(
+            (
+                pltpu.make_async_copy(moved_ref.at[piece], taken.at[piece], in_sems.at[i, 0]),
+                pltpu.make_async_copy(update_ref.at[:, :, piece], change.at[:, :, piece], in_sems.at[i, 1]),
+            )
+        )
+        for copy in arrivals[i]:
+            copy.start()
+    for i in range(chunks):
+        piece = pl.ds(i * size, size)
+        for copy in arrivals[i]:
+            copy.wait()
+
+        def subtract(g, _):
+            for z in range(height):
+                for c in range(FIELDS):
+                    new[c, z, g] = taken[g, z, c] - change[c, z, g]
+            return 0
+
+        lax.fori_loop(i * size, (i + 1) * size, subtract, 0)
+        ends = ((new.at[0, :, piece], density_ref.at[:, piece]), (new.at[1:, :, piece], carried_ref.at[:, :, piece]))
+        for k, (source, target) in enumerate(ends):
+            departures.append(pltpu.make_async_copy(source, target, out_sems.at[i, k]))
+            departures[-1].start()
+    for copy in departures:
+        copy.wait()
+
+
+def finish(moved, update, chunks=8):
+    groups, height, _, _, width = moved.shape
+    hbm = pl.BlockSpec(memory_space=pltpu.HBM)
+    natural = (height, groups, ROWS, width)
+    return pl.pallas_call(
+        functools.partial(finish_kernel, groups, height, chunks),
+        out_shape=[
+            jax.ShapeDtypeStruct(natural, jnp.float32),
+            jax.ShapeDtypeStruct((FIELDS - 1,) + natural, jnp.float32),
+        ],
+        in_specs=[hbm, hbm],
+        out_specs=[hbm, hbm],
+        scratch_shapes=[
+            pltpu.VMEM(moved.shape, jnp.float32),
+            pltpu.VMEM((FIELDS,) + natural, jnp.float32),
+            pltpu.VMEM((FIELDS,) + natural, jnp.float32),
+            pltpu.SemaphoreType.DMA((chunks, 2)),
+            pltpu.SemaphoreType.DMA((chunks, 2)),
+        ],
+        cost_estimate=pl.CostEstimate(flops=moved.size, bytes_accessed=12 * moved.size, transcendentals=0),
+        compiler_params=pltpu.CompilerParams(vmem_limit_bytes=20 * 2**20),
+        name="finish",
+    )(in_hbm(moved), in_hbm(update.reshape((FIELDS,) + natural)))
 
 
 def flux2(v_left, v_right, speed, q_left, q_right):
@@ -169,7 +328,7 @@
     vmem = pl.BlockSpec(memory_space=pltpu.VMEM)
     return pl.pallas_call(
         functools.partial(update_kernel, rows // ROWS, width),
-        out_shape=jax.ShapeDtypeStruct((FIELDS,) + density.shape, density.dtype),
+        out_shape=pltpu.HBM((FIELDS,) + density.shape, density.dtype),
         in_specs=[vmem] * 6,
         out_specs=vmem,
         scratch_shapes=[pltpu.VMEM((FIELDS, 2, ROWS, width), jnp.float32)],
@@ -182,28 +341,33 @@
 def local(density, carried, cycle_shift, cycle_fraction):
     height, rows, width = density.shape
     devices = lax.axis_size("phi")
-    groups, tiles = rows // ROWS, width // LANES
+    packed = pack(density, carried)
+    received = lax.all_to_all(
+        packed.reshape(devices, FIELDS, ROWS, width), "phi", 0, 0, tiled=True
+    )
+
     state = jnp.concatenate([density[None], carried], axis=0)
-    sent = state.reshape(FIELDS, height, groups, ROWS, tiles, LANES)
-    sent = sent.transpose(2, 1, 0, 4, 3, 5).reshape(devices, FIELDS, tiles, ROWS, LANES)
-    received = lax.all_to_all(sent, "phi", 0, 0, tiled=True)
-
     inner = neighbours(state[:, :, -1:], "rad", 1, False)
     outer = neighbours(state[:, :, :1], "rad", -1, False)
     left = neighbours(state[:, :, :, -1], "phi", 1, True)
     right = neighbours(state[:, :, :, 0], "phi", -1, True)
     left = left.reshape(FIELDS * height, rows).T
     right = right.reshape(FIELDS * height, rows).T
-    update = update_of(density, carried, inner, outer, left, right)
 
     group = lax.axis_index("phi") // height
     shifts = lax.dynamic_slice_in_dim(cycle_shift, group * ROWS, ROWS)
     fractions = lax.dynamic_slice_in_dim(cycle_fraction, group * ROWS, ROWS)
-    moved = shift_rows(received, shifts, fractions, devices, tiles)
+    received, inner, outer, left, right = lax.optimization_barrier(
+        (received, inner, outer, left, right)
+    )
+    moved = shift_rows(received, shifts, fractions)
+    moved, inner, outer, left, right = lax.optimization_barrier(
+        (moved, inner, outer, left, right)
+    )
     moved = lax.all_to_all(moved, "phi", 0, 0, tiled=True)
-    moved = moved.reshape(groups, height, FIELDS, tiles, ROWS, LANES).transpose(2, 1, 0, 4, 3, 5)
-    new_state = moved.reshape(state.shape) - update
-    return new_state[0], new_state[1:]
+    update = update_of(density, carried, inner, outer, left, right)
+    density_next, carried_next = finish(moved.reshape(packed.shape), update)
+    return density_next.reshape(density.shape), carried_next.reshape(carried.shape)
 
 
 def solution(mesh):

time: 180 us -> 154 us (0.86)
  waiting for transfers between devices: 101 us -> 89.7 us
  local copies, waits for them, and re-layouts: 12.7 us -> 3.08 us
  other arithmetic: 8.87 us -> 1.64 us
    all_to_all x1, waiting for transfers between devices: 61 us -> 8.02 us  [local(): lax.all_to_all(packed.reshape(devices, FIELDS, ROWS, width), 'phi', 0, 0,...]
    all_to_all x1, waiting for transfers between devices: 0.01 us -> 43.4 us  [local(): moved = lax.all_to_all(moved, 'phi', 0, 0, tiled=True)]
    sub x1 -> x0, other arithmetic: 4.48 us -> none  [local(): new_state = moved.reshape(state.shape) - update]
    unnamed x14 -> x10, local copies, waits for them, and re-layouts: 5.99 us -> 2.06 us
    transpose x1 -> x0, other arithmetic: 2.75 us -> none  [local(): sent.transpose(2, 1, 0, 4, 3, 5)]
    transpose x1 -> x0, local copies, waits for them, and re-layouts: 2.62 us -> none  [local(): sent.transpose(2, 1, 0, 4, 3, 5)]
    slice x1 -> x0, local copies, waits for them, and re-layouts: 2.21 us -> none  [local(): return (new_state[0], new_state[1:])]
    pallas_call x1, Pallas kernels: 13 us -> 15 us  [update_of(): pl.pallas_call(functools.partial(update_kernel, rows // ROWS, width), out...]
  transfers between devices with their start and end apart: 6 -> 6, of which waited for: 2 -> 4; matrix products, arithmetic and copies ran while one was open for 1% -> 2% of each run, Pallas kernels for 7% -> 10%
where the time goes in v2:
time: 154 us
  waiting for transfers between devices  89.7 us (58%)
  Pallas kernels  30.3 us (20%)
  starting transfers between devices  27.9 us (18%)
  local copies, waits for them, and re-layouts  3.08 us (2%)
  other arithmetic  1.64 us (1%)
    all_to_all x1, waiting for transfers between devices, local(): moved = lax.all_to_all(moved, 'phi', 0, 0, tiled=True)  43.4 us
    ppermute x4, waiting for transfers between devices, neighbours(): return lax.ppermute(value, axis, pairs)  38.3 us
    pallas_call x1, Pallas kernels, update_of(): pl.pallas_call(functools.partial(update_kernel, rows // ROWS, width), out...  15 us
    ppermute x4, starting transfers between devices, neighbours(): return lax.ppermute(value, axis, pairs)  12.1 us
    all_to_all x1, starting transfers between devices, local(): lax.all_to_all(packed.reshape(devices, FIELDS, ROWS, width), 'phi', 0, 0,...  11 us
    all_to_all x1, waiting for transfers between devices, local(): lax.all_to_all(packed.reshape(devices, FIELDS, ROWS, width), 'phi', 0, 0,...  8.02 us
    pallas_call x1, Pallas kernels, shift_rows(): pl.pallas_call(functools.partial(shift_kernel, blocks, tiles, chunks), ou...  6.22 us
    pallas_call x1, Pallas kernels, finish(): pl.pallas_call(functools.partial(finish_kernel, groups, height, chunks),...  5.44 us
  transfers between devices with their start and end apart: 6, of which 4 were waited for; matrix products, arithmetic and copies ran while one was open for 2% of the time, Pallas kernels for 10%

profile of v2, /device:TPU:0, one launch (start us, length us, event | category | flops | bytes accessed | tf_op | source)
XLA Modules:
  0.0 153.5 jit_solution(17760809490769764507)
XLA Ops:
  0.6 3.7 %pack.1 = f32[16,2,8,8,512]{4,3,2,1,0:T(8,128)} custom-call(f32[2,16,8,512]{3,2,1,0:T(8,128)} %bitcast.15, f32[7,2,16,8,512]{4,3,2,1,0:T(8,128)} %bitcast.14), custom_call_target="tpu_custom_call" | custom-call | bytes 8388608 | tf_op jit(solution)/shard_map/pack/pallas_call | solution.py:62
  4.3 0.0 copy-start.2
  4.3 11.0 %all-to-all-start = ((f32[32,8,8,512]{3,2,1,0:T(8,128)}), f32[32,8,8,512]{3,2,1,0:T(8,128)}, u32[]{:S(2)}, u32[]{:S(2)}) async-start(f32[32,8,8,512]{3,2,1,0:T(8,128)} %bitcast.20), calls=%async_computation | async-start | bytes 8388608 | tf_op jit(solution)/shard_map/all_to_all | solution.py:345
  15.3 0.0 copy-start
  15.3 0.0 copy-done.2
  15.3 1.3 pad_maximum_fusion.2
  16.6 1.4 collective-permute-start.1
  18.0 0.0 copy-start.3
  18.0 0.0 copy-start.4
  18.0 3.0 %collective-permute-start = (f32[8,2,1,512]{3,2,1,0:T(1,128)S(1)}, f32[8,2,1,512]{3,2,1,0:T(1,128)S(1)}, u32[]{:S(2)}, u32[]{:S(2)}) collective-permute-start(f32[8,2,1,512]{3,2,1,0:T(1,128)S(1)} %get-tuple-element.29), channel_id=1, source_target_pairs={{0,32},{32,64},{64,96},{1,33},{33,65},{65,97},{2,34},{34,66},{66,9... | collective-permute-start | bytes 98312 | tf_op jit(solution)/shard_map/ppermute | solution.py:22
  21.1 0.0 copy-done
  21.1 0.4 pad_maximum_fusion
  21.5 0.3 copy.11
  21.8 7.6 %collective-permute-start.3 = (f32[8,2,128]{2,0,1:T(8,128)S(1)}, f32[8,2,128]{2,0,1:T(8,128)S(1)}, u32[]{:S(2)}, u32[]{:S(2)}) collective-permute-start(f32[8,2,128]{2,0,1:T(8,128)S(1)} %bitcast.25), channel_id=1, source_target_pairs={{0,31},{1,0},{2,1},{3,2},{4,3},{5,4},{6,5},{7,6},{8,7},{9,8},{10,9... | collective-permute-start | bytes 24584 | tf_op jit(solution)/shard_map/ppermute | solution.py:22
  29.4 0.3 copy.8
  29.7 0.0 collective-permute-start.2
  29.8 0.1 dynamic_slice.6.shift_ref
  29.9 0.1 dynamic_slice.7.fraction_ref
  29.9 26.6 %collective-permute-done.3 = f32[8,2,128]{2,0,1:T(8,128)S(1)} collective-permute-done((f32[8,2,128]{2,0,1:T(8,128)S(1)}, f32[8,2,128]{2,0,1:T(8,128)S(1)}, u32[]{:S(2)}, u32[]{:S(2)}) %collective-permute-start.3) | collective-permute-done | bytes 8224 | tf_op jit(solution)/shard_map/ppermute | solution.py:22
  56.5 0.1 copy.13
  56.6 11.7 %collective-permute-done.2 = f32[8,2,128]{2,0,1:T(8,128)S(1)} collective-permute-done((f32[8,2,128]{2,0,1:T(8,128)S(1)}, f32[8,2,128]{2,0,1:T(8,128)S(1)}, u32[]{:S(2)}, u32[]{:S(2)}) %collective-permute-start.2) | collective-permute-done | bytes 8224 | tf_op jit(solution)/shard_map/ppermute | solution.py:22
  68.4 0.1 copy.10
  68.5 0.0 collective-permute-done.1.outer_ref
  68.5 0.0 collective-permute-done.inner_ref
  68.5 8.0 %all-to-all-done.x_ref = f32[32,8,8,512]{3,2,1,0:T(8,128)} async-done(((f32[32,8,8,512]{3,2,1,0:T(8,128)}), f32[32,8,8,512]{3,2,1,0:T(8,128)}, u32[]{:S(2)}, u32[]{:S(2)}) %all-to-all-start) | async-done | bytes 4194336 | tf_op jit(solution)/shard_map/all_to_all | solution.py:345
  76.5 6.2 %shift_rows.1 = f32[32,8,8,512]{3,2,1,0:T(8,128)} custom-call(s32[8]{0:T(128)S(1)} %dynamic_slice.6.shift_ref, f32[8]{0:T(128)S(1)} %dynamic_slice.7.fraction_ref, f32[32,8,8,512]{3,2,1,0:T(8,128)} %all-to-all-done.x_ref), custom_call_target="tpu_custom_call" | custom-call | flops 8388608 | bytes 8388608 | tf_op jit(solution)/shard_map/shift_rows/pallas_call | solution.py:168
  82.7 4.9 %all-to-all-start.1 = ((f32[32,8,8,512]{3,2,1,0:T(8,128)}), f32[32,8,8,512]{3,2,1,0:T(8,128)}, u32[]{:S(2)}, u32[]{:S(2)}) async-start(f32[32,8,8,512]{3,2,1,0:T(8,128)} %shift_rows.1), calls=%async_computation.1 | async-start | bytes 8388608 | tf_op jit(solution)/shard_map/all_to_all | solution.py:367
  87.6 0.0 copy-start.1
  87.6 2.0 %copy-done.1 = f32[7,2,128,512]{3,2,1,0:T(8,128)S(1)} copy-done((f32[7,2,128,512]{3,2,1,0:T(8,128)S(1)}, f32[7,2,128,512]{3,2,1,0:T(8,128)}, u32[]{:S(2)}) %copy-start.1) | copy-done | bytes 3670040
  89.6 15.0 %flux_update.1 = f32[8,2,128,512]{3,2,1,0:T(8,128)} custom-call(f32[2,128,512]{2,1,0:T(8,128)S(1)} %copy-done.2, f32[7,2,128,512]{3,2,1,0:T(8,128)S(1)} %copy-done.1, f32[8,2,1,512]{3,2,1,0:T(1,128)S(1)} %collective-permute-done.inner_ref, f32[8,2,1,512]{3,2,1,0:T(1,128)S(1)} %collective-permute-done.1.outer_ref, f32[128,16]{1,0:T(8,128)S(1)} %bitcast.19, ...), custom_call_target="tpu_custom_call" | custom-call | flops 41943040 | bytes 8388608 | tf_op jit(solution)/shard_map/flux_update/pallas_call | solution.py:329
  104.6 43.4 %all-to-all-done.1 = f32[32,8,8,512]{3,2,1,0:T(8,128)} async-done(((f32[32,8,8,512]{3,2,1,0:T(8,128)}), f32[32,8,8,512]{3,2,1,0:T(8,128)}, u32[]{:S(2)}, u32[]{:S(2)}) %all-to-all-start.1) | async-done | bytes 4194336 | tf_op jit(solution)/shard_map/all_to_all | solution.py:367
  148.1 5.4 %finish.1 = (f32[2,16,8,512]{3,2,1,0:T(8,128)}, f32[7,2,16,8,512]{4,3,2,1,0:T(8,128)}) custom-call(f32[16,2,8,8,512]{4,3,2,1,0:T(8,128)} %bitcast.10.moved_ref, f32[8,2,16,8,512]{4,3,2,1,0:T(8,128)} %bitcast.21), custom_call_target="tpu_custom_call" | custom-call | flops 1048576 | bytes 12582912 | tf_op jit(solution)/shard_map/finish/pallas_call | solution.py:225
  (4 shorter events, 0.0 us)
Async XLA Ops:
  4.3 11.0 %copy-start.2 = (f32[2,128,512]{2,1,0:T(8,128)S(1)}, f32[2,128,512]{2,1,0:T(8,128)}, u32[]{:S(2)}) copy-start(f32[2,128,512]{2,1,0:T(8,128)} %density_ref.1) | copy-start | bytes 1572868
  4.3 72.2 %all-to-all-start = ((f32[32,8,8,512]{3,2,1,0:T(8,128)}), f32[32,8,8,512]{3,2,1,0:T(8,128)}, u32[]{:S(2)}, u32[]{:S(2)}) async-start(f32[32,8,8,512]{3,2,1,0:T(8,128)} %bitcast.20), calls=%async_computation | async-start | bytes 8388608 | tf_op jit(solution)/shard_map/all_to_all | solution.py:345
  15.3 5.8 %copy-start = (f32[7,2,128,512]{3,2,1,0:T(8,128)S(1)}, f32[7,2,128,512]{3,2,1,0:T(8,128)}, u32[]{:S(2)}) copy-start(f32[7,2,128,512]{3,2,1,0:T(8,128)} %carried_ref.1) | copy-start | bytes 11010052
  16.6 51.9 %collective-permute-start.1 = (f32[8,2,1,512]{3,2,1,0:T(1,128)S(1)}, f32[8,2,1,512]{3,2,1,0:T(1,128)S(1)}, u32[]{:S(2)}, u32[]{:S(2)}) collective-permute-start(f32[8,2,1,512]{3,2,1,0:T(1,128)S(1)} %get-tuple-element.28), channel_id=1, source_target_pairs={{32,0},{64,32},{96,64},{33,1},{65,33},{97,65},{34,2},{66,34},{98,6... | collective-permute-start | bytes 98312 | tf_op jit(solution)/shard_map/ppermute | solution.py:22
  18.0 11.8 %copy-start.3 = (s32[128]{0:T(128)S(1)}, s32[128]{0:T(128)}, u32[]{:S(2)}) copy-start(s32[128]{0:T(128)} %param.6) | copy-start | bytes 1540
  18.0 11.8 %copy-start.4 = (f32[128]{0:T(128)S(1)}, f32[128]{0:T(128)}, u32[]{:S(2)}) copy-start(f32[128]{0:T(128)} %param.7) | copy-start | bytes 1540
  18.0 50.4 %collective-permute-start = (f32[8,2,1,512]{3,2,1,0:T(1,128)S(1)}, f32[8,2,1,512]{3,2,1,0:T(1,128)S(1)}, u32[]{:S(2)}, u32[]{:S(2)}) collective-permute-start(f32[8,2,1,512]{3,2,1,0:T(1,128)S(1)} %get-tuple-element.29), channel_id=1, source_target_pairs={{0,32},{32,64},{64,96},{1,33},{33,65},{65,97},{2,34},{34,66},{66,9... | collective-permute-start | bytes 98312 | tf_op jit(solution)/shard_map/ppermute | solution.py:22
  21.8 34.7 %collective-permute-start.3 = (f32[8,2,128]{2,0,1:T(8,128)S(1)}, f32[8,2,128]{2,0,1:T(8,128)S(1)}, u32[]{:S(2)}, u32[]{:S(2)}) collective-permute-start(f32[8,2,128]{2,0,1:T(8,128)S(1)} %bitcast.25), channel_id=1, source_target_pairs={{0,31},{1,0},{2,1},{3,2},{4,3},{5,4},{6,5},{7,6},{8,7},{9,8},{10,9... | collective-permute-start | bytes 24584 | tf_op jit(solution)/shard_map/ppermute | solution.py:22
  29.7 38.6 %collective-permute-start.2 = (f32[8,2,128]{2,0,1:T(8,128)S(1)}, f32[8,2,128]{2,0,1:T(8,128)S(1)}, u32[]{:S(2)}, u32[]{:S(2)}) collective-permute-start(f32[8,2,128]{2,0,1:T(8,128)S(1)} %bitcast.24), channel_id=1, source_target_pairs={{0,1},{1,2},{2,3},{3,4},{4,5},{5,6},{6,7},{7,8},{8,9},{9,10},{10,1... | collective-permute-start | bytes 24584 | tf_op jit(solution)/shard_map/ppermute | solution.py:22
  82.7 65.3 %all-to-all-start.1 = ((f32[32,8,8,512]{3,2,1,0:T(8,128)}), f32[32,8,8,512]{3,2,1,0:T(8,128)}, u32[]{:S(2)}, u32[]{:S(2)}) async-start(f32[32,8,8,512]{3,2,1,0:T(8,128)} %shift_rows.1), calls=%async_computation.1 | async-start | bytes 8388608 | tf_op jit(solution)/shard_map/all_to_all | solution.py:367
  87.6 2.0 %copy-start.1 = (f32[7,2,128,512]{3,2,1,0:T(8,128)S(1)}, f32[7,2,128,512]{3,2,1,0:T(8,128)}, u32[]{:S(2)}) copy-start(f32[7,2,128,512]{3,2,1,0:T(8,128)} %carried_ref.1) | copy-start | bytes 11010052

commit v3 on v2

v3 whole, which is shorter than its diff:
```python
import functools

import jax
import jax.numpy as jnp
from jax import lax
from jax.experimental import pallas as pl
from jax.experimental.pallas import tpu as pltpu
from jax.sharding import PartitionSpec as P

FIELDS = 8
ROWS = 8
LANES = 128


def neighbours(value, axis, step, wrap):
    count = lax.axis_size(axis)
    pairs = [(i, i + step) for i in range(count)]
    if wrap:
        pairs = [(i, j % count) for i, j in pairs]
    else:
        pairs = [(i, j) for i, j in pairs if 0 <= j < count]
    return lax.ppermute(value, axis, pairs)


def in_hbm(value):
    return pltpu.with_memory_space_constraint(value, pltpu.HBM)


def pack_kernel(height, density_ref, carried_ref, o_ref, sems):
    copies = []
    for c in range(FIELDS):
        for z in range(height):
            source = density_ref.at[z] if c == 0 else carried_ref.at[c - 1, z]
            copies.append(pltpu.make_async_copy(source, o_ref.at[:, z, c], sems.at[c, z]))
    for copy in copies:
        copy.start()
    for copy in copies:
        copy.wait()


def pack(density, carried):
    height, rows, width = density.shape
    groups = rows // ROWS
    natural = (height, groups, ROWS, width)
    hbm = pl.BlockSpec(memory_space=pltpu.HBM)
    return pl.pallas_call(
        functools.partial(pack_kernel, height),
        out_shape=pltpu.VMEM((groups, height, FIELDS, ROWS, width), density.dtype),
        in_specs=[hbm, hbm],
        out_specs=pl.BlockSpec(memory_space=pltpu.VMEM),
        scratch_shapes=[pltpu.SemaphoreType.DMA((FIELDS, height))],
        cost_estimate=pl.CostEstimate(flops=0, bytes_accessed=64 * density.size, transcendentals=0),
        compiler_params=pltpu.CompilerParams(vmem_limit_bytes=8 * 2**20),
        name="pack",
    )(in_hbm(density.reshape(natural)), in_hbm(carried.reshape((FIELDS - 1,) + natural)))


def exchanged(registers, sub):
    values = list(registers)
    for k in (4, 2, 1):
        low = (sub & k) == 0
        result = list(values)
        for i in range(ROWS):
            if not i & k:
                a, b = values[i], values[i + k]
                result[i] = jnp.where(low, a, pltpu.roll(b, k, 0))
                result[i + k] = jnp.where(low, pltpu.roll(a, ROWS - k, 0), b)
        values = result
    return values


def shift_kernel(
    blocks, tiles, chunks, height, shift_ref, fraction_ref, x_ref, o_ref, cycles, placed, out_sems
):
    size = blocks // chunks
    total = blocks * tiles
    lane = lax.broadcasted_iota(jnp.int32, (FIELDS, LANES), 1)
    sub = lax.broadcasted_iota(jnp.int32, (FIELDS, LANES), 0)
    base = (lax.axis_index("phi") // height) * ROWS
    shifts = [shift_ref[base + row] for row in range(ROWS)]
    whole = [s // LANES for s in shifts]
    part = [s % LANES for s in shifts]
    fraction = [fraction_ref[base + row] for row in range(ROWS)]

    def lanes(t):
        return pl.ds(t * LANES, LANES)

    def collect(block, _):
        for t in range(tiles):
            by_row = exchanged([x_ref[block, c, :, lanes(t)] for c in range(FIELDS)], sub)
            for row in range(ROWS):
                cycles[row, block * tiles + t] = by_row[row]
        return 0

    lax.fori_loop(0, blocks, collect, 0, unroll=4)

    def turned(row, tile):
        return pltpu.roll(cycles[row, (tile - whole[row]) & (total - 1)], part[row], 1)

    def step(tile, row, carry):
        turned_before, moved_before = carry
        now = turned(row, tile)
        first = jnp.where(lane >= part[row], now, turned_before)
        rolled = pltpu.roll(first, 1, 1)
        second = jnp.where(lane >= 1, rolled, moved_before)
        value = (1.0 - fraction[row]) * first + fraction[row] * second
        return value, (now, rolled)

    def place(block, carries):
        carries = list(carries)
        for t in range(tiles):
            by_row = []
            for row in range(ROWS):
                value, carries[row] = step(block * tiles + t, row, carries[row])
                by_row.append(value)
            by_field = exchanged(by_row, sub)
            for c in range(FIELDS):
                placed[block, c, :, lanes(t)] = by_field[c]
        return tuple(carries)

    carries = []
    for row in range(ROWS):
        before = turned(row, -2)
        carries.append(step(-1, row, (before, before))[1])
    carries = tuple(carries)
    departures = []
    for i in range(chunks):
        piece = pl.ds(i * size, size)
        carries = lax.fori_loop(i * size, (i + 1) * size, place, carries, unroll=4)
        departures.append(pltpu.make_async_copy(placed.at[piece], o_ref.at[piece], out_sems.at[i]))
        departures[i].start()
    for copy in departures:
        copy.wait()


def shift_rows(received, shifts, fractions, height, chunks=8):
    blocks, _, _, width = received.shape
    tiles = width // LANES
    smem, hbm = pl.BlockSpec(memory_space=pltpu.SMEM), pl.BlockSpec(memory_space=pltpu.HBM)
    return pl.pallas_call(
        functools.partial(shift_kernel, blocks, tiles, chunks, height),
        out_shape=pltpu.HBM(received.shape, received.dtype),
        in_specs=[smem, smem, pl.BlockSpec(memory_space=pltpu.VMEM)],
        out_specs=hbm,
        scratch_shapes=[
            pltpu.VMEM((ROWS, blocks * tiles, FIELDS, LANES), jnp.float32),
            pltpu.VMEM(received.shape, jnp.float32),
            pltpu.SemaphoreType.DMA((chunks,)),
        ],
        cost_estimate=pl.CostEstimate(
            flops=8 * received.size, bytes_accessed=8 * received.size, transcendentals=0
        ),
        compiler_params=pltpu.CompilerParams(vmem_limit_bytes=20 * 2**20),
        name="shift_rows",
    )(shifts, fractions, pltpu.with_memory_space_constraint(received, pltpu.VMEM))


def edge_fluxes(height, inner, first_rows, last_rows, outer, left, first_cells, last_cells, right, rows_ref, cells_ref):
    def layer(ref, c):
        return ref[c * height : (c + 1) * height, :]

    def radial(ref):
        rho = layer(ref, 0)
        return layer(ref, 1) / jnp.where(rho == 0.0, 1.0, rho)

    for lower, upper, sign, start in ((inner, first_rows, 0.04, 0), (last_rows, outer, -0.04, FIELDS * height)):
        v_lower, v_upper = radial(lower), radial(upper)
        speed = face_speed(v_lower, v_upper)
        for c in range(FIELDS):
            flux = flux2(v_lower, v_upper, speed, layer(lower, c), layer(upper, c))
            rows_ref[start + c * height : start + (c + 1) * height, :] = sign * flux

    odd = lax.broadcasted_iota(jnp.int32, cells_ref.shape, 1) % 2 == 1

    def azimuthal(cells):
        v = [cells[:, 4 + z : 5 + z] / cells[:, z : z + 1] for z in range(2)]
        return jnp.where(odd, v[1], v[0])

    def flux(lower, upper):
        v_lower, v_upper = azimuthal(lower), azimuthal(upper)
        return 0.04 * flux2(v_lower, v_upper, face_speed(v_lower, v_upper), lower, upper)

    upper_faces = pltpu.roll(flux(last_cells[...], right[...]), FIELDS * height, 1)
    cells_ref[...] = flux(left[...], first_cells[...]) - upper_faces


def finish_kernel(
    groups,
    height,
    chunks,
    moved_ref,
    update_ref,
    *refs,
):
    row_refs, cell_refs = refs[:4], refs[4:8]
    density_ref, carried_ref, layer_rows, layer_cells, taken, change, edge_rows, edge_cells, new = refs[8:17]
    edge_sems, in_sems, out_sems = refs[17:]
    size = groups // chunks
    width = moved_ref.shape[-1]
    lane = lax.broadcasted_iota(jnp.int32, (ROWS, LANES), 1)
    edges = []
    for i in range(4):
        edges.append(pltpu.make_async_copy(row_refs[i], layer_rows.at[i], edge_sems.at[0, i]))
        edges.append(pltpu.make_async_copy(cell_refs[i], layer_cells.at[i], edge_sems.at[1, i]))
    for copy in edges:
        copy.start()
    arrivals, departures = [], []
    for i in range(chunks):
        piece = pl.ds(i * size, size)
        ends = ((moved_ref.at[piece], taken.at[piece]), (update_ref.at[:, :, piece], change.at[:, :, piece]))
        arrivals.append([pltpu.make_async_copy(*pair, in_sems.at[i, k]) for k, pair in enumerate(ends)])
        for copy in arrivals[i]:
            copy.start()
    for copy in edges:
        copy.wait()
    layers = [layer_rows.at[i] for i in range(4)] + [layer_cells.at[i] for i in range(4)]
    edge_fluxes(height, *layers, edge_rows, edge_cells)

    def subtract(g, _):
        cells = edge_cells[pl.ds(pl.multiple_of(g * ROWS, ROWS), ROWS), :]
        for z in range(height):
            for c in range(FIELDS):
                k = c * height + z
                for at in range(0, width, LANES):
                    value = taken[g, z, c, :, at : at + LANES] - change[c, z, g, :, at : at + LANES]
                    if at == 0:
                        value = value + jnp.where(lane == 0, cells[:, k : k + 1], 0.0)
                    if at == width - LANES:
                        m = FIELDS * height + k
                        value = value + jnp.where(lane == LANES - 1, cells[:, m : m + 1], 0.0)
                    new[c, z, g, :, at : at + LANES] = value
        return 0

    for i in range(chunks):
        piece = pl.ds(i * size, size)
        for copy in arrivals[i]:
            copy.wait()
        lax.fori_loop(i * size, (i + 1) * size, subtract, 0)
        for side, chunk, g, row in ((0, 0, 0, 0), (1, chunks - 1, groups - 1, ROWS - 1)):
            if i == chunk:
                for c in range(FIELDS):
                    for z in range(height):
                        k = (side * FIELDS + c) * height + z
                        here = (c, z, g, slice(row, row + 1), slice(None))
                        new[here] = new[here] + edge_rows[k : k + 1, :]
        ends = ((new.at[0, :, piece], density_ref.at[:, piece]), (new.at[1:, :, piece], carried_ref.at[:, :, piece]))
        for k, pair in enumerate(ends):
            departures.append(pltpu.make_async_copy(*pair, out_sems.at[i, k]))
            departures[-1].start()
    for copy in departures:
        copy.wait()


def finish(moved, update, row_layers, cell_layers, chunks=8):
    height, rows, width = update.shape[1:]
    groups = rows // ROWS
    hbm = pl.BlockSpec(memory_space=pltpu.HBM)
    natural = (height, groups, ROWS, width)
    layers = [in_hbm(layer) for layer in row_layers + cell_layers]
    return pl.pallas_call(
        functools.partial(finish_kernel, groups, height, chunks),
        out_shape=[
            jax.ShapeDtypeStruct(natural, jnp.float32),
            jax.ShapeDtypeStruct((FIELDS - 1,) + natural, jnp.float32),
        ],
        in_specs=[hbm] * 10,
        out_specs=[hbm, hbm],
        scratch_shapes=[
            pltpu.VMEM((4,) + row_layers[0].shape, jnp.float32),
            pltpu.VMEM((4,) + cell_layers[0].shape, jnp.float32),
            pltpu.VMEM((groups, height, FIELDS, ROWS, width), jnp.float32),
            pltpu.VMEM((FIELDS,) + natural, jnp.float32),
            pltpu.VMEM((2 * FIELDS * height, width), jnp.float32),
            pltpu.VMEM(cell_layers[0].shape, jnp.float32),
            pltpu.VMEM((FIELDS,) + natural, jnp.float32),
            pltpu.SemaphoreType.DMA((2, 4)),
            pltpu.SemaphoreType.DMA((chunks, 2)),
            pltpu.SemaphoreType.DMA((chunks, 2)),
        ],
        cost_estimate=pl.CostEstimate(flops=moved.size, bytes_accessed=12 * moved.size, transcendentals=0),
        compiler_params=pltpu.CompilerParams(vmem_limit_bytes=20 * 2**20),
        name="finish",
    )(in_hbm(moved.reshape(groups, height, FIELDS, ROWS, width)), in_hbm(update.reshape((FIELDS,) + natural)), *layers)


def flux2(v_left, v_right, speed, q_left, q_right):
    return v_left * q_left + v_right * q_right - speed * (q_right - q_left)


def face_speed(v_left, v_right):
    return jnp.maximum(jnp.abs(v_left), jnp.abs(v_right)) + 1.0


def update_kernel(groups, width, density_ref, carried_ref, o_ref, lower_ref):
    column = lax.broadcasted_iota(jnp.int32, (ROWS, width), 1)
    sub = lax.broadcasted_iota(jnp.int32, (ROWS, width), 0)
    lower_ref[...] = jnp.zeros_like(lower_ref)

    def field(c, z, rows):
        return density_ref[z, rows, :] if c == 0 else carried_ref[c - 1, z, rows, :]

    def body(g, _):
        rows = pl.ds(pl.multiple_of(g * ROWS, ROWS), ROWS)
        after = pl.ds(pl.multiple_of(jnp.minimum(g + 1, groups - 1) * ROWS, ROWS), ROWS)
        inside = jnp.where(g == groups - 1, ROWS - 1, ROWS)
        rho = [field(0, z, rows) for z in range(2)]
        v_height = [field(3, z, rows) / rho[z] for z in range(2)]
        speed_height = 2.0 * face_speed(v_height[0], v_height[1])
        for z in range(2):
            v_r = field(1, z, rows) / rho[z]
            v_a = field(2, z, rows) / rho[z]
            v_r_next = field(1, z, after) / field(0, z, after)
            v_r_up = pltpu.roll(jnp.where(sub == 0, v_r_next, v_r), ROWS - 1, 0)
            speed_r = face_speed(v_r, v_r_up)
            v_a_up = pltpu.roll(v_a, width - 1, 1)
            speed_a = face_speed(v_a, v_a_up)
            for c in range(FIELDS):
                q = field(c, z, rows)
                q_up = pltpu.roll(jnp.where(sub == 0, field(c, z, after), q), ROWS - 1, 0)
                upper = jnp.where(sub < inside, flux2(v_r, v_r_up, speed_r, q, q_up), 0.0)
                lower = pltpu.roll(jnp.where(sub == ROWS - 1, lower_ref[c, z], upper), 1, 0)
                lower_ref[c, z] = upper
                total = upper - lower
                q_up = pltpu.roll(q, width - 1, 1)
                upper = jnp.where(column < width - 1, flux2(v_a, v_a_up, speed_a, q, q_up), 0.0)
                total = total + (upper - pltpu.roll(upper, 1, 1))
                total = total + speed_height * (q - field(c, 1 - z, rows))
                o_ref[c, z, rows, :] = 0.04 * total
        return 0

    lax.fori_loop(0, groups, body, 0)


def update_of(density, carried):
    rows, width = density.shape[1:]
    size = FIELDS * density.size
    vmem = pl.BlockSpec(memory_space=pltpu.VMEM)
    return pl.pallas_call(
        functools.partial(update_kernel, rows // ROWS, width),
        out_shape=pltpu.HBM((FIELDS,) + density.shape, density.dtype),
        in_specs=[vmem] * 2,
        out_specs=vmem,
        scratch_shapes=[pltpu.VMEM((FIELDS, 2, ROWS, width), jnp.float32)],
        cost_estimate=pl.CostEstimate(flops=40 * size, bytes_accessed=8 * size, transcendentals=0),
        compiler_params=pltpu.CompilerParams(vmem_limit_bytes=24 * 2**20),
        name="flux_update",
    )(density, carried)


def border_kernel(groups, height, width, density_ref, carried_ref, first_rows, last_rows, first_cells, last_cells, rows, cells, sems):
    copies = []
    for side, g, at in ((0, 0, 0), (1, groups - 1, width - LANES)):
        for i, (source, fields) in enumerate(((density_ref, 0), (carried_ref, pl.ds(1, FIELDS - 1)))):
            lead = (slice(None),) * (1 + i)
            rest = (slice(None),) * 2
            copies.append(pltpu.make_async_copy(source.at[lead + (g,)], rows.at[side, fields], sems.at[side, i, 0]))
            copies.append(
                pltpu.make_async_copy(
                    source.at[lead + rest + (pl.ds(at, LANES),)], cells.at[side, fields], sems.at[side, i, 1]
                )
            )
    for copy in copies:
        copy.start()
    for copy in copies:
        copy.wait()
    lane = lax.broadcasted_iota(jnp.int32, (ROWS, LANES), 1)
    for side, out, row in ((0, first_rows, 0), (1, last_rows, ROWS - 1)):
        for k in range(FIELDS * height):
            out[k : k + 1, :] = rows[side, k // height, k % height, row : row + 1, :]

    def gather(g, _):
        here = pl.ds(pl.multiple_of(g * ROWS, ROWS), ROWS)
        for side, out, at in ((0, first_cells, 0), (1, last_cells, LANES - 1)):
            total = jnp.zeros((ROWS, LANES), jnp.float32)
            for k in range(FIELDS * height):
                value = pltpu.roll(cells[side, k // height, k % height, g], (k - at) % LANES, 1)
                total = jnp.where(lane == k, value, total)
            out[here, :] = total
        return 0

    lax.fori_loop(0, groups, gather, 0)


def borders_of(density, carried):
    height, rows, width = density.shape
    groups = rows // ROWS
    natural = (height, groups, ROWS, width)
    row_shape = pltpu.HBM((FIELDS * height, width), jnp.float32)
    cell_shape = pltpu.HBM((rows, LANES), jnp.float32)
    return pl.pallas_call(
        functools.partial(border_kernel, groups, height, width),
        out_shape=[row_shape, row_shape, cell_shape, cell_shape],
        in_specs=[pl.BlockSpec(memory_space=pltpu.HBM)] * 2,
        out_specs=[pl.BlockSpec(memory_space=pltpu.VMEM)] * 4,
        scratch_shapes=[
            pltpu.VMEM((2, FIELDS, height, ROWS, width), jnp.float32),
            pltpu.VMEM((2, FIELDS, height, groups, ROWS, LANES), jnp.float32),
            pltpu.SemaphoreType.DMA((2, 2, 2)),
        ],
        compiler_params=pltpu.CompilerParams(vmem_limit_bytes=8 * 2**20),
        name="borders",
    )(in_hbm(density.reshape(natural)), in_hbm(carried.reshape((FIELDS - 1,) + natural)))


def local(density, carried, cycle_shift, cycle_fraction):
    height, rows, width = density.shape
    devices = lax.axis_size("phi")
    packed = pack(density, carried)
    received = lax.all_to_all(
        packed.reshape(devices, FIELDS, ROWS, width), "phi", 0, 0, tiled=True
    )
    moved = shift_rows(received, cycle_shift, cycle_fraction, height)
    moved, density, carried = lax.optimization_barrier((moved, density, carried))
    moved = lax.all_to_all(moved, "phi", 0, 0, tiled=True)

    first_rows, last_rows, first_cells, last_cells = borders_of(density, carried)
    inner = neighbours(last_rows, "rad", 1, False)
    outer = neighbours(first_rows, "rad", -1, False)
    left = neighbours(last_cells, "phi", 1, True)
    right = neighbours(first_cells, "phi", -1, True)
    update = update_of(density, carried)
    density_next, carried_next = finish(
        moved,
        update,
        [inner, first_rows, last_rows, outer],
        [left, first_cells, last_cells, right],
    )
    return density_next.reshape(density.shape), carried_next.reshape(carried.shape)


def solution(mesh):
    placed = (P(None, "rad", "phi"), P(None, None, "rad", "phi"), P("rad"), P("rad"))
    return jax.shard_map(
        local,
        mesh=mesh,
        in_specs=placed,
        out_specs=(P(None, "rad", "phi"), P(None, None, "rad", "phi")),
        check_vma=False,
    )
```

time: 154 us -> 138 us (0.90)
  blocking collectives: 0 us -> 63.2 us
  waiting for transfers between devices: 89.7 us -> 32.4 us
  starting transfers between devices: 27.9 us -> 15.3 us
  Pallas kernels: 30.3 us -> 25.6 us
  local copies, waits for them, and re-layouts: 3.08 us -> 0.65 us
  other arithmetic: 1.64 us -> 0 us
    all_to_all x0 -> x1, blocking collectives: none -> 63.2 us  [local(): lax.all_to_all(packed.reshape(devices, FIELDS, ROWS, width), 'phi', 0, 0,...]
    all_to_all x1, waiting for transfers between devices: 43.4 us -> 0.01 us  [local(): moved = lax.all_to_all(moved, 'phi', 0, 0, tiled=True)]
    all_to_all x1 -> x0, starting transfers between devices: 11 us -> none  [local(): lax.all_to_all(packed.reshape(devices, FIELDS, ROWS, width), 'phi', 0, 0,...]
    all_to_all x1 -> x0, waiting for transfers between devices: 8.02 us -> none  [local(): lax.all_to_all(packed.reshape(devices, FIELDS, ROWS, width), 'phi', 0, 0,...]
    pallas_call x1, Pallas kernels: 15 us -> 7.21 us  [update_of(): pl.pallas_call(functools.partial(update_kernel, rows // ROWS, width), out...]
    ppermute x4, waiting for transfers between devices: 38.3 us -> 32.4 us  [neighbours(): return lax.ppermute(value, axis, pairs)]
    ppermute x4, starting transfers between devices: 12.1 us -> 10.4 us  [neighbours(): return lax.ppermute(value, axis, pairs)]
    pallas_call x2 -> x3, Pallas kernels: 9.89 us -> 11.4 us  [the longest x1 4.84 us: shift_rows(): pl.pallas_call(functools.partial(shift_kernel, blocks, tiles, chunks, hei...]
  transfers between devices with their start and end apart: 6 -> 5, of which waited for: 4 -> 1; matrix products, arithmetic and copies ran while one was open for 2% -> 0% of each run, Pallas kernels for 10% -> 8%
where the time goes in v3:
time: 138 us
  blocking collectives  63.2 us (46%)
  waiting for transfers between devices  32.4 us (23%)
  Pallas kernels  25.6 us (19%)
  starting transfers between devices  15.3 us (11%)
    all_to_all x1, blocking collectives, local(): lax.all_to_all(packed.reshape(devices, FIELDS, ROWS, width), 'phi', 0, 0,...  63.2 us
    ppermute x4, waiting for transfers between devices, neighbours(): return lax.ppermute(value, axis, pairs)  32.4 us
    ppermute x4, starting transfers between devices, neighbours(): return lax.ppermute(value, axis, pairs)  10.4 us
    pallas_call x1, Pallas kernels, update_of(): pl.pallas_call(functools.partial(update_kernel, rows // ROWS, width), out...  7.21 us
    pallas_call x1, Pallas kernels, finish(): pl.pallas_call(functools.partial(finish_kernel, groups, height, chunks),...  6.93 us
    all_to_all x1, starting transfers between devices, local(): moved = lax.all_to_all(moved, 'phi', 0, 0, tiled=True)  4.88 us
    pallas_call x1, Pallas kernels, shift_rows(): pl.pallas_call(functools.partial(shift_kernel, blocks, tiles, chunks, hei...  4.84 us
    pallas_call x1, Pallas kernels, borders_of(): pl.pallas_call(functools.partial(border_kernel, groups, height, width), o...  4.3 us
  transfers between devices with their start and end apart: 5, of which 1 were waited for; matrix products, arithmetic and copies ran while one was open for 0% of the time, Pallas kernels for 8%

profile of v3, /device:TPU:0, one launch (start us, length us, event | category | flops | bytes accessed | tf_op | source)
XLA Modules:
  0.0 137.8 jit_solution(3281354559775424576)
XLA Ops:
  0.6 2.3 %pack.1 = f32[16,2,8,8,512]{4,3,2,1,0:T(8,128)S(1)} custom-call(f32[2,16,8,512]{3,2,1,0:T(8,128)} %bitcast.12, f32[7,2,16,8,512]{4,3,2,1,0:T(8,128)} %bitcast.9), custom_call_target="tpu_custom_call" | custom-call | bytes 8388608 | tf_op jit(solution)/shard_map/pack/pallas_call | solution.py:46
  2.9 0.0 copy-start.2
  2.9 0.0 copy-start.3
  2.9 63.2 %all_to_all.10.x_ref = f32[32,8,8,512]{3,2,1,0:T(8,128)S(1)} all-to-all(f32[32,8,8,512]{3,2,1,0:T(8,128)S(1)} %bitcast.11), channel_id=1, replica_groups=mesh['rad'=4,'phi'=32] {'phi'}, dimensions={0} | all-to-all | bytes 8388608 | tf_op jit(solution)/shard_map/all_to_all | solution.py:409
  66.2 0.0 copy-done.2
  66.2 0.0 copy-done.3
  66.2 4.8 %shift_rows.1 = f32[32,8,8,512]{3,2,1,0:T(8,128)} custom-call(s32[128]{0:T(128)S(1)} %copy-done.2, f32[128]{0:T(128)S(1)} %copy-done.3, f32[32,8,8,512]{3,2,1,0:T(8,128)S(1)} %all_to_all.10.x_ref), custom_call_target="tpu_custom_call" | custom-call | flops 8388608 | bytes 8388608 | tf_op jit(solution)/shard_map/shift_rows/pallas_call | solution.py:140
  71.0 4.9 %all-to-all-start.1 = ((f32[32,8,8,512]{3,2,1,0:T(8,128)}), f32[32,8,8,512]{3,2,1,0:T(8,128)}, u32[]{:S(2)}, u32[]{:S(2)}) async-start(f32[32,8,8,512]{3,2,1,0:T(8,128)} %shift_rows.1), calls=%async_computation.1 | async-start | bytes 8388608 | tf_op jit(solution)/shard_map/all_to_all | solution.py:414
  75.9 0.0 copy-start
  75.9 0.0 copy-start.1
  75.9 4.3 %borders.1 = (f32[16,512]{1,0:T(8,128)}, f32[16,512]{1,0:T(8,128)}, f32[128,128]{1,0:T(8,128)}, f32[128,128]{1,0:T(8,128)}) custom-call(f32[2,16,8,512]{3,2,1,0:T(8,128)} %bitcast.13, f32[7,2,16,8,512]{4,3,2,1,0:T(8,128)} %bitcast.10), custom_call_target="tpu_custom_call" | custom-call | tf_op jit(solution)/shard_map/borders/pallas_call | solution.py:390
  80.2 3.2 %collective-permute-start.2 = (f32[128,128]{1,0:T(8,128)}, f32[128,128]{1,0:T(8,128)S(1)}, u32[]{:S(2)}, u32[]{:S(2)}) collective-permute-start(f32[128,128]{1,0:T(8,128)} %get-tuple-element.16.refs_6_), channel_id=1, source_target_pairs={{0,1},{1,2},{2,3},{3,4},{4,5},{5,6},{6,7},{7,8},{8,9},{9,10},{10,1... | collective-permute-start | bytes 196616 | tf_op jit(solution)/shard_map/ppermute | solution.py:22
  83.4 4.6 %collective-permute-start.3 = (f32[128,128]{1,0:T(8,128)}, f32[128,128]{1,0:T(8,128)S(1)}, u32[]{:S(2)}, u32[]{:S(2)}) collective-permute-start(f32[128,128]{1,0:T(8,128)} %get-tuple-element.17.refs_5_), channel_id=1, source_target_pairs={{0,31},{1,0},{2,1},{3,2},{4,3},{5,4},{6,5},{7,6},{8,7},{9,8},{10,9... | collective-permute-start | bytes 196616 | tf_op jit(solution)/shard_map/ppermute | solution.py:22
  88.0 1.3 collective-permute-start
  89.3 1.3 collective-permute-start.1
  90.6 0.0 copy-done
  90.6 0.0 copy-done.1
  90.7 7.2 %flux_update.1 = f32[8,2,128,512]{3,2,1,0:T(8,128)} custom-call(f32[2,128,512]{2,1,0:T(8,128)S(1)} %copy-done.1, f32[7,2,128,512]{3,2,1,0:T(8,128)S(1)} %copy-done), custom_call_target="tpu_custom_call" | custom-call | flops 41943040 | bytes 8388608 | tf_op jit(solution)/shard_map/flux_update/pallas_call | solution.py:338
  97.9 0.0 collective-permute-done.refs_0_
  97.9 0.0 copy-start.6
  97.9 0.0 collective-permute-done.1.refs_3_
  97.9 0.0 copy-start.7
  97.9 32.4 %collective-permute-done.2.refs_4_ = f32[128,128]{1,0:T(8,128)S(1)} collective-permute-done((f32[128,128]{1,0:T(8,128)}, f32[128,128]{1,0:T(8,128)S(1)}, u32[]{:S(2)}, u32[]{:S(2)}) %collective-permute-start.2) | collective-permute-done | bytes 65568 | tf_op jit(solution)/shard_map/ppermute | solution.py:22
  130.3 0.0 copy-start.4
  130.3 0.0 collective-permute-done.3.refs_7_
  130.3 0.0 copy-start.5
  130.3 0.0 all-to-all-done.1
  130.3 0.0 copy-done.6
  130.3 0.0 copy-done.7
  130.3 0.6 copy-done.4
  130.9 0.0 copy-done.5
  130.9 6.9 %finish.1 = (f32[2,16,8,512]{3,2,1,0:T(8,128)}, f32[7,2,16,8,512]{4,3,2,1,0:T(8,128)}) custom-call(f32[16,2,8,8,512]{4,3,2,1,0:T(8,128)} %bitcast.3.moved_ref, f32[8,2,16,8,512]{4,3,2,1,0:T(8,128)} %bitcast.14, f32[16,512]{1,0:T(8,128)} %copy-done.6, f32[16,512]{1,0:T(8,128)} %get-tuple-element.15.refs_1_, f32[16,512]{1,0:T(8,128)} %get-tuple-element.14.refs_2_, ...), custom_call_target="tpu_custom_call" | custom-call | flops 1048576 | bytes 12582912 | tf_op jit(solution)/shard_map/finish/pallas_call | solution.py:260
Async XLA Ops:
  2.9 63.2 %copy-start.2 = (s32[128]{0:T(128)S(1)}, s32[128]{0:T(128)}, u32[]{:S(2)}) copy-start(s32[128]{0:T(128)} %shift_ref.1) | copy-start | bytes 1540
  2.9 63.2 %copy-start.3 = (f32[128]{0:T(128)S(1)}, f32[128]{0:T(128)}, u32[]{:S(2)}) copy-start(f32[128]{0:T(128)} %fraction_ref.1) | copy-start | bytes 1540
  71.0 59.3 %all-to-all-start.1 = ((f32[32,8,8,512]{3,2,1,0:T(8,128)}), f32[32,8,8,512]{3,2,1,0:T(8,128)}, u32[]{:S(2)}, u32[]{:S(2)}) async-start(f32[32,8,8,512]{3,2,1,0:T(8,128)} %shift_rows.1), calls=%async_computation.1 | async-start | bytes 8388608 | tf_op jit(solution)/shard_map/all_to_all | solution.py:414
  75.9 14.7 %copy-start = (f32[7,2,128,512]{3,2,1,0:T(8,128)S(1)}, f32[7,2,128,512]{3,2,1,0:T(8,128)}, u32[]{:S(2)}) copy-start(f32[7,2,128,512]{3,2,1,0:T(8,128)} %carried_ref) | copy-start | bytes 11010052
  75.9 14.7 %copy-start.1 = (f32[2,128,512]{2,1,0:T(8,128)S(1)}, f32[2,128,512]{2,1,0:T(8,128)}, u32[]{:S(2)}) copy-start(f32[2,128,512]{2,1,0:T(8,128)} %density_ref) | copy-start | bytes 1572868
  80.2 50.0 %collective-permute-start.2 = (f32[128,128]{1,0:T(8,128)}, f32[128,128]{1,0:T(8,128)S(1)}, u32[]{:S(2)}, u32[]{:S(2)}) collective-permute-start(f32[128,128]{1,0:T(8,128)} %get-tuple-element.16.refs_6_), channel_id=1, source_target_pairs={{0,1},{1,2},{2,3},{3,4},{4,5},{5,6},{6,7},{7,8},{8,9},{9,10},{10,1... | collective-permute-start | bytes 196616 | tf_op jit(solution)/shard_map/ppermute | solution.py:22
  83.4 46.9 %collective-permute-start.3 = (f32[128,128]{1,0:T(8,128)}, f32[128,128]{1,0:T(8,128)S(1)}, u32[]{:S(2)}, u32[]{:S(2)}) collective-permute-start(f32[128,128]{1,0:T(8,128)} %get-tuple-element.17.refs_5_), channel_id=1, source_target_pairs={{0,31},{1,0},{2,1},{3,2},{4,3},{5,4},{6,5},{7,6},{8,7},{9,8},{10,9... | collective-permute-start | bytes 196616 | tf_op jit(solution)/shard_map/ppermute | solution.py:22
  88.0 9.8 %collective-permute-start = (f32[16,512]{1,0:T(8,128)}, f32[16,512]{1,0:T(8,128)S(1)}, u32[]{:S(2)}, u32[]{:S(2)}) collective-permute-start(f32[16,512]{1,0:T(8,128)} %get-tuple-element.14.refs_2_), channel_id=1, source_target_pairs={{0,32},{32,64},{64,96},{1,33},{33,65},{65,97},{2,34},{34,66},{66,9... | collective-permute-start | bytes 98312 | tf_op jit(solution)/shard_map/ppermute | solution.py:22
  89.3 8.5 %collective-permute-start.1 = (f32[16,512]{1,0:T(8,128)}, f32[16,512]{1,0:T(8,128)S(1)}, u32[]{:S(2)}, u32[]{:S(2)}) collective-permute-start(f32[16,512]{1,0:T(8,128)} %get-tuple-element.15.refs_1_), channel_id=1, source_target_pairs={{32,0},{64,32},{96,64},{33,1},{65,33},{97,65},{34,2},{66,34},{98,6... | collective-permute-start | bytes 98312 | tf_op jit(solution)/shard_map/ppermute | solution.py:22
  97.9 32.4 %copy-start.6 = (f32[16,512]{1,0:T(8,128)}, f32[16,512]{1,0:T(8,128)S(1)}, u32[]{:S(2)}) copy-start(f32[16,512]{1,0:T(8,128)S(1)} %collective-permute-done.refs_0_) | copy-start | bytes 98308
  97.9 32.4 %copy-start.7 = (f32[16,512]{1,0:T(8,128)}, f32[16,512]{1,0:T(8,128)S(1)}, u32[]{:S(2)}) copy-start(f32[16,512]{1,0:T(8,128)S(1)} %collective-permute-done.1.refs_3_) | copy-start | bytes 98308
  130.3 0.6 copy-start.4
  130.3 0.6 copy-start.5

commit v4 on v3

--- a/solution.py
+++ b/solution.py
@@ -24,35 +24,6 @@
 
 def in_hbm(value):
     return pltpu.with_memory_space_constraint(value, pltpu.HBM)
-
-
-def pack_kernel(height, density_ref, carried_ref, o_ref, sems):
-    copies = []
-    for c in range(FIELDS):
-        for z in range(height):
-            source = density_ref.at[z] if c == 0 else carried_ref.at[c - 1, z]
-            copies.append(pltpu.make_async_copy(source, o_ref.at[:, z, c], sems.at[c, z]))
-    for copy in copies:
-        copy.start()
-    for copy in copies:
-        copy.wait()
-
-
-def pack(density, carried):
-    height, rows, width = density.shape
-    groups = rows // ROWS
-    natural = (height, groups, ROWS, width)
-    hbm = pl.BlockSpec(memory_space=pltpu.HBM)
-    return pl.pallas_call(
-        functools.partial(pack_kernel, height),
-        out_shape=pltpu.VMEM((groups, height, FIELDS, ROWS, width), density.dtype),
-        in_specs=[hbm, hbm],
-        out_specs=pl.BlockSpec(memory_space=pltpu.VMEM),
-        scratch_shapes=[pltpu.SemaphoreType.DMA((FIELDS, height))],
-        cost_estimate=pl.CostEstimate(flops=0, bytes_accessed=64 * density.size, transcendentals=0),
-        compiler_params=pltpu.CompilerParams(vmem_limit_bytes=8 * 2**20),
-        name="pack",
-    )(in_hbm(density.reshape(natural)), in_hbm(carried.reshape((FIELDS - 1,) + natural)))
 
 
 def exchanged(registers, sub):
@@ -69,33 +40,63 @@
     return values
 
 
-def shift_kernel(
-    blocks, tiles, chunks, height, shift_ref, fraction_ref, x_ref, o_ref, cycles, placed, out_sems
-):
+def pack_kernel(groups, height, chunks, density_ref, carried_ref, o_ref, taken, sems):
+    size = groups // chunks
+    width = taken.shape[-1]
+    sub = lax.broadcasted_iota(jnp.int32, (ROWS, LANES), 0)
+    arrivals = []
+    for i in range(chunks):
+        piece = pl.ds(i * size, size)
+        ends = ((density_ref.at[:, piece], taken.at[0, :, piece]), (carried_ref.at[:, :, piece], taken.at[1:, :, piece]))
+        arrivals.append([pltpu.make_async_copy(*pair, sems.at[i, k]) for k, pair in enumerate(ends)])
+        for copy in arrivals[i]:
+            copy.start()
+
+    def reorder(g, _):
+        for z in range(height):
+            for t in range(width // LANES):
+                by_row = exchanged([taken[c, z, g, :, t * LANES : (t + 1) * LANES] for c in range(FIELDS)], sub)
+                for row in range(ROWS):
+                    o_ref[g * height + z, row, t] = by_row[row]
+        return 0
+
+    for i in range(chunks):
+        for copy in arrivals[i]:
+            copy.wait()
+        lax.fori_loop(i * size, (i + 1) * size, reorder, 0, unroll=2)
+
+
+def pack(density, carried, chunks=4):
+    height, rows, width = density.shape
+    groups = rows // ROWS
+    natural = (height, groups, ROWS, width)
+    hbm = pl.BlockSpec(memory_space=pltpu.HBM)
+    return pl.pallas_call(
+        functools.partial(pack_kernel, groups, height, chunks),
+        out_shape=pltpu.VMEM((groups * height, ROWS, width // LANES, FIELDS, LANES), density.dtype),
+        in_specs=[hbm, hbm],
+        out_specs=pl.BlockSpec(memory_space=pltpu.VMEM),
+        scratch_shapes=[pltpu.VMEM((FIELDS,) + natural, jnp.float32), pltpu.SemaphoreType.DMA((chunks, 2))],
+        cost_estimate=pl.CostEstimate(flops=0, bytes_accessed=64 * density.size, transcendentals=0),
+        compiler_params=pltpu.CompilerParams(vmem_limit_bytes=12 * 2**20),
+        name="pack",
+    )(in_hbm(density.reshape(natural)), in_hbm(carried.reshape((FIELDS - 1,) + natural)))
+
+
+def shift_kernel(blocks, tiles, chunks, height, shift_ref, fraction_ref, x_ref, o_ref, placed, out_sems):
     size = blocks // chunks
+    tile_bits, skip = tiles.bit_length() - 1, (ROWS - 1) * tiles
     total = blocks * tiles
     lane = lax.broadcasted_iota(jnp.int32, (FIELDS, LANES), 1)
-    sub = lax.broadcasted_iota(jnp.int32, (FIELDS, LANES), 0)
     base = (lax.axis_index("phi") // height) * ROWS
     shifts = [shift_ref[base + row] for row in range(ROWS)]
     whole = [s // LANES for s in shifts]
     part = [s % LANES for s in shifts]
     fraction = [fraction_ref[base + row] for row in range(ROWS)]
 
-    def lanes(t):
-        return pl.ds(t * LANES, LANES)
-
-    def collect(block, _):
-        for t in range(tiles):
-            by_row = exchanged([x_ref[block, c, :, lanes(t)] for c in range(FIELDS)], sub)
-            for row in range(ROWS):
-                cycles[row, block * tiles + t] = by_row[row]
-        return 0
-
-    lax.fori_loop(0, blocks, collect, 0, unroll=4)
-
     def turned(row, tile):
-        return pltpu.roll(cycles[row, (tile - whole[row]) & (total - 1)], part[row], 1)
+        source = (tile - whole[row]) & (total - 1)
+        return pltpu.roll(x_ref[source + (source >> tile_bits) * skip + row * tiles], part[row], 1)
 
     def step(tile, row, carry):
         turned_before, moved_before = carry
@@ -109,13 +110,8 @@
     def place(block, carries):
         carries = list(carries)
         for t in range(tiles):
-            by_row = []
             for row in range(ROWS):
-                value, carries[row] = step(block * tiles + t, row, carries[row])
-                by_row.append(value)
-            by_field = exchanged(by_row, sub)
-            for c in range(FIELDS):
-                placed[block, c, :, lanes(t)] = by_field[c]
+                placed[block, row, t], carries[row] = step(block * tiles + t, row, carries[row])
         return tuple(carries)
 
     carries = []
@@ -134,25 +130,20 @@
 
 
 def shift_rows(received, shifts, fractions, height, chunks=8):
-    blocks, _, _, width = received.shape
-    tiles = width // LANES
+    blocks, _, tiles, _, _ = received.shape
     smem, hbm = pl.BlockSpec(memory_space=pltpu.SMEM), pl.BlockSpec(memory_space=pltpu.HBM)
     return pl.pallas_call(
         functools.partial(shift_kernel, blocks, tiles, chunks, height),
         out_shape=pltpu.HBM(received.shape, received.dtype),
         in_specs=[smem, smem, pl.BlockSpec(memory_space=pltpu.VMEM)],
         out_specs=hbm,
-        scratch_shapes=[
-            pltpu.VMEM((ROWS, blocks * tiles, FIELDS, LANES), jnp.float32),
-            pltpu.VMEM(received.shape, jnp.float32),
-            pltpu.SemaphoreType.DMA((chunks,)),
-        ],
+        scratch_shapes=[pltpu.VMEM(received.shape, jnp.float32), pltpu.SemaphoreType.DMA((chunks,))],
         cost_estimate=pl.CostEstimate(
             flops=8 * received.size, bytes_accessed=8 * received.size, transcendentals=0
         ),
         compiler_params=pltpu.CompilerParams(vmem_limit_bytes=20 * 2**20),
         name="shift_rows",
-    )(shifts, fractions, pltpu.with_memory_space_constraint(received, pltpu.VMEM))
+    )(shifts, fractions, pltpu.with_memory_space_constraint(received.reshape(-1, FIELDS, LANES), pltpu.VMEM))
 
 
 def edge_fluxes(height, inner, first_rows, last_rows, outer, left, first_cells, last_cells, right, rows_ref, cells_ref):
@@ -196,8 +187,9 @@
     density_ref, carried_ref, layer_rows, layer_cells, taken, change, edge_rows, edge_cells, new = refs[8:17]
     edge_sems, in_sems, out_sems = refs[17:]
     size = groups // chunks
-    width = moved_ref.shape[-1]
+    width = change.shape[-1]
     lane = lax.broadcasted_iota(jnp.int32, (ROWS, LANES), 1)
+    sub = lax.broadcasted_iota(jnp.int32, (ROWS, LANES), 0)
     edges = []
     for i in range(4):
         edges.append(pltpu.make_async_copy(row_refs[i], layer_rows.at[i], edge_sems.at[0, i]))
@@ -219,10 +211,12 @@
     def subtract(g, _):
         cells = edge_cells[pl.ds(pl.multiple_of(g * ROWS, ROWS), ROWS), :]
         for z in range(height):
-            for c in range(FIELDS):
-                k = c * height + z
-                for at in range(0, width, LANES):
-                    value = taken[g, z, c, :, at : at + LANES] - change[c, z, g, :, at : at + LANES]
+            for t in range(width // LANES):
+                at = t * LANES
+                by_field = exchanged([taken[g, z, row, t] for row in range(ROWS)], sub)
+                for c in range(FIELDS):
+                    k = c * height + z
+                    value = by_field[c] - change[c, z, g, :, at : at + LANES]
                     if at == 0:
                         value = value + jnp.where(lane == 0, cells[:, k : k + 1], 0.0)
                     if at == width - LANES:
@@ -235,7 +229,7 @@
         piece = pl.ds(i * size, size)
         for copy in arrivals[i]:
             copy.wait()
-        lax.fori_loop(i * size, (i + 1) * size, subtract, 0)
+        lax.fori_loop(i * size, (i + 1) * size, subtract, 0, unroll=4)
         for side, chunk, g, row in ((0, 0, 0, 0), (1, chunks - 1, groups - 1, ROWS - 1)):
             if i == chunk:
                 for c in range(FIELDS):
@@ -251,7 +245,7 @@
         copy.wait()
 
 
-def finish(moved, update, row_layers, cell_layers, chunks=8):
+def finish(moved, update, row_layers, cell_layers, chunks=4):
     height, rows, width = update.shape[1:]
     groups = rows // ROWS
     hbm = pl.BlockSpec(memory_space=pltpu.HBM)
@@ -268,7 +262,7 @@
         scratch_shapes=[
             pltpu.VMEM((4,) + row_layers[0].shape, jnp.float32),
             pltpu.VMEM((4,) + cell_layers[0].shape, jnp.float32),
-            pltpu.VMEM((groups, height, FIELDS, ROWS, width), jnp.float32),
+            pltpu.VMEM((groups, height) + moved.shape[1:], jnp.float32),
             pltpu.VMEM((FIELDS,) + natural, jnp.float32),
             pltpu.VMEM((2 * FIELDS * height, width), jnp.float32),
             pltpu.VMEM(cell_layers[0].shape, jnp.float32),
@@ -280,7 +274,7 @@
         cost_estimate=pl.CostEstimate(flops=moved.size, bytes_accessed=12 * moved.size, transcendentals=0),
         compiler_params=pltpu.CompilerParams(vmem_limit_bytes=20 * 2**20),
         name="finish",
-    )(in_hbm(moved.reshape(groups, height, FIELDS, ROWS, width)), in_hbm(update.reshape((FIELDS,) + natural)), *layers)
+    )(in_hbm(moved.reshape((groups, height) + moved.shape[1:])), in_hbm(update.reshape((FIELDS,) + natural)), *layers)
 
 
 def flux2(v_left, v_right, speed, q_left, q_right):
@@ -403,12 +397,8 @@
 
 
 def local(density, carried, cycle_shift, cycle_fraction):
-    height, rows, width = density.shape
-    devices = lax.axis_size("phi")
-    packed = pack(density, carried)
-    received = lax.all_to_all(
-        packed.reshape(devices, FIELDS, ROWS, width), "phi", 0, 0, tiled=True
-    )
+    height = density.shape[0]
+    received = lax.all_to_all(pack(density, carried), "phi", 0, 0, tiled=True)
     moved = shift_rows(received, cycle_shift, cycle_fraction, height)
     moved, density, carried = lax.optimization_barrier((moved, density, carried))
     moved = lax.all_to_all(moved, "phi", 0, 0, tiled=True)

time: 138 us -> 137 us (level)
  Pallas kernels: 25.6 us -> 24.2 us
where the time goes in v4:
time: 137 us; the launch traced here: 136 us
  blocking collectives  63.2 us (46%)
  waiting for transfers between devices  32.3 us (24%)
  Pallas kernels  24.2 us (18%)
  starting transfers between devices  15.3 us (11%)
    all_to_all x1, blocking collectives, local(): received = lax.all_to_all(pack(density, carried), 'phi', 0, 0, tiled=True)  63.2 us
    ppermute x4, waiting for transfers between devices, neighbours(): return lax.ppermute(value, axis, pairs)  32.3 us
    ppermute x4, starting transfers between devices, neighbours(): return lax.ppermute(value, axis, pairs)  10.4 us
    pallas_call x1, Pallas kernels, update_of(): pl.pallas_call(functools.partial(update_kernel, rows // ROWS, width), out...  7.21 us
    pallas_call x1, Pallas kernels, finish(): pl.pallas_call(functools.partial(finish_kernel, groups, height, chunks),...  6.22 us
    all_to_all x1, starting transfers between devices, local(): moved = lax.all_to_all(moved, 'phi', 0, 0, tiled=True)  4.88 us
    pallas_call x1, Pallas kernels, borders_of(): pl.pallas_call(functools.partial(border_kernel, groups, height, width), o...  4.3 us
    pallas_call x1, Pallas kernels, shift_rows(): pl.pallas_call(functools.partial(shift_kernel, blocks, tiles, chunks, hei...  4.02 us
  transfers between devices with their start and end apart: 5, of which 1 were waited for; matrix products, arithmetic and copies ran while one was open for 0% of the time, Pallas kernels for 8%

profile of v4, /device:TPU:0, one launch (start us, length us, event | category | flops | bytes accessed | tf_op | source)
XLA Modules:
  0.0 136.4 jit_solution(11758383089526785048)
XLA Ops:
  0.6 2.5 %pack.1 = f32[32,8,4,8,128]{4,3,2,1,0:T(8,128)S(1)} custom-call(f32[2,16,8,512]{3,2,1,0:T(8,128)} %bitcast.12, f32[7,2,16,8,512]{4,3,2,1,0:T(8,128)} %bitcast.9), custom_call_target="tpu_custom_call" | custom-call | bytes 8388608 | tf_op jit(solution)/shard_map/pack/pallas_call | solution.py:74
  3.1 0.0 copy-start.2
  3.1 0.0 copy-start.3
  3.1 63.2 %all_to_all.10 = f32[32,8,4,8,128]{4,3,2,1,0:T(8,128)S(1)} all-to-all(f32[32,8,4,8,128]{4,3,2,1,0:T(8,128)S(1)} %pack.1), channel_id=1, replica_groups=mesh['rad'=4,'phi'=32] {'phi'}, dimensions={0} | all-to-all | bytes 8388608 | tf_op jit(solution)/shard_map/all_to_all | solution.py:401
  66.4 0.0 copy-done.2
  66.4 0.0 copy-done.3
  66.4 4.0 %shift_rows.1 = f32[32,8,4,8,128]{4,3,2,1,0:T(8,128)} custom-call(s32[128]{0:T(128)S(1)} %copy-done.2, f32[128]{0:T(128)S(1)} %copy-done.3, f32[1024,8,128]{2,1,0:T(8,128)S(1)} %bitcast.11), custom_call_target="tpu_custom_call" | custom-call | flops 8388608 | bytes 8388608 | tf_op jit(solution)/shard_map/shift_rows/pallas_call | solution.py:135
  70.4 4.9 %all-to-all-start.1 = ((f32[32,8,4,8,128]{4,3,2,1,0:T(8,128)}), f32[32,8,4,8,128]{4,3,2,1,0:T(8,128)}, u32[]{:S(2)}, u32[]{:S(2)}) async-start(f32[32,8,4,8,128]{4,3,2,1,0:T(8,128)} %shift_rows.1), calls=%async_computation.1 | async-start | bytes 8388608 | tf_op jit(solution)/shard_map/all_to_all | solution.py:404
  75.3 0.0 copy-start
  75.3 0.0 copy-start.1
  75.3 4.3 %borders.1 = (f32[16,512]{1,0:T(8,128)}, f32[16,512]{1,0:T(8,128)}, f32[128,128]{1,0:T(8,128)}, f32[128,128]{1,0:T(8,128)}) custom-call(f32[2,16,8,512]{3,2,1,0:T(8,128)} %bitcast.13, f32[7,2,16,8,512]{4,3,2,1,0:T(8,128)} %bitcast.10), custom_call_target="tpu_custom_call" | custom-call | tf_op jit(solution)/shard_map/borders/pallas_call | solution.py:384
  79.6 3.2 %collective-permute-start.2 = (f32[128,128]{1,0:T(8,128)}, f32[128,128]{1,0:T(8,128)S(1)}, u32[]{:S(2)}, u32[]{:S(2)}) collective-permute-start(f32[128,128]{1,0:T(8,128)} %get-tuple-element.16.refs_6_), channel_id=1, source_target_pairs={{0,1},{1,2},{2,3},{3,4},{4,5},{5,6},{6,7},{7,8},{8,9},{9,10},{10,1... | collective-permute-start | bytes 196616 | tf_op jit(solution)/shard_map/ppermute | solution.py:22
  82.8 4.6 %collective-permute-start.3 = (f32[128,128]{1,0:T(8,128)}, f32[128,128]{1,0:T(8,128)S(1)}, u32[]{:S(2)}, u32[]{:S(2)}) collective-permute-start(f32[128,128]{1,0:T(8,128)} %get-tuple-element.17.refs_5_), channel_id=1, source_target_pairs={{0,31},{1,0},{2,1},{3,2},{4,3},{5,4},{6,5},{7,6},{8,7},{9,8},{10,9... | collective-permute-start | bytes 196616 | tf_op jit(solution)/shard_map/ppermute | solution.py:22
  87.4 1.3 collective-permute-start
  88.7 1.3 collective-permute-start.1
  90.0 0.0 copy-done
  90.0 0.0 copy-done.1
  90.0 7.2 %flux_update.1 = f32[8,2,128,512]{3,2,1,0:T(8,128)} custom-call(f32[2,128,512]{2,1,0:T(8,128)S(1)} %copy-done.1, f32[7,2,128,512]{3,2,1,0:T(8,128)S(1)} %copy-done), custom_call_target="tpu_custom_call" | custom-call | flops 41943040 | bytes 8388608 | tf_op jit(solution)/shard_map/flux_update/pallas_call | solution.py:332
  97.3 0.0 collective-permute-done.refs_0_
  97.3 0.0 copy-start.6
  97.3 0.0 collective-permute-done.1.refs_3_
  97.3 0.0 copy-start.7
  97.3 32.3 %collective-permute-done.2.refs_4_ = f32[128,128]{1,0:T(8,128)S(1)} collective-permute-done((f32[128,128]{1,0:T(8,128)}, f32[128,128]{1,0:T(8,128)S(1)}, u32[]{:S(2)}, u32[]{:S(2)}) %collective-permute-start.2) | collective-permute-done | bytes 65568 | tf_op jit(solution)/shard_map/ppermute | solution.py:22
  129.6 0.0 copy-start.4
  129.6 0.0 collective-permute-done.3.refs_7_
  129.6 0.0 copy-start.5
  129.6 0.0 all-to-all-done.1
  129.6 0.0 copy-done.6
  129.6 0.0 copy-done.7
  129.6 0.6 copy-done.4
  130.2 0.0 copy-done.5
  130.2 6.2 %finish.1 = (f32[2,16,8,512]{3,2,1,0:T(8,128)}, f32[7,2,16,8,512]{4,3,2,1,0:T(8,128)}) custom-call(f32[16,2,8,4,8,128]{5,4,3,2,1,0:T(8,128)} %bitcast.3.moved_ref, f32[8,2,16,8,512]{4,3,2,1,0:T(8,128)} %bitcast.14, f32[16,512]{1,0:T(8,128)} %copy-done.6, f32[16,512]{1,0:T(8,128)} %get-tuple-element.15.refs_1_, f32[16,512]{1,0:T(8,128)} %get-tuple-element.14.refs_2_, ...), custom_call_target="tpu_custom_call" | custom-call | flops 1048576 | bytes 12582912 | tf_op jit(solution)/shard_map/finish/pallas_call | solution.py:254
Async XLA Ops:
  3.1 63.2 %copy-start.2 = (s32[128]{0:T(128)S(1)}, s32[128]{0:T(128)}, u32[]{:S(2)}) copy-start(s32[128]{0:T(128)} %shift_ref.1) | copy-start | bytes 1540
  3.1 63.2 %copy-start.3 = (f32[128]{0:T(128)S(1)}, f32[128]{0:T(128)}, u32[]{:S(2)}) copy-start(f32[128]{0:T(128)} %fraction_ref.1) | copy-start | bytes 1540
  70.4 59.2 %all-to-all-start.1 = ((f32[32,8,4,8,128]{4,3,2,1,0:T(8,128)}), f32[32,8,4,8,128]{4,3,2,1,0:T(8,128)}, u32[]{:S(2)}, u32[]{:S(2)}) async-start(f32[32,8,4,8,128]{4,3,2,1,0:T(8,128)} %shift_rows.1), calls=%async_computation.1 | async-start | bytes 8388608 | tf_op jit(solution)/shard_map/all_to_all | solution.py:404
  75.3 14.7 %copy-start = (f32[7,2,128,512]{3,2,1,0:T(8,128)S(1)}, f32[7,2,128,512]{3,2,1,0:T(8,128)}, u32[]{:S(2)}) copy-start(f32[7,2,128,512]{3,2,1,0:T(8,128)} %carried_ref) | copy-start | bytes 11010052
  75.3 14.7 %copy-start.1 = (f32[2,128,512]{2,1,0:T(8,128)S(1)}, f32[2,128,512]{2,1,0:T(8,128)}, u32[]{:S(2)}) copy-start(f32[2,128,512]{2,1,0:T(8,128)} %density_ref) | copy-start | bytes 1572868
  79.6 50.0 %collective-permute-start.2 = (f32[128,128]{1,0:T(8,128)}, f32[128,128]{1,0:T(8,128)S(1)}, u32[]{:S(2)}, u32[]{:S(2)}) collective-permute-start(f32[128,128]{1,0:T(8,128)} %get-tuple-element.16.refs_6_), channel_id=1, source_target_pairs={{0,1},{1,2},{2,3},{3,4},{4,5},{5,6},{6,7},{7,8},{8,9},{9,10},{10,1... | collective-permute-start | bytes 196616 | tf_op jit(solution)/shard_map/ppermute | solution.py:22
  82.8 46.8 %collective-permute-start.3 = (f32[128,128]{1,0:T(8,128)}, f32[128,128]{1,0:T(8,128)S(1)}, u32[]{:S(2)}, u32[]{:S(2)}) collective-permute-start(f32[128,128]{1,0:T(8,128)} %get-tuple-element.17.refs_5_), channel_id=1, source_target_pairs={{0,31},{1,0},{2,1},{3,2},{4,3},{5,4},{6,5},{7,6},{8,7},{9,8},{10,9... | collective-permute-start | bytes 196616 | tf_op jit(solution)/shard_map/ppermute | solution.py:22
  87.4 9.8 %collective-permute-start = (f32[16,512]{1,0:T(8,128)}, f32[16,512]{1,0:T(8,128)S(1)}, u32[]{:S(2)}, u32[]{:S(2)}) collective-permute-start(f32[16,512]{1,0:T(8,128)} %get-tuple-element.14.refs_2_), channel_id=1, source_target_pairs={{0,32},{32,64},{64,96},{1,33},{33,65},{65,97},{2,34},{34,66},{66,9... | collective-permute-start | bytes 98312 | tf_op jit(solution)/shard_map/ppermute | solution.py:22
  88.7 8.5 %collective-permute-start.1 = (f32[16,512]{1,0:T(8,128)}, f32[16,512]{1,0:T(8,128)S(1)}, u32[]{:S(2)}, u32[]{:S(2)}) collective-permute-start(f32[16,512]{1,0:T(8,128)} %get-tuple-element.15.refs_1_), channel_id=1, source_target_pairs={{32,0},{64,32},{96,64},{33,1},{65,33},{97,65},{34,2},{66,34},{98,6... | collective-permute-start | bytes 98312 | tf_op jit(solution)/shard_map/ppermute | solution.py:22
  97.3 32.3 %copy-start.6 = (f32[16,512]{1,0:T(8,128)}, f32[16,512]{1,0:T(8,128)S(1)}, u32[]{:S(2)}) copy-start(f32[16,512]{1,0:T(8,128)S(1)} %collective-permute-done.refs_0_) | copy-start | bytes 98308
  97.3 32.3 %copy-start.7 = (f32[16,512]{1,0:T(8,128)}, f32[16,512]{1,0:T(8,128)S(1)}, u32[]{:S(2)}) copy-start(f32[16,512]{1,0:T(8,128)S(1)} %collective-permute-done.1.refs_3_) | copy-start | bytes 98308
  129.6 0.6 copy-start.4
  129.6 0.6 copy-start.5

commit v5 on v4

--- a/solution.py
+++ b/solution.py
@@ -150,29 +150,21 @@
     def layer(ref, c):
         return ref[c * height : (c + 1) * height, :]
 
-    def radial(ref):
+    def velocity(ref, direction):
         rho = layer(ref, 0)
-        return layer(ref, 1) / jnp.where(rho == 0.0, 1.0, rho)
-
-    for lower, upper, sign, start in ((inner, first_rows, 0.04, 0), (last_rows, outer, -0.04, FIELDS * height)):
-        v_lower, v_upper = radial(lower), radial(upper)
+        return layer(ref, 1 + direction) / jnp.where(rho == 0.0, 1.0, rho)
+
+    def fluxes(lower, upper, direction, scale, out, start):
+        v_lower, v_upper = velocity(lower, direction), velocity(upper, direction)
         speed = face_speed(v_lower, v_upper)
         for c in range(FIELDS):
             flux = flux2(v_lower, v_upper, speed, layer(lower, c), layer(upper, c))
-            rows_ref[start + c * height : start + (c + 1) * height, :] = sign * flux
-
-    odd = lax.broadcasted_iota(jnp.int32, cells_ref.shape, 1) % 2 == 1
-
-    def azimuthal(cells):
-        v = [cells[:, 4 + z : 5 + z] / cells[:, z : z + 1] for z in range(2)]
-        return jnp.where(odd, v[1], v[0])
-
-    def flux(lower, upper):
-        v_lower, v_upper = azimuthal(lower), azimuthal(upper)
-        return 0.04 * flux2(v_lower, v_upper, face_speed(v_lower, v_upper), lower, upper)
-
-    upper_faces = pltpu.roll(flux(last_cells[...], right[...]), FIELDS * height, 1)
-    cells_ref[...] = flux(left[...], first_cells[...]) - upper_faces
+            out[start + c * height : start + (c + 1) * height, :] = scale * flux
+
+    fluxes(inner, first_rows, 0, 0.04, rows_ref, 0)
+    fluxes(last_rows, outer, 0, -0.04, rows_ref, FIELDS * height)
+    fluxes(left, first_cells, 1, 0.04, cells_ref, 0)
+    fluxes(last_cells, right, 1, -0.04, cells_ref, FIELDS * height)
 
 
 def finish_kernel(
@@ -206,7 +198,11 @@
     for copy in edges:
         copy.wait()
     layers = [layer_rows.at[i] for i in range(4)] + [layer_cells.at[i] for i in range(4)]
+    edge_cells[2 * FIELDS * height :, :] = jnp.zeros(
+        (LANES - 2 * FIELDS * height, edge_cells.shape[1]), jnp.float32
+    )
     edge_fluxes(height, *layers, edge_rows, edge_cells)
+    edge_cells[...] = edge_cells[...].T
 
     def subtract(g, _):
         cells = edge_cells[pl.ds(pl.multiple_of(g * ROWS, ROWS), ROWS), :]
@@ -250,14 +246,14 @@
     groups = rows // ROWS
     hbm = pl.BlockSpec(memory_space=pltpu.HBM)
     natural = (height, groups, ROWS, width)
-    layers = [in_hbm(layer) for layer in row_layers + cell_layers]
+    layers = row_layers + cell_layers
     return pl.pallas_call(
         functools.partial(finish_kernel, groups, height, chunks),
         out_shape=[
             jax.ShapeDtypeStruct(natural, jnp.float32),
             jax.ShapeDtypeStruct((FIELDS - 1,) + natural, jnp.float32),
         ],
-        in_specs=[hbm] * 10,
+        in_specs=[hbm] * 2 + [pl.BlockSpec(memory_space=pl.ANY)] * 8,
         out_specs=[hbm, hbm],
         scratch_shapes=[
             pltpu.VMEM((4,) + row_layers[0].shape, jnp.float32),
@@ -265,7 +261,7 @@
             pltpu.VMEM((groups, height) + moved.shape[1:], jnp.float32),
             pltpu.VMEM((FIELDS,) + natural, jnp.float32),
             pltpu.VMEM((2 * FIELDS * height, width), jnp.float32),
-            pltpu.VMEM(cell_layers[0].shape, jnp.float32),
+            pltpu.VMEM((LANES, rows), jnp.float32),
             pltpu.VMEM((FIELDS,) + natural, jnp.float32),
             pltpu.SemaphoreType.DMA((2, 4)),
             pltpu.SemaphoreType.DMA((chunks, 2)),
@@ -341,7 +337,7 @@
     )(density, carried)
 
 
-def border_kernel(groups, height, width, density_ref, carried_ref, first_rows, last_rows, first_cells, last_cells, rows, cells, sems):
+def border_kernel(groups, height, width, density_ref, carried_ref, first_rows, last_rows, first_cells, last_cells, rows, cells, columns, sems):
     copies = []
     for side, g, at in ((0, 0, 0), (1, groups - 1, width - LANES)):
         for i, (source, fields) in enumerate(((density_ref, 0), (carried_ref, pl.ds(1, FIELDS - 1)))):
@@ -364,15 +360,17 @@
 
     def gather(g, _):
         here = pl.ds(pl.multiple_of(g * ROWS, ROWS), ROWS)
-        for side, out, at in ((0, first_cells, 0), (1, last_cells, LANES - 1)):
+        for side, at in ((0, 0), (1, LANES - 1)):
             total = jnp.zeros((ROWS, LANES), jnp.float32)
             for k in range(FIELDS * height):
                 value = pltpu.roll(cells[side, k // height, k % height, g], (k - at) % LANES, 1)
                 total = jnp.where(lane == k, value, total)
-            out[here, :] = total
+            columns[side, here, :] = total
         return 0
 
     lax.fori_loop(0, groups, gather, 0)
+    first_cells[...] = columns[0].T[: FIELDS * height]
+    last_cells[...] = columns[1].T[: FIELDS * height]
 
 
 def borders_of(density, carried):
@@ -380,7 +378,7 @@
     groups = rows // ROWS
     natural = (height, groups, ROWS, width)
     row_shape = pltpu.HBM((FIELDS * height, width), jnp.float32)
-    cell_shape = pltpu.HBM((rows, LANES), jnp.float32)
+    cell_shape = pltpu.HBM((FIELDS * height, rows), jnp.float32)
     return pl.pallas_call(
         functools.partial(border_kernel, groups, height, width),
         out_shape=[row_shape, row_shape, cell_shape, cell_shape],
@@ -389,6 +387,7 @@
         scratch_shapes=[
             pltpu.VMEM((2, FIELDS, height, ROWS, width), jnp.float32),
             pltpu.VMEM((2, FIELDS, height, groups, ROWS, LANES), jnp.float32),
+            pltpu.VMEM((2, rows, LANES), jnp.float32),
             pltpu.SemaphoreType.DMA((2, 2, 2)),
         ],
         compiler_params=pltpu.CompilerParams(vmem_limit_bytes=8 * 2**20),

time: 137 us -> 135 us (0.985)
    ppermute x4, waiting for transfers between devices: 32.3 us -> 29.5 us  [neighbours(): return lax.ppermute(value, axis, pairs)]
    all_to_all x1, waiting for transfers between devices: 0.01 us -> 1.68 us  [local(): moved = lax.all_to_all(moved, 'phi', 0, 0, tiled=True)]
  transfers between devices with their start and end apart: 5 -> 5, of which waited for: 1 -> 2; matrix products, arithmetic and copies ran while one was open for 0% -> 0% of each run, Pallas kernels for 8% -> 9%
where the time goes in v5:
time: 135 us
  blocking collectives  63.2 us (47%)
  waiting for transfers between devices  31.1 us (23%)
  Pallas kernels  24.1 us (18%)
  starting transfers between devices  15.4 us (11%)
    all_to_all x1, blocking collectives, local(): received = lax.all_to_all(pack(density, carried), 'phi', 0, 0, tiled=True)  63.2 us
    ppermute x4, waiting for transfers between devices, neighbours(): return lax.ppermute(value, axis, pairs)  29.5 us
    ppermute x4, starting transfers between devices, neighbours(): return lax.ppermute(value, axis, pairs)  10.5 us
    pallas_call x1, Pallas kernels, update_of(): pl.pallas_call(functools.partial(update_kernel, rows // ROWS, width), out...  7.21 us
    pallas_call x1, Pallas kernels, finish(): pl.pallas_call(functools.partial(finish_kernel, groups, height, chunks),...  6.06 us
    all_to_all x1, starting transfers between devices, local(): moved = lax.all_to_all(moved, 'phi', 0, 0, tiled=True)  4.88 us
    pallas_call x1, Pallas kernels, borders_of(): pl.pallas_call(functools.partial(border_kernel, groups, height, width), o...  4.33 us
    pallas_call x1, Pallas kernels, shift_rows(): pl.pallas_call(functools.partial(shift_kernel, blocks, tiles, chunks, hei...  4.02 us
  transfers between devices with their start and end apart: 5, of which 2 were waited for; matrix products, arithmetic and copies ran while one was open for 0% of the time, Pallas kernels for 9%

profile of v5, /device:TPU:0, one launch (start us, length us, event | category | flops | bytes accessed | tf_op | source)
XLA Modules:
  0.0 134.6 jit_solution(8483022721148214151)
XLA Ops:
  0.6 2.5 %pack.1 = f32[32,8,4,8,128]{4,3,2,1,0:T(8,128)S(1)} custom-call(f32[2,16,8,512]{3,2,1,0:T(8,128)} %bitcast.12, f32[7,2,16,8,512]{4,3,2,1,0:T(8,128)} %bitcast.9), custom_call_target="tpu_custom_call" | custom-call | bytes 8388608 | tf_op jit(solution)/shard_map/pack/pallas_call | solution.py:74
  3.1 0.0 copy-start.6
  3.1 0.0 copy-start.7
  3.1 63.2 %all_to_all.10 = f32[32,8,4,8,128]{4,3,2,1,0:T(8,128)S(1)} all-to-all(f32[32,8,4,8,128]{4,3,2,1,0:T(8,128)S(1)} %pack.1), channel_id=1, replica_groups=mesh['rad'=4,'phi'=32] {'phi'}, dimensions={0} | all-to-all | bytes 8388608 | tf_op jit(solution)/shard_map/all_to_all | solution.py:400
  66.4 0.0 copy-done.6
  66.4 0.0 copy-done.7
  66.4 4.0 %shift_rows.1 = f32[32,8,4,8,128]{4,3,2,1,0:T(8,128)} custom-call(s32[128]{0:T(128)S(1)} %copy-done.6, f32[128]{0:T(128)S(1)} %copy-done.7, f32[1024,8,128]{2,1,0:T(8,128)S(1)} %bitcast.11), custom_call_target="tpu_custom_call" | custom-call | flops 8388608 | bytes 8388608 | tf_op jit(solution)/shard_map/shift_rows/pallas_call | solution.py:135
  70.4 4.9 %all-to-all-start.1 = ((f32[32,8,4,8,128]{4,3,2,1,0:T(8,128)}), f32[32,8,4,8,128]{4,3,2,1,0:T(8,128)}, u32[]{:S(2)}, u32[]{:S(2)}) async-start(f32[32,8,4,8,128]{4,3,2,1,0:T(8,128)} %shift_rows.1), calls=%async_computation.1 | async-start | bytes 8388608 | tf_op jit(solution)/shard_map/all_to_all | solution.py:403
  75.3 0.0 copy-start
  75.3 0.0 copy-start.1
  75.3 4.3 %borders.1 = (f32[16,512]{1,0:T(8,128)}, f32[16,512]{1,0:T(8,128)}, f32[16,128]{1,0:T(8,128)}, f32[16,128]{1,0:T(8,128)}) custom-call(f32[2,16,8,512]{3,2,1,0:T(8,128)} %bitcast.13, f32[7,2,16,8,512]{4,3,2,1,0:T(8,128)} %bitcast.10), custom_call_target="tpu_custom_call" | custom-call | tf_op jit(solution)/shard_map/borders/pallas_call | solution.py:382
  79.6 1.3 collective-permute-start
  80.9 1.3 collective-permute-start.1
  82.2 3.2 %collective-permute-start.2 = (f32[16,128]{1,0:T(8,128)}, f32[16,128]{1,0:T(8,128)S(1)}, u32[]{:S(2)}, u32[]{:S(2)}) collective-permute-start(f32[16,128]{1,0:T(8,128)} %get-tuple-element.16.refs_6_), channel_id=1, source_target_pairs={{0,1},{1,2},{2,3},{3,4},{4,5},{5,6},{6,7},{7,8},{8,9},{9,10},{10,1... | collective-permute-start | bytes 24584 | tf_op jit(solution)/shard_map/ppermute | solution.py:22
  85.4 0.0 copy-start.2
  85.4 0.0 copy-start.3
  85.4 0.0 copy-start.4
  85.4 0.0 copy-start.5
  85.4 4.7 %collective-permute-start.3 = (f32[16,128]{1,0:T(8,128)}, f32[16,128]{1,0:T(8,128)S(1)}, u32[]{:S(2)}, u32[]{:S(2)}) collective-permute-start(f32[16,128]{1,0:T(8,128)} %get-tuple-element.17.refs_5_), channel_id=1, source_target_pairs={{0,31},{1,0},{2,1},{3,2},{4,3},{5,4},{6,5},{7,6},{8,7},{9,8},{10,9... | collective-permute-start | bytes 24584 | tf_op jit(solution)/shard_map/ppermute | solution.py:22
  90.1 0.0 copy-done
  90.1 0.0 copy-done.1
  90.1 7.2 %flux_update.1 = f32[8,2,128,512]{3,2,1,0:T(8,128)} custom-call(f32[2,128,512]{2,1,0:T(8,128)S(1)} %copy-done.1, f32[7,2,128,512]{3,2,1,0:T(8,128)S(1)} %copy-done), custom_call_target="tpu_custom_call" | custom-call | flops 41943040 | bytes 8388608 | tf_op jit(solution)/shard_map/flux_update/pallas_call | solution.py:328
  97.4 29.4 %collective-permute-done.2.refs_4_ = f32[16,128]{1,0:T(8,128)S(1)} collective-permute-done((f32[16,128]{1,0:T(8,128)}, f32[16,128]{1,0:T(8,128)S(1)}, u32[]{:S(2)}, u32[]{:S(2)}) %collective-permute-start.2) | collective-permute-done | bytes 8224 | tf_op jit(solution)/shard_map/ppermute | solution.py:22
  126.8 0.0 collective-permute-done.3.refs_7_
  126.8 0.0 collective-permute-done.refs_0_
  126.8 0.0 collective-permute-done.1.refs_3_
  126.8 1.7 %all-to-all-done.1 = f32[32,8,4,8,128]{4,3,2,1,0:T(8,128)} async-done(((f32[32,8,4,8,128]{4,3,2,1,0:T(8,128)}), f32[32,8,4,8,128]{4,3,2,1,0:T(8,128)}, u32[]{:S(2)}, u32[]{:S(2)}) %all-to-all-start.1) | async-done | bytes 4194336 | tf_op jit(solution)/shard_map/all_to_all | solution.py:403
  128.5 0.0 copy-done.2
  128.5 0.0 copy-done.3
  128.5 0.0 copy-done.4
  128.5 0.0 copy-done.5
  128.5 6.1 %finish.1 = (f32[2,16,8,512]{3,2,1,0:T(8,128)}, f32[7,2,16,8,512]{4,3,2,1,0:T(8,128)}) custom-call(f32[16,2,8,4,8,128]{5,4,3,2,1,0:T(8,128)} %bitcast.3.moved_ref, f32[8,2,16,8,512]{4,3,2,1,0:T(8,128)} %bitcast.14, f32[16,512]{1,0:T(8,128)S(1)} %collective-permute-done.refs_0_, f32[16,512]{1,0:T(8,128)S(1)} %copy-done.2, f32[16,512]{1,0:T(8,128)S(1)} %copy-done.3, ...), custom_call_target="tpu_custom_call" | custom-call | flops 1048576 | bytes 12582912 | tf_op jit(solution)/shard_map/finish/pallas_call | solution.py:250
Async XLA Ops:
  3.1 63.2 %copy-start.6 = (s32[128]{0:T(128)S(1)}, s32[128]{0:T(128)}, u32[]{:S(2)}) copy-start(s32[128]{0:T(128)} %shift_ref.1) | copy-start | bytes 1540
  3.1 63.2 %copy-start.7 = (f32[128]{0:T(128)S(1)}, f32[128]{0:T(128)}, u32[]{:S(2)}) copy-start(f32[128]{0:T(128)} %fraction_ref.1) | copy-start | bytes 1540
  70.4 58.1 %all-to-all-start.1 = ((f32[32,8,4,8,128]{4,3,2,1,0:T(8,128)}), f32[32,8,4,8,128]{4,3,2,1,0:T(8,128)}, u32[]{:S(2)}, u32[]{:S(2)}) async-start(f32[32,8,4,8,128]{4,3,2,1,0:T(8,128)} %shift_rows.1), calls=%async_computation.1 | async-start | bytes 8388608 | tf_op jit(solution)/shard_map/all_to_all | solution.py:403
  75.3 14.9 %copy-start = (f32[7,2,128,512]{3,2,1,0:T(8,128)S(1)}, f32[7,2,128,512]{3,2,1,0:T(8,128)}, u32[]{:S(2)}) copy-start(f32[7,2,128,512]{3,2,1,0:T(8,128)} %carried_ref) | copy-start | bytes 11010052
  75.3 14.9 %copy-start.1 = (f32[2,128,512]{2,1,0:T(8,128)S(1)}, f32[2,128,512]{2,1,0:T(8,128)}, u32[]{:S(2)}) copy-start(f32[2,128,512]{2,1,0:T(8,128)} %density_ref) | copy-start | bytes 1572868
  79.6 47.2 %collective-permute-start = (f32[16,512]{1,0:T(8,128)}, f32[16,512]{1,0:T(8,128)S(1)}, u32[]{:S(2)}, u32[]{:S(2)}) collective-permute-start(f32[16,512]{1,0:T(8,128)} %get-tuple-element.14.refs_2_), channel_id=1, source_target_pairs={{0,32},{32,64},{64,96},{1,33},{33,65},{65,97},{2,34},{34,66},{66,9... | collective-permute-start | bytes 98312 | tf_op jit(solution)/shard_map/ppermute | solution.py:22
  80.9 45.9 %collective-permute-start.1 = (f32[16,512]{1,0:T(8,128)}, f32[16,512]{1,0:T(8,128)S(1)}, u32[]{:S(2)}, u32[]{:S(2)}) collective-permute-start(f32[16,512]{1,0:T(8,128)} %get-tuple-element.15.refs_1_), channel_id=1, source_target_pairs={{32,0},{64,32},{96,64},{33,1},{65,33},{97,65},{34,2},{66,34},{98,6... | collective-permute-start | bytes 98312 | tf_op jit(solution)/shard_map/ppermute | solution.py:22
  82.2 44.6 %collective-permute-start.2 = (f32[16,128]{1,0:T(8,128)}, f32[16,128]{1,0:T(8,128)S(1)}, u32[]{:S(2)}, u32[]{:S(2)}) collective-permute-start(f32[16,128]{1,0:T(8,128)} %get-tuple-element.16.refs_6_), channel_id=1, source_target_pairs={{0,1},{1,2},{2,3},{3,4},{4,5},{5,6},{6,7},{7,8},{8,9},{9,10},{10,1... | collective-permute-start | bytes 24584 | tf_op jit(solution)/shard_map/ppermute | solution.py:22
  85.4 43.1 %copy-start.2 = (f32[16,512]{1,0:T(8,128)S(1)}, f32[16,512]{1,0:T(8,128)}, u32[]{:S(2)}) copy-start(f32[16,512]{1,0:T(8,128)} %get-tuple-element.15.refs_1_) | copy-start | bytes 98308
  85.4 43.1 %copy-start.3 = (f32[16,512]{1,0:T(8,128)S(1)}, f32[16,512]{1,0:T(8,128)}, u32[]{:S(2)}) copy-start(f32[16,512]{1,0:T(8,128)} %get-tuple-element.14.refs_2_) | copy-start | bytes 98308
  85.4 43.1 %copy-start.4 = (f32[16,128]{1,0:T(8,128)S(1)}, f32[16,128]{1,0:T(8,128)}, u32[]{:S(2)}) copy-start(f32[16,128]{1,0:T(8,128)} %get-tuple-element.17.refs_5_) | copy-start | bytes 24580
  85.4 43.1 %copy-start.5 = (f32[16,128]{1,0:T(8,128)S(1)}, f32[16,128]{1,0:T(8,128)}, u32[]{:S(2)}) copy-start(f32[16,128]{1,0:T(8,128)} %get-tuple-element.16.refs_6_) | copy-start | bytes 24580
  85.4 41.4 %collective-permute-start.3 = (f32[16,128]{1,0:T(8,128)}, f32[16,128]{1,0:T(8,128)S(1)}, u32[]{:S(2)}, u32[]{:S(2)}) collective-permute-start(f32[16,128]{1,0:T(8,128)} %get-tuple-element.17.refs_5_), channel_id=1, source_target_pairs={{0,31},{1,0},{2,1},{3,2},{4,3},{5,4},{6,5},{7,6},{8,7},{9,8},{10,9... | collective-permute-start | bytes 24584 | tf_op jit(solution)/shard_map/ppermute | solution.py:22

commit v6 on v5

--- a/solution.py
+++ b/solution.py
@@ -10,6 +10,7 @@
 FIELDS = 8
 ROWS = 8
 LANES = 128
+NEAR = 6
 
 
 def neighbours(value, axis, step, wrap):
@@ -172,7 +173,8 @@
     height,
     chunks,
     moved_ref,
-    update_ref,
+    near_ref,
+    far_ref,
     *refs,
 ):
     row_refs, cell_refs = refs[:4], refs[4:8]
@@ -191,7 +193,7 @@
     arrivals, departures = [], []
     for i in range(chunks):
         piece = pl.ds(i * size, size)
-        ends = ((moved_ref.at[piece], taken.at[piece]), (update_ref.at[:, :, piece], change.at[:, :, piece]))
+        ends = ((moved_ref.at[piece], taken.at[piece]), (far_ref.at[:, :, piece], change.at[:, :, piece]))
         arrivals.append([pltpu.make_async_copy(*pair, in_sems.at[i, k]) for k, pair in enumerate(ends)])
         for copy in arrivals[i]:
             copy.start()
@@ -212,7 +214,8 @@
                 by_field = exchanged([taken[g, z, row, t] for row in range(ROWS)], sub)
                 for c in range(FIELDS):
                     k = c * height + z
-                    value = by_field[c] - change[c, z, g, :, at : at + LANES]
+                    by = (near_ref[c, z, g, :, at : at + LANES] if c < NEAR else change[c - NEAR, z, g, :, at : at + LANES])
+                    value = by_field[c] - by
                     if at == 0:
                         value = value + jnp.where(lane == 0, cells[:, k : k + 1], 0.0)
                     if at == width - LANES:
@@ -241,8 +244,8 @@
         copy.wait()
 
 
-def finish(moved, update, row_layers, cell_layers, chunks=4):
-    height, rows, width = update.shape[1:]
+def finish(moved, near, far, row_layers, cell_layers, chunks=4):
+    height, rows, width = near.shape[1:]
     groups = rows // ROWS
     hbm = pl.BlockSpec(memory_space=pltpu.HBM)
     natural = (height, groups, ROWS, width)
@@ -253,13 +256,13 @@
             jax.ShapeDtypeStruct(natural, jnp.float32),
             jax.ShapeDtypeStruct((FIELDS - 1,) + natural, jnp.float32),
         ],
-        in_specs=[hbm] * 2 + [pl.BlockSpec(memory_space=pl.ANY)] * 8,
+        in_specs=[hbm, pl.BlockSpec(memory_space=pltpu.VMEM), hbm] + [pl.BlockSpec(memory_space=pl.ANY)] * 8,
         out_specs=[hbm, hbm],
         scratch_shapes=[
             pltpu.VMEM((4,) + row_layers[0].shape, jnp.float32),
             pltpu.VMEM((4,) + cell_layers[0].shape, jnp.float32),
             pltpu.VMEM((groups, height) + moved.shape[1:], jnp.float32),
-            pltpu.VMEM((FIELDS,) + natural, jnp.float32),
+            pltpu.VMEM((FIELDS - NEAR,) + natural, jnp.float32),
             pltpu.VMEM((2 * FIELDS * height, width), jnp.float32),
             pltpu.VMEM((LANES, rows), jnp.float32),
             pltpu.VMEM((FIELDS,) + natural, jnp.float32),
@@ -268,9 +271,9 @@
             pltpu.SemaphoreType.DMA((chunks, 2)),
         ],
         cost_estimate=pl.CostEstimate(flops=moved.size, bytes_accessed=12 * moved.size, transcendentals=0),
-        compiler_params=pltpu.CompilerParams(vmem_limit_bytes=20 * 2**20),
+        compiler_params=pltpu.CompilerParams(vmem_limit_bytes=16 * 2**20),
         name="finish",
-    )(in_hbm(moved.reshape((groups, height) + moved.shape[1:])), in_hbm(update.reshape((FIELDS,) + natural)), *layers)
+    )(in_hbm(moved.reshape((groups, height) + moved.shape[1:])), near.reshape((NEAR,) + natural), in_hbm(far.reshape((FIELDS - NEAR,) + natural)), *layers)
 
 
 def flux2(v_left, v_right, speed, q_left, q_right):
@@ -281,7 +284,7 @@
     return jnp.maximum(jnp.abs(v_left), jnp.abs(v_right)) + 1.0
 
 
-def update_kernel(groups, width, density_ref, carried_ref, o_ref, lower_ref):
+def update_kernel(groups, width, density_ref, carried_ref, near_ref, far_ref, lower_ref):
     column = lax.broadcasted_iota(jnp.int32, (ROWS, width), 1)
     sub = lax.broadcasted_iota(jnp.int32, (ROWS, width), 0)
     lower_ref[...] = jnp.zeros_like(lower_ref)
@@ -315,7 +318,10 @@
                 upper = jnp.where(column < width - 1, flux2(v_a, v_a_up, speed_a, q, q_up), 0.0)
                 total = total + (upper - pltpu.roll(upper, 1, 1))
                 total = total + speed_height * (q - field(c, 1 - z, rows))
-                o_ref[c, z, rows, :] = 0.04 * total
+                if c < NEAR:
+                    near_ref[c, z, rows, :] = 0.04 * total
+                else:
+                    far_ref[c - NEAR, z, rows, :] = 0.04 * total
         return 0
 
     lax.fori_loop(0, groups, body, 0)
@@ -327,9 +333,12 @@
     vmem = pl.BlockSpec(memory_space=pltpu.VMEM)
     return pl.pallas_call(
         functools.partial(update_kernel, rows // ROWS, width),
-        out_shape=pltpu.HBM((FIELDS,) + density.shape, density.dtype),
+        out_shape=[
+            jax.ShapeDtypeStruct((NEAR,) + density.shape, density.dtype),
+            pltpu.HBM((FIELDS - NEAR,) + density.shape, density.dtype),
+        ],
         in_specs=[vmem] * 2,
-        out_specs=vmem,
+        out_specs=[vmem] * 2,
         scratch_shapes=[pltpu.VMEM((FIELDS, 2, ROWS, width), jnp.float32)],
         cost_estimate=pl.CostEstimate(flops=40 * size, bytes_accessed=8 * size, transcendentals=0),
         compiler_params=pltpu.CompilerParams(vmem_limit_bytes=24 * 2**20),
@@ -407,10 +416,11 @@
     outer = neighbours(first_rows, "rad", -1, False)
     left = neighbours(last_cells, "phi", 1, True)
     right = neighbours(first_cells, "phi", -1, True)
-    update = update_of(density, carried)
+    near, far = update_of(density, carried)
     density_next, carried_next = finish(
         moved,
-        update,
+        near,
+        far,
         [inner, first_rows, last_rows, outer],
         [left, first_cells, last_cells, right],
     )

time: 135 us -> 133 us (0.985)
  Pallas kernels: 24.1 us -> 21.4 us
    pallas_call x1, Pallas kernels: 6.06 us -> 4.21 us  [finish(): pl.pallas_call(functools.partial(finish_kernel, groups, height, chunks),...]
  transfers between devices with their start and end apart: 5 -> 5, of which waited for: 2 -> 2; matrix products, arithmetic and copies ran while one was open for 0% -> 0% of each run, Pallas kernels for 9% -> 8%
where the time goes in v6:
time: 133 us
  blocking collectives  63.2 us (48%)
  waiting for transfers between devices  31.9 us (24%)
  Pallas kernels  21.4 us (16%)
  starting transfers between devices  15.4 us (12%)
    all_to_all x1, blocking collectives, local(): received = lax.all_to_all(pack(density, carried), 'phi', 0, 0, tiled=True)  63.2 us
    ppermute x4, waiting for transfers between devices, neighbours(): return lax.ppermute(value, axis, pairs)  30.3 us
    ppermute x4, starting transfers between devices, neighbours(): return lax.ppermute(value, axis, pairs)  10.5 us
    pallas_call x1, Pallas kernels, update_of(): pl.pallas_call(functools.partial(update_kernel, rows // ROWS, width), out...  6.31 us
    all_to_all x1, starting transfers between devices, local(): moved = lax.all_to_all(moved, 'phi', 0, 0, tiled=True)  4.88 us
    pallas_call x1, Pallas kernels, borders_of(): pl.pallas_call(functools.partial(border_kernel, groups, height, width), o...  4.33 us
    pallas_call x1, Pallas kernels, finish(): pl.pallas_call(functools.partial(finish_kernel, groups, height, chunks),...  4.21 us
    pallas_call x1, Pallas kernels, shift_rows(): pl.pallas_call(functools.partial(shift_kernel, blocks, tiles, chunks, hei...  4.03 us
  transfers between devices with their start and end apart: 5, of which 2 were waited for; matrix products, arithmetic and copies ran while one was open for 0% of the time, Pallas kernels for 8%

profile of v6, /device:TPU:0, one launch (start us, length us, event | category | flops | bytes accessed | tf_op | source)
XLA Modules:
  0.0 132.7 jit_solution(16343125168110179662)
XLA Ops:
  0.6 2.5 %pack.1 = f32[32,8,4,8,128]{4,3,2,1,0:T(8,128)S(1)} custom-call(f32[2,16,8,512]{3,2,1,0:T(8,128)} %bitcast.13, f32[7,2,16,8,512]{4,3,2,1,0:T(8,128)} %bitcast.10), custom_call_target="tpu_custom_call" | custom-call | bytes 8388608 | tf_op jit(solution)/shard_map/pack/pallas_call | solution.py:75
  3.1 0.0 copy-start.6
  3.1 0.0 copy-start.7
  3.1 63.2 %all_to_all.10 = f32[32,8,4,8,128]{4,3,2,1,0:T(8,128)S(1)} all-to-all(f32[32,8,4,8,128]{4,3,2,1,0:T(8,128)S(1)} %pack.1), channel_id=1, replica_groups=mesh['rad'=4,'phi'=32] {'phi'}, dimensions={0} | all-to-all | bytes 8388608 | tf_op jit(solution)/shard_map/all_to_all | solution.py:409
  66.4 0.0 copy-done.6
  66.4 0.0 copy-done.7
  66.4 4.0 %shift_rows.1 = f32[32,8,4,8,128]{4,3,2,1,0:T(8,128)} custom-call(s32[128]{0:T(128)S(1)} %copy-done.6, f32[128]{0:T(128)S(1)} %copy-done.7, f32[1024,8,128]{2,1,0:T(8,128)S(1)} %bitcast.12), custom_call_target="tpu_custom_call" | custom-call | flops 8388608 | bytes 8388608 | tf_op jit(solution)/shard_map/shift_rows/pallas_call | solution.py:136
  70.4 4.9 %all-to-all-start.1 = ((f32[32,8,4,8,128]{4,3,2,1,0:T(8,128)}), f32[32,8,4,8,128]{4,3,2,1,0:T(8,128)}, u32[]{:S(2)}, u32[]{:S(2)}) async-start(f32[32,8,4,8,128]{4,3,2,1,0:T(8,128)} %shift_rows.1), calls=%async_computation.1 | async-start | bytes 8388608 | tf_op jit(solution)/shard_map/all_to_all | solution.py:412
  75.3 0.0 copy-start
  75.3 0.0 copy-start.1
  75.3 4.3 %borders.1 = (f32[16,512]{1,0:T(8,128)}, f32[16,512]{1,0:T(8,128)}, f32[16,128]{1,0:T(8,128)}, f32[16,128]{1,0:T(8,128)}) custom-call(f32[2,16,8,512]{3,2,1,0:T(8,128)} %bitcast.14, f32[7,2,16,8,512]{4,3,2,1,0:T(8,128)} %bitcast.11), custom_call_target="tpu_custom_call" | custom-call | tf_op jit(solution)/shard_map/borders/pallas_call | solution.py:391
  79.7 0.0 copy-start.2
  79.7 0.0 copy-start.3
  79.7 0.0 copy-start.4
  79.7 0.0 copy-start.5
  79.7 1.4 %collective-permute-start = (f32[16,512]{1,0:T(8,128)}, f32[16,512]{1,0:T(8,128)S(1)}, u32[]{:S(2)}, u32[]{:S(2)}) collective-permute-start(f32[16,512]{1,0:T(8,128)} %get-tuple-element.18.refs_2_), channel_id=1, source_target_pairs={{0,32},{32,64},{64,96},{1,33},{33,65},{65,97},{2,34},{34,66},{66,9... | collective-permute-start | bytes 98312 | tf_op jit(solution)/shard_map/ppermute | solution.py:23
  81.1 1.3 collective-permute-start.1
  82.4 3.2 %collective-permute-start.2 = (f32[16,128]{1,0:T(8,128)}, f32[16,128]{1,0:T(8,128)S(1)}, u32[]{:S(2)}, u32[]{:S(2)}) collective-permute-start(f32[16,128]{1,0:T(8,128)} %get-tuple-element.20.refs_6_), channel_id=1, source_target_pairs={{0,1},{1,2},{2,3},{3,4},{4,5},{5,6},{6,7},{7,8},{8,9},{9,10},{10,1... | collective-permute-start | bytes 24584 | tf_op jit(solution)/shard_map/ppermute | solution.py:23
  85.6 4.6 %collective-permute-start.3 = (f32[16,128]{1,0:T(8,128)}, f32[16,128]{1,0:T(8,128)S(1)}, u32[]{:S(2)}, u32[]{:S(2)}) collective-permute-start(f32[16,128]{1,0:T(8,128)} %get-tuple-element.21.refs_5_), channel_id=1, source_target_pairs={{0,31},{1,0},{2,1},{3,2},{4,3},{5,4},{6,5},{7,6},{8,7},{9,8},{10,9... | collective-permute-start | bytes 24584 | tf_op jit(solution)/shard_map/ppermute | solution.py:23
  90.2 0.0 copy-done
  90.3 0.0 copy-done.1
  90.3 6.3 %flux_update.1 = (f32[6,2,128,512]{3,2,1,0:T(8,128)S(1)}, f32[2,2,128,512]{3,2,1,0:T(8,128)}) custom-call(f32[2,128,512]{2,1,0:T(8,128)S(1)} %copy-done.1, f32[7,2,128,512]{3,2,1,0:T(8,128)S(1)} %copy-done), custom_call_target="tpu_custom_call" | custom-call | flops 41943040 | bytes 8388608 | tf_op jit(solution)/shard_map/flux_update/pallas_call | solution.py:334
  96.6 30.3 %collective-permute-done.2.refs_4_ = f32[16,128]{1,0:T(8,128)S(1)} collective-permute-done((f32[16,128]{1,0:T(8,128)}, f32[16,128]{1,0:T(8,128)S(1)}, u32[]{:S(2)}, u32[]{:S(2)}) %collective-permute-start.2) | collective-permute-done | bytes 8224 | tf_op jit(solution)/shard_map/ppermute | solution.py:23
  126.8 0.0 collective-permute-done.3.refs_7_
  126.8 0.0 collective-permute-done.refs_0_
  126.8 0.0 collective-permute-done.1.refs_3_
  126.8 1.7 %all-to-all-done.1 = f32[32,8,4,8,128]{4,3,2,1,0:T(8,128)} async-done(((f32[32,8,4,8,128]{4,3,2,1,0:T(8,128)}), f32[32,8,4,8,128]{4,3,2,1,0:T(8,128)}, u32[]{:S(2)}, u32[]{:S(2)}) %all-to-all-start.1) | async-done | bytes 4194336 | tf_op jit(solution)/shard_map/all_to_all | solution.py:412
  128.5 0.0 copy-done.2
  128.5 0.0 copy-done.3
  128.5 0.0 copy-done.4
  128.5 0.0 copy-done.5
  128.5 4.2 %finish.1 = (f32[2,16,8,512]{3,2,1,0:T(8,128)}, f32[7,2,16,8,512]{4,3,2,1,0:T(8,128)}) custom-call(f32[16,2,8,4,8,128]{5,4,3,2,1,0:T(8,128)} %bitcast.3.moved_ref, f32[6,2,16,8,512]{4,3,2,1,0:T(8,128)S(1)} %bitcast.15, f32[2,2,16,8,512]{4,3,2,1,0:T(8,128)} %bitcast.16, f32[16,512]{1,0:T(8,128)S(1)} %collective-permute-done.refs_0_, f32[16,512]{1,0:T(8,128)S(1)} %copy-done.2, ...), custom_call_target="tpu_custom_call" | custom-call | flops 1048576 | bytes 12582912 | tf_op jit(solution)/shard_map/finish/pallas_call | solution.py:253
Async XLA Ops:
  3.1 63.2 %copy-start.6 = (s32[128]{0:T(128)S(1)}, s32[128]{0:T(128)}, u32[]{:S(2)}) copy-start(s32[128]{0:T(128)} %shift_ref.1) | copy-start | bytes 1540
  3.1 63.2 %copy-start.7 = (f32[128]{0:T(128)S(1)}, f32[128]{0:T(128)}, u32[]{:S(2)}) copy-start(f32[128]{0:T(128)} %fraction_ref.1) | copy-start | bytes 1540
  70.4 58.1 %all-to-all-start.1 = ((f32[32,8,4,8,128]{4,3,2,1,0:T(8,128)}), f32[32,8,4,8,128]{4,3,2,1,0:T(8,128)}, u32[]{:S(2)}, u32[]{:S(2)}) async-start(f32[32,8,4,8,128]{4,3,2,1,0:T(8,128)} %shift_rows.1), calls=%async_computation.1 | async-start | bytes 8388608 | tf_op jit(solution)/shard_map/all_to_all | solution.py:412
  75.3 15.0 %copy-start = (f32[7,2,128,512]{3,2,1,0:T(8,128)S(1)}, f32[7,2,128,512]{3,2,1,0:T(8,128)}, u32[]{:S(2)}) copy-start(f32[7,2,128,512]{3,2,1,0:T(8,128)} %carried_ref) | copy-start | bytes 11010052
  75.3 15.0 %copy-start.1 = (f32[2,128,512]{2,1,0:T(8,128)S(1)}, f32[2,128,512]{2,1,0:T(8,128)}, u32[]{:S(2)}) copy-start(f32[2,128,512]{2,1,0:T(8,128)} %density_ref) | copy-start | bytes 1572868
  79.7 48.8 %copy-start.2 = (f32[16,512]{1,0:T(8,128)S(1)}, f32[16,512]{1,0:T(8,128)}, u32[]{:S(2)}) copy-start(f32[16,512]{1,0:T(8,128)} %get-tuple-element.19.refs_1_) | copy-start | bytes 98308
  79.7 48.8 %copy-start.3 = (f32[16,512]{1,0:T(8,128)S(1)}, f32[16,512]{1,0:T(8,128)}, u32[]{:S(2)}) copy-start(f32[16,512]{1,0:T(8,128)} %get-tuple-element.18.refs_2_) | copy-start | bytes 98308
  79.7 48.8 %copy-start.4 = (f32[16,128]{1,0:T(8,128)S(1)}, f32[16,128]{1,0:T(8,128)}, u32[]{:S(2)}) copy-start(f32[16,128]{1,0:T(8,128)} %get-tuple-element.21.refs_5_) | copy-start | bytes 24580
  79.7 48.8 %copy-start.5 = (f32[16,128]{1,0:T(8,128)S(1)}, f32[16,128]{1,0:T(8,128)}, u32[]{:S(2)}) copy-start(f32[16,128]{1,0:T(8,128)} %get-tuple-element.20.refs_6_) | copy-start | bytes 24580
  79.7 47.1 %collective-permute-start = (f32[16,512]{1,0:T(8,128)}, f32[16,512]{1,0:T(8,128)S(1)}, u32[]{:S(2)}, u32[]{:S(2)}) collective-permute-start(f32[16,512]{1,0:T(8,128)} %get-tuple-element.18.refs_2_), channel_id=1, source_target_pairs={{0,32},{32,64},{64,96},{1,33},{33,65},{65,97},{2,34},{34,66},{66,9... | collective-permute-start | bytes 98312 | tf_op jit(solution)/shard_map/ppermute | solution.py:23
  81.1 45.7 %collective-permute-start.1 = (f32[16,512]{1,0:T(8,128)}, f32[16,512]{1,0:T(8,128)S(1)}, u32[]{:S(2)}, u32[]{:S(2)}) collective-permute-start(f32[16,512]{1,0:T(8,128)} %get-tuple-element.19.refs_1_), channel_id=1, source_target_pairs={{32,0},{64,32},{96,64},{33,1},{65,33},{97,65},{34,2},{66,34},{98,6... | collective-permute-start | bytes 98312 | tf_op jit(solution)/shard_map/ppermute | solution.py:23
  82.4 44.4 %collective-permute-start.2 = (f32[16,128]{1,0:T(8,128)}, f32[16,128]{1,0:T(8,128)S(1)}, u32[]{:S(2)}, u32[]{:S(2)}) collective-permute-start(f32[16,128]{1,0:T(8,128)} %get-tuple-element.20.refs_6_), channel_id=1, source_target_pairs={{0,1},{1,2},{2,3},{3,4},{4,5},{5,6},{6,7},{7,8},{8,9},{9,10},{10,1... | collective-permute-start | bytes 24584 | tf_op jit(solution)/shard_map/ppermute | solution.py:23
  85.6 41.2 %collective-permute-start.3 = (f32[16,128]{1,0:T(8,128)}, f32[16,128]{1,0:T(8,128)S(1)}, u32[]{:S(2)}, u32[]{:S(2)}) collective-permute-start(f32[16,128]{1,0:T(8,128)} %get-tuple-element.21.refs_5_), channel_id=1, source_target_pairs={{0,31},{1,0},{2,1},{3,2},{4,3},{5,4},{6,5},{7,6},{8,7},{9,8},{10,9... | collective-permute-start | bytes 24584 | tf_op jit(solution)/shard_map/ppermute | solution.py:23

commit v7 on v6

--- a/solution.py
+++ b/solution.py
@@ -177,19 +177,12 @@
     far_ref,
     *refs,
 ):
-    row_refs, cell_refs = refs[:4], refs[4:8]
-    density_ref, carried_ref, layer_rows, layer_cells, taken, change, edge_rows, edge_cells, new = refs[8:17]
-    edge_sems, in_sems, out_sems = refs[17:]
+    density_ref, carried_ref, taken, change, edge_rows, edge_cells, new = refs[8:15]
+    in_sems, out_sems = refs[15:]
     size = groups // chunks
     width = change.shape[-1]
     lane = lax.broadcasted_iota(jnp.int32, (ROWS, LANES), 1)
     sub = lax.broadcasted_iota(jnp.int32, (ROWS, LANES), 0)
-    edges = []
-    for i in range(4):
-        edges.append(pltpu.make_async_copy(row_refs[i], layer_rows.at[i], edge_sems.at[0, i]))
-        edges.append(pltpu.make_async_copy(cell_refs[i], layer_cells.at[i], edge_sems.at[1, i]))
-    for copy in edges:
-        copy.start()
     arrivals, departures = [], []
     for i in range(chunks):
         piece = pl.ds(i * size, size)
@@ -197,13 +190,10 @@
         arrivals.append([pltpu.make_async_copy(*pair, in_sems.at[i, k]) for k, pair in enumerate(ends)])
         for copy in arrivals[i]:
             copy.start()
-    for copy in edges:
-        copy.wait()
-    layers = [layer_rows.at[i] for i in range(4)] + [layer_cells.at[i] for i in range(4)]
     edge_cells[2 * FIELDS * height :, :] = jnp.zeros(
         (LANES - 2 * FIELDS * height, edge_cells.shape[1]), jnp.float32
     )
-    edge_fluxes(height, *layers, edge_rows, edge_cells)
+    edge_fluxes(height, *refs[:8], edge_rows, edge_cells)
     edge_cells[...] = edge_cells[...].T
 
     def subtract(g, _):
@@ -256,17 +246,14 @@
             jax.ShapeDtypeStruct(natural, jnp.float32),
             jax.ShapeDtypeStruct((FIELDS - 1,) + natural, jnp.float32),
         ],
-        in_specs=[hbm, pl.BlockSpec(memory_space=pltpu.VMEM), hbm] + [pl.BlockSpec(memory_space=pl.ANY)] * 8,
+        in_specs=[hbm, pl.BlockSpec(memory_space=pltpu.VMEM), hbm] + [pl.BlockSpec(memory_space=pltpu.VMEM)] * 8,
         out_specs=[hbm, hbm],
         scratch_shapes=[
-            pltpu.VMEM((4,) + row_layers[0].shape, jnp.float32),
-            pltpu.VMEM((4,) + cell_layers[0].shape, jnp.float32),
             pltpu.VMEM((groups, height) + moved.shape[1:], jnp.float32),
             pltpu.VMEM((FIELDS - NEAR,) + natural, jnp.float32),
             pltpu.VMEM((2 * FIELDS * height, width), jnp.float32),
             pltpu.VMEM((LANES, rows), jnp.float32),
             pltpu.VMEM((FIELDS,) + natural, jnp.float32),
-            pltpu.SemaphoreType.DMA((2, 4)),
             pltpu.SemaphoreType.DMA((chunks, 2)),
             pltpu.SemaphoreType.DMA((chunks, 2)),
         ],

time: 133 us -> 133 us (level)
  no operation moved by 1% of the time
where the time goes in v7:
time: 133 us; the launch traced here: 132 us
  blocking collectives  63.2 us (48%)
  waiting for transfers between devices  32 us (24%)
  Pallas kernels  21.1 us (16%)
  starting transfers between devices  15.4 us (12%)
    all_to_all x1, blocking collectives, local(): received = lax.all_to_all(pack(density, carried), 'phi', 0, 0, tiled=True)  63.2 us
    ppermute x4, waiting for transfers between devices, neighbours(): return lax.ppermute(value, axis, pairs)  30.3 us
    ppermute x4, starting transfers between devices, neighbours(): return lax.ppermute(value, axis, pairs)  10.5 us
    pallas_call x1, Pallas kernels, update_of(): pl.pallas_call(functools.partial(update_kernel, rows // ROWS, width), out...  6.31 us
    all_to_all x1, starting transfers between devices, local(): moved = lax.all_to_all(moved, 'phi', 0, 0, tiled=True)  4.88 us
    pallas_call x1, Pallas kernels, borders_of(): pl.pallas_call(functools.partial(border_kernel, groups, height, width), o...  4.33 us
    pallas_call x1, Pallas kernels, shift_rows(): pl.pallas_call(functools.partial(shift_kernel, blocks, tiles, chunks, hei...  4.02 us
    pallas_call x1, Pallas kernels, finish(): pl.pallas_call(functools.partial(finish_kernel, groups, height, chunks),...  3.93 us
  transfers between devices with their start and end apart: 5, of which 2 were waited for; matrix products, arithmetic and copies ran while one was open for 0% of the time, Pallas kernels for 8%

profile of v7, /device:TPU:0, one launch (start us, length us, event | category | flops | bytes accessed | tf_op | source)
XLA Modules:
  0.0 132.5 jit_solution(8343397268005100362)
XLA Ops:
  0.6 2.5 %pack.1 = f32[32,8,4,8,128]{4,3,2,1,0:T(8,128)S(1)} custom-call(f32[2,16,8,512]{3,2,1,0:T(8,128)} %bitcast.13, f32[7,2,16,8,512]{4,3,2,1,0:T(8,128)} %bitcast.10), custom_call_target="tpu_custom_call" | custom-call | bytes 8388608 | tf_op jit(solution)/shard_map/pack/pallas_call | solution.py:75
  3.1 0.0 copy-start.6
  3.1 0.0 copy-start.7
  3.1 63.2 %all_to_all.10 = f32[32,8,4,8,128]{4,3,2,1,0:T(8,128)S(1)} all-to-all(f32[32,8,4,8,128]{4,3,2,1,0:T(8,128)S(1)} %pack.1), channel_id=1, replica_groups=mesh['rad'=4,'phi'=32] {'phi'}, dimensions={0} | all-to-all | bytes 8388608 | tf_op jit(solution)/shard_map/all_to_all | solution.py:396
  66.4 0.0 copy-done.6
  66.4 0.0 copy-done.7
  66.4 4.0 %shift_rows.1 = f32[32,8,4,8,128]{4,3,2,1,0:T(8,128)} custom-call(s32[128]{0:T(128)S(1)} %copy-done.6, f32[128]{0:T(128)S(1)} %copy-done.7, f32[1024,8,128]{2,1,0:T(8,128)S(1)} %bitcast.12), custom_call_target="tpu_custom_call" | custom-call | flops 8388608 | bytes 8388608 | tf_op jit(solution)/shard_map/shift_rows/pallas_call | solution.py:136
  70.4 4.9 %all-to-all-start.1 = ((f32[32,8,4,8,128]{4,3,2,1,0:T(8,128)}), f32[32,8,4,8,128]{4,3,2,1,0:T(8,128)}, u32[]{:S(2)}, u32[]{:S(2)}) async-start(f32[32,8,4,8,128]{4,3,2,1,0:T(8,128)} %shift_rows.1), calls=%async_computation.1 | async-start | bytes 8388608 | tf_op jit(solution)/shard_map/all_to_all | solution.py:399
  75.3 0.0 copy-start
  75.3 0.0 copy-start.1
  75.3 4.3 %borders.1 = (f32[16,512]{1,0:T(8,128)}, f32[16,512]{1,0:T(8,128)}, f32[16,128]{1,0:T(8,128)}, f32[16,128]{1,0:T(8,128)}) custom-call(f32[2,16,8,512]{3,2,1,0:T(8,128)} %bitcast.14, f32[7,2,16,8,512]{4,3,2,1,0:T(8,128)} %bitcast.11), custom_call_target="tpu_custom_call" | custom-call | tf_op jit(solution)/shard_map/borders/pallas_call | solution.py:378
  79.6 0.0 copy-start.2
  79.7 0.0 copy-start.3
  79.7 0.0 copy-start.4
  79.7 0.0 copy-start.5
  79.7 1.4 %collective-permute-start = (f32[16,512]{1,0:T(8,128)}, f32[16,512]{1,0:T(8,128)S(1)}, u32[]{:S(2)}, u32[]{:S(2)}) collective-permute-start(f32[16,512]{1,0:T(8,128)} %get-tuple-element.18.refs_2_), channel_id=1, source_target_pairs={{0,32},{32,64},{64,96},{1,33},{33,65},{65,97},{2,34},{34,66},{66,9... | collective-permute-start | bytes 98312 | tf_op jit(solution)/shard_map/ppermute | solution.py:23
  81.1 1.3 collective-permute-start.1
  82.4 3.2 %collective-permute-start.2 = (f32[16,128]{1,0:T(8,128)}, f32[16,128]{1,0:T(8,128)S(1)}, u32[]{:S(2)}, u32[]{:S(2)}) collective-permute-start(f32[16,128]{1,0:T(8,128)} %get-tuple-element.20.refs_6_), channel_id=1, source_target_pairs={{0,1},{1,2},{2,3},{3,4},{4,5},{5,6},{6,7},{7,8},{8,9},{9,10},{10,1... | collective-permute-start | bytes 24584 | tf_op jit(solution)/shard_map/ppermute | solution.py:23
  85.6 4.6 %collective-permute-start.3 = (f32[16,128]{1,0:T(8,128)}, f32[16,128]{1,0:T(8,128)S(1)}, u32[]{:S(2)}, u32[]{:S(2)}) collective-permute-start(f32[16,128]{1,0:T(8,128)} %get-tuple-element.21.refs_5_), channel_id=1, source_target_pairs={{0,31},{1,0},{2,1},{3,2},{4,3},{5,4},{6,5},{7,6},{8,7},{9,8},{10,9... | collective-permute-start | bytes 24584 | tf_op jit(solution)/shard_map/ppermute | solution.py:23
  90.2 0.0 copy-done
  90.2 0.0 copy-done.1
  90.2 6.3 %flux_update.1 = (f32[6,2,128,512]{3,2,1,0:T(8,128)S(1)}, f32[2,2,128,512]{3,2,1,0:T(8,128)}) custom-call(f32[2,128,512]{2,1,0:T(8,128)S(1)} %copy-done.1, f32[7,2,128,512]{3,2,1,0:T(8,128)S(1)} %copy-done), custom_call_target="tpu_custom_call" | custom-call | flops 41943040 | bytes 8388608 | tf_op jit(solution)/shard_map/flux_update/pallas_call | solution.py:321
  96.6 30.3 %collective-permute-done.2.refs_4_ = f32[16,128]{1,0:T(8,128)S(1)} collective-permute-done((f32[16,128]{1,0:T(8,128)}, f32[16,128]{1,0:T(8,128)S(1)}, u32[]{:S(2)}, u32[]{:S(2)}) %collective-permute-start.2) | collective-permute-done | bytes 8224 | tf_op jit(solution)/shard_map/ppermute | solution.py:23
  126.9 0.0 collective-permute-done.3.refs_7_
  126.9 0.0 collective-permute-done.refs_0_
  126.9 0.0 collective-permute-done.1.refs_3_
  126.9 1.7 %all-to-all-done.1 = f32[32,8,4,8,128]{4,3,2,1,0:T(8,128)} async-done(((f32[32,8,4,8,128]{4,3,2,1,0:T(8,128)}), f32[32,8,4,8,128]{4,3,2,1,0:T(8,128)}, u32[]{:S(2)}, u32[]{:S(2)}) %all-to-all-start.1) | async-done | bytes 4194336 | tf_op jit(solution)/shard_map/all_to_all | solution.py:399
  128.5 0.0 copy-done.2
  128.5 0.0 copy-done.3
  128.5 0.0 copy-done.4
  128.5 0.0 copy-done.5
  128.6 3.9 %finish.1 = (f32[2,16,8,512]{3,2,1,0:T(8,128)}, f32[7,2,16,8,512]{4,3,2,1,0:T(8,128)}) custom-call(f32[16,2,8,4,8,128]{5,4,3,2,1,0:T(8,128)} %bitcast.3.moved_ref, f32[6,2,16,8,512]{4,3,2,1,0:T(8,128)S(1)} %bitcast.15, f32[2,2,16,8,512]{4,3,2,1,0:T(8,128)} %bitcast.16, f32[16,512]{1,0:T(8,128)S(1)} %collective-permute-done.refs_0_, f32[16,512]{1,0:T(8,128)S(1)} %copy-done.2, ...), custom_call_target="tpu_custom_call" | custom-call | flops 1048576 | bytes 12582912 | tf_op jit(solution)/shard_map/finish/pallas_call | solution.py:243
Async XLA Ops:
  3.1 63.2 %copy-start.6 = (s32[128]{0:T(128)S(1)}, s32[128]{0:T(128)}, u32[]{:S(2)}) copy-start(s32[128]{0:T(128)} %shift_ref.1) | copy-start | bytes 1540
  3.1 63.2 %copy-start.7 = (f32[128]{0:T(128)S(1)}, f32[128]{0:T(128)}, u32[]{:S(2)}) copy-start(f32[128]{0:T(128)} %fraction_ref.1) | copy-start | bytes 1540
  70.4 58.1 %all-to-all-start.1 = ((f32[32,8,4,8,128]{4,3,2,1,0:T(8,128)}), f32[32,8,4,8,128]{4,3,2,1,0:T(8,128)}, u32[]{:S(2)}, u32[]{:S(2)}) async-start(f32[32,8,4,8,128]{4,3,2,1,0:T(8,128)} %shift_rows.1), calls=%async_computation.1 | async-start | bytes 8388608 | tf_op jit(solution)/shard_map/all_to_all | solution.py:399
  75.3 15.0 %copy-start = (f32[7,2,128,512]{3,2,1,0:T(8,128)S(1)}, f32[7,2,128,512]{3,2,1,0:T(8,128)}, u32[]{:S(2)}) copy-start(f32[7,2,128,512]{3,2,1,0:T(8,128)} %carried_ref) | copy-start | bytes 11010052
  75.3 15.0 %copy-start.1 = (f32[2,128,512]{2,1,0:T(8,128)S(1)}, f32[2,128,512]{2,1,0:T(8,128)}, u32[]{:S(2)}) copy-start(f32[2,128,512]{2,1,0:T(8,128)} %density_ref) | copy-start | bytes 1572868
  79.6 48.9 %copy-start.2 = (f32[16,512]{1,0:T(8,128)S(1)}, f32[16,512]{1,0:T(8,128)}, u32[]{:S(2)}) copy-start(f32[16,512]{1,0:T(8,128)} %get-tuple-element.19.refs_1_) | copy-start | bytes 98308
  79.7 48.9 %copy-start.3 = (f32[16,512]{1,0:T(8,128)S(1)}, f32[16,512]{1,0:T(8,128)}, u32[]{:S(2)}) copy-start(f32[16,512]{1,0:T(8,128)} %get-tuple-element.18.refs_2_) | copy-start | bytes 98308
  79.7 48.9 %copy-start.4 = (f32[16,128]{1,0:T(8,128)S(1)}, f32[16,128]{1,0:T(8,128)}, u32[]{:S(2)}) copy-start(f32[16,128]{1,0:T(8,128)} %get-tuple-element.21.refs_5_) | copy-start | bytes 24580
  79.7 48.9 %copy-start.5 = (f32[16,128]{1,0:T(8,128)S(1)}, f32[16,128]{1,0:T(8,128)}, u32[]{:S(2)}) copy-start(f32[16,128]{1,0:T(8,128)} %get-tuple-element.20.refs_6_) | copy-start | bytes 24580
  79.7 47.2 %collective-permute-start = (f32[16,512]{1,0:T(8,128)}, f32[16,512]{1,0:T(8,128)S(1)}, u32[]{:S(2)}, u32[]{:S(2)}) collective-permute-start(f32[16,512]{1,0:T(8,128)} %get-tuple-element.18.refs_2_), channel_id=1, source_target_pairs={{0,32},{32,64},{64,96},{1,33},{33,65},{65,97},{2,34},{34,66},{66,9... | collective-permute-start | bytes 98312 | tf_op jit(solution)/shard_map/ppermute | solution.py:23
  81.1 45.8 %collective-permute-start.1 = (f32[16,512]{1,0:T(8,128)}, f32[16,512]{1,0:T(8,128)S(1)}, u32[]{:S(2)}, u32[]{:S(2)}) collective-permute-start(f32[16,512]{1,0:T(8,128)} %get-tuple-element.19.refs_1_), channel_id=1, source_target_pairs={{32,0},{64,32},{96,64},{33,1},{65,33},{97,65},{34,2},{66,34},{98,6... | collective-permute-start | bytes 98312 | tf_op jit(solution)/shard_map/ppermute | solution.py:23
  82.4 44.4 %collective-permute-start.2 = (f32[16,128]{1,0:T(8,128)}, f32[16,128]{1,0:T(8,128)S(1)}, u32[]{:S(2)}, u32[]{:S(2)}) collective-permute-start(f32[16,128]{1,0:T(8,128)} %get-tuple-element.20.refs_6_), channel_id=1, source_target_pairs={{0,1},{1,2},{2,3},{3,4},{4,5},{5,6},{6,7},{7,8},{8,9},{9,10},{10,1... | collective-permute-start | bytes 24584 | tf_op jit(solution)/shard_map/ppermute | solution.py:23
  85.6 41.3 %collective-permute-start.3 = (f32[16,128]{1,0:T(8,128)}, f32[16,128]{1,0:T(8,128)S(1)}, u32[]{:S(2)}, u32[]{:S(2)}) collective-permute-start(f32[16,128]{1,0:T(8,128)} %get-tuple-element.21.refs_5_), channel_id=1, source_target_pairs={{0,31},{1,0},{2,1},{3,2},{4,3},{5,4},{6,5},{7,6},{8,7},{9,8},{10,9... | collective-permute-start | bytes 24584 | tf_op jit(solution)/shard_map/ppermute | solution.py:23

commit v8 on v7

--- a/solution.py
+++ b/solution.py
@@ -64,10 +64,10 @@
     for i in range(chunks):
         for copy in arrivals[i]:
             copy.wait()
-        lax.fori_loop(i * size, (i + 1) * size, reorder, 0, unroll=2)
-
-
-def pack(density, carried, chunks=4):
+        lax.fori_loop(i * size, (i + 1) * size, reorder, 0, unroll=1)
+
+
+def pack(density, carried, chunks=8):
     height, rows, width = density.shape
     groups = rows // ROWS
     natural = (height, groups, ROWS, width)

time: 133 us -> 133 us (level)
  no operation moved by 1% of the time
where the time goes in v8:
time: 133 us; the launch traced here: 132 us
  blocking collectives  63.2 us (48%)
  waiting for transfers between devices  32 us (24%)
  Pallas kernels  21 us (16%)
  starting transfers between devices  15.4 us (12%)
    all_to_all x1, blocking collectives, local(): received = lax.all_to_all(pack(density, carried), 'phi', 0, 0, tiled=True)  63.2 us
    ppermute x4, waiting for transfers between devices, neighbours(): return lax.ppermute(value, axis, pairs)  30.3 us
    ppermute x4, starting transfers between devices, neighbours(): return lax.ppermute(value, axis, pairs)  10.5 us
    pallas_call x1, Pallas kernels, update_of(): pl.pallas_call(functools.partial(update_kernel, rows // ROWS, width), out...  6.31 us
    all_to_all x1, starting transfers between devices, local(): moved = lax.all_to_all(moved, 'phi', 0, 0, tiled=True)  4.88 us
    pallas_call x1, Pallas kernels, borders_of(): pl.pallas_call(functools.partial(border_kernel, groups, height, width), o...  4.33 us
    pallas_call x1, Pallas kernels, shift_rows(): pl.pallas_call(functools.partial(shift_kernel, blocks, tiles, chunks, hei...  4.03 us
    pallas_call x1, Pallas kernels, finish(): pl.pallas_call(functools.partial(finish_kernel, groups, height, chunks),...  3.93 us
  transfers between devices with their start and end apart: 5, of which 2 were waited for; matrix products, arithmetic and copies ran while one was open for 0% of the time, Pallas kernels for 8%

profile of v8, /device:TPU:0, one launch (start us, length us, event | category | flops | bytes accessed | tf_op | source)
XLA Modules:
  0.0 132.4 jit_solution(8384342183829776321)
XLA Ops:
  0.6 2.4 %pack.1 = f32[32,8,4,8,128]{4,3,2,1,0:T(8,128)S(1)} custom-call(f32[2,16,8,512]{3,2,1,0:T(8,128)} %bitcast.13, f32[7,2,16,8,512]{4,3,2,1,0:T(8,128)} %bitcast.10), custom_call_target="tpu_custom_call" | custom-call | bytes 8388608 | tf_op jit(solution)/shard_map/pack/pallas_call | solution.py:75
  3.1 0.0 copy-start.6
  3.1 0.0 copy-start.7
  3.1 63.2 %all_to_all.10 = f32[32,8,4,8,128]{4,3,2,1,0:T(8,128)S(1)} all-to-all(f32[32,8,4,8,128]{4,3,2,1,0:T(8,128)S(1)} %pack.1), channel_id=1, replica_groups=mesh['rad'=4,'phi'=32] {'phi'}, dimensions={0} | all-to-all | bytes 8388608 | tf_op jit(solution)/shard_map/all_to_all | solution.py:396
  66.3 0.0 copy-done.6
  66.3 0.0 copy-done.7
  66.3 4.0 %shift_rows.1 = f32[32,8,4,8,128]{4,3,2,1,0:T(8,128)} custom-call(s32[128]{0:T(128)S(1)} %copy-done.6, f32[128]{0:T(128)S(1)} %copy-done.7, f32[1024,8,128]{2,1,0:T(8,128)S(1)} %bitcast.12), custom_call_target="tpu_custom_call" | custom-call | flops 8388608 | bytes 8388608 | tf_op jit(solution)/shard_map/shift_rows/pallas_call | solution.py:136
  70.3 4.9 %all-to-all-start.1 = ((f32[32,8,4,8,128]{4,3,2,1,0:T(8,128)}), f32[32,8,4,8,128]{4,3,2,1,0:T(8,128)}, u32[]{:S(2)}, u32[]{:S(2)}) async-start(f32[32,8,4,8,128]{4,3,2,1,0:T(8,128)} %shift_rows.1), calls=%async_computation.1 | async-start | bytes 8388608 | tf_op jit(solution)/shard_map/all_to_all | solution.py:399
  75.2 0.0 copy-start
  75.2 0.0 copy-start.1
  75.3 4.3 %borders.1 = (f32[16,512]{1,0:T(8,128)}, f32[16,512]{1,0:T(8,128)}, f32[16,128]{1,0:T(8,128)}, f32[16,128]{1,0:T(8,128)}) custom-call(f32[2,16,8,512]{3,2,1,0:T(8,128)} %bitcast.14, f32[7,2,16,8,512]{4,3,2,1,0:T(8,128)} %bitcast.11), custom_call_target="tpu_custom_call" | custom-call | tf_op jit(solution)/shard_map/borders/pallas_call | solution.py:378
  79.6 0.0 copy-start.2
  79.6 0.0 copy-start.3
  79.6 0.0 copy-start.4
  79.6 0.0 copy-start.5
  79.6 1.4 %collective-permute-start = (f32[16,512]{1,0:T(8,128)}, f32[16,512]{1,0:T(8,128)S(1)}, u32[]{:S(2)}, u32[]{:S(2)}) collective-permute-start(f32[16,512]{1,0:T(8,128)} %get-tuple-element.18.refs_2_), channel_id=1, source_target_pairs={{0,32},{32,64},{64,96},{1,33},{33,65},{65,97},{2,34},{34,66},{66,9... | collective-permute-start | bytes 98312 | tf_op jit(solution)/shard_map/ppermute | solution.py:23
  81.1 1.3 collective-permute-start.1
  82.4 3.2 %collective-permute-start.2 = (f32[16,128]{1,0:T(8,128)}, f32[16,128]{1,0:T(8,128)S(1)}, u32[]{:S(2)}, u32[]{:S(2)}) collective-permute-start(f32[16,128]{1,0:T(8,128)} %get-tuple-element.20.refs_6_), channel_id=1, source_target_pairs={{0,1},{1,2},{2,3},{3,4},{4,5},{5,6},{6,7},{7,8},{8,9},{9,10},{10,1... | collective-permute-start | bytes 24584 | tf_op jit(solution)/shard_map/ppermute | solution.py:23
  85.5 4.6 %collective-permute-start.3 = (f32[16,128]{1,0:T(8,128)}, f32[16,128]{1,0:T(8,128)S(1)}, u32[]{:S(2)}, u32[]{:S(2)}) collective-permute-start(f32[16,128]{1,0:T(8,128)} %get-tuple-element.21.refs_5_), channel_id=1, source_target_pairs={{0,31},{1,0},{2,1},{3,2},{4,3},{5,4},{6,5},{7,6},{8,7},{9,8},{10,9... | collective-permute-start | bytes 24584 | tf_op jit(solution)/shard_map/ppermute | solution.py:23
  90.2 0.0 copy-done
  90.2 0.0 copy-done.1
  90.2 6.3 %flux_update.1 = (f32[6,2,128,512]{3,2,1,0:T(8,128)S(1)}, f32[2,2,128,512]{3,2,1,0:T(8,128)}) custom-call(f32[2,128,512]{2,1,0:T(8,128)S(1)} %copy-done.1, f32[7,2,128,512]{3,2,1,0:T(8,128)S(1)} %copy-done), custom_call_target="tpu_custom_call" | custom-call | flops 41943040 | bytes 8388608 | tf_op jit(solution)/shard_map/flux_update/pallas_call | solution.py:321
  96.5 30.3 %collective-permute-done.2.refs_4_ = f32[16,128]{1,0:T(8,128)S(1)} collective-permute-done((f32[16,128]{1,0:T(8,128)}, f32[16,128]{1,0:T(8,128)S(1)}, u32[]{:S(2)}, u32[]{:S(2)}) %collective-permute-start.2) | collective-permute-done | bytes 8224 | tf_op jit(solution)/shard_map/ppermute | solution.py:23
  126.8 0.0 collective-permute-done.3.refs_7_
  126.8 0.0 collective-permute-done.refs_0_
  126.8 0.0 collective-permute-done.1.refs_3_
  126.8 1.7 %all-to-all-done.1 = f32[32,8,4,8,128]{4,3,2,1,0:T(8,128)} async-done(((f32[32,8,4,8,128]{4,3,2,1,0:T(8,128)}), f32[32,8,4,8,128]{4,3,2,1,0:T(8,128)}, u32[]{:S(2)}, u32[]{:S(2)}) %all-to-all-start.1) | async-done | bytes 4194336 | tf_op jit(solution)/shard_map/all_to_all | solution.py:399
  128.5 0.0 copy-done.2
  128.5 0.0 copy-done.3
  128.5 0.0 copy-done.4
  128.5 0.0 copy-done.5
  128.5 3.9 %finish.1 = (f32[2,16,8,512]{3,2,1,0:T(8,128)}, f32[7,2,16,8,512]{4,3,2,1,0:T(8,128)}) custom-call(f32[16,2,8,4,8,128]{5,4,3,2,1,0:T(8,128)} %bitcast.3.moved_ref, f32[6,2,16,8,512]{4,3,2,1,0:T(8,128)S(1)} %bitcast.15, f32[2,2,16,8,512]{4,3,2,1,0:T(8,128)} %bitcast.16, f32[16,512]{1,0:T(8,128)S(1)} %collective-permute-done.refs_0_, f32[16,512]{1,0:T(8,128)S(1)} %copy-done.2, ...), custom_call_target="tpu_custom_call" | custom-call | flops 1048576 | bytes 12582912 | tf_op jit(solution)/shard_map/finish/pallas_call | solution.py:243
Async XLA Ops:
  3.1 63.2 %copy-start.6 = (s32[128]{0:T(128)S(1)}, s32[128]{0:T(128)}, u32[]{:S(2)}) copy-start(s32[128]{0:T(128)} %shift_ref.1) | copy-start | bytes 1540
  3.1 63.2 %copy-start.7 = (f32[128]{0:T(128)S(1)}, f32[128]{0:T(128)}, u32[]{:S(2)}) copy-start(f32[128]{0:T(128)} %fraction_ref.1) | copy-start | bytes 1540
  70.3 58.1 %all-to-all-start.1 = ((f32[32,8,4,8,128]{4,3,2,1,0:T(8,128)}), f32[32,8,4,8,128]{4,3,2,1,0:T(8,128)}, u32[]{:S(2)}, u32[]{:S(2)}) async-start(f32[32,8,4,8,128]{4,3,2,1,0:T(8,128)} %shift_rows.1), calls=%async_computation.1 | async-start | bytes 8388608 | tf_op jit(solution)/shard_map/all_to_all | solution.py:399
  75.2 15.0 %copy-start = (f32[7,2,128,512]{3,2,1,0:T(8,128)S(1)}, f32[7,2,128,512]{3,2,1,0:T(8,128)}, u32[]{:S(2)}) copy-start(f32[7,2,128,512]{3,2,1,0:T(8,128)} %carried_ref) | copy-start | bytes 11010052
  75.2 15.0 %copy-start.1 = (f32[2,128,512]{2,1,0:T(8,128)S(1)}, f32[2,128,512]{2,1,0:T(8,128)}, u32[]{:S(2)}) copy-start(f32[2,128,512]{2,1,0:T(8,128)} %density_ref) | copy-start | bytes 1572868
  79.6 48.9 %copy-start.2 = (f32[16,512]{1,0:T(8,128)S(1)}, f32[16,512]{1,0:T(8,128)}, u32[]{:S(2)}) copy-start(f32[16,512]{1,0:T(8,128)} %get-tuple-element.19.refs_1_) | copy-start | bytes 98308
  79.6 48.9 %copy-start.3 = (f32[16,512]{1,0:T(8,128)S(1)}, f32[16,512]{1,0:T(8,128)}, u32[]{:S(2)}) copy-start(f32[16,512]{1,0:T(8,128)} %get-tuple-element.18.refs_2_) | copy-start | bytes 98308
  79.6 48.9 %copy-start.4 = (f32[16,128]{1,0:T(8,128)S(1)}, f32[16,128]{1,0:T(8,128)}, u32[]{:S(2)}) copy-start(f32[16,128]{1,0:T(8,128)} %get-tuple-element.21.refs_5_) | copy-start | bytes 24580
  79.6 48.9 %copy-start.5 = (f32[16,128]{1,0:T(8,128)S(1)}, f32[16,128]{1,0:T(8,128)}, u32[]{:S(2)}) copy-start(f32[16,128]{1,0:T(8,128)} %get-tuple-element.20.refs_6_) | copy-start | bytes 24580
  79.6 47.2 %collective-permute-start = (f32[16,512]{1,0:T(8,128)}, f32[16,512]{1,0:T(8,128)S(1)}, u32[]{:S(2)}, u32[]{:S(2)}) collective-permute-start(f32[16,512]{1,0:T(8,128)} %get-tuple-element.18.refs_2_), channel_id=1, source_target_pairs={{0,32},{32,64},{64,96},{1,33},{33,65},{65,97},{2,34},{34,66},{66,9... | collective-permute-start | bytes 98312 | tf_op jit(solution)/shard_map/ppermute | solution.py:23
  81.1 45.7 %collective-permute-start.1 = (f32[16,512]{1,0:T(8,128)}, f32[16,512]{1,0:T(8,128)S(1)}, u32[]{:S(2)}, u32[]{:S(2)}) collective-permute-start(f32[16,512]{1,0:T(8,128)} %get-tuple-element.19.refs_1_), channel_id=1, source_target_pairs={{32,0},{64,32},{96,64},{33,1},{65,33},{97,65},{34,2},{66,34},{98,6... | collective-permute-start | bytes 98312 | tf_op jit(solution)/shard_map/ppermute | solution.py:23
  82.4 44.4 %collective-permute-start.2 = (f32[16,128]{1,0:T(8,128)}, f32[16,128]{1,0:T(8,128)S(1)}, u32[]{:S(2)}, u32[]{:S(2)}) collective-permute-start(f32[16,128]{1,0:T(8,128)} %get-tuple-element.20.refs_6_), channel_id=1, source_target_pairs={{0,1},{1,2},{2,3},{3,4},{4,5},{5,6},{6,7},{7,8},{8,9},{9,10},{10,1... | collective-permute-start | bytes 24584 | tf_op jit(solution)/shard_map/ppermute | solution.py:23
  85.5 41.2 %collective-permute-start.3 = (f32[16,128]{1,0:T(8,128)}, f32[16,128]{1,0:T(8,128)S(1)}, u32[]{:S(2)}, u32[]{:S(2)}) collective-permute-start(f32[16,128]{1,0:T(8,128)} %get-tuple-element.21.refs_5_), channel_id=1, source_target_pairs={{0,31},{1,0},{2,1},{3,2},{4,3},{5,4},{6,5},{7,6},{8,7},{9,8},{10,9... | collective-permute-start | bytes 24584 | tf_op jit(solution)/shard_map/ppermute | solution.py:23
